TPU v7x, 128 devices: a whole 4x4x4 slice. The times are simulated.
128 devices in a mesh: ens: 8 (over x, core), map: 16 (over y, z).
Axes of the slice: x: 4, y: 4, z: 4, core: 2. Of those that a mesh axis runs over, the one named last changes fastest.
Arguments:
- ensemble_weather: bfloat16 [128, 16, 64, 1440], P('ens', None, 'map'), may hold values from -6 to 6
- conv_in: bfloat16 [128, 16, 3, 3], replicated, may hold values from -0.5 to 0.5
- bias_in: float32 [128], replicated, may hold values from -3 to 3
- conv_out: bfloat16 [16, 128, 3, 3], replicated, may hold values from -0.1875 to 0.1875
- bias_out: float32 [16], replicated, may hold values from -3 to 3
- observed_entry_index: int32 [4096], P('map'), may hold values from 0 to 92159
- obs_count: int32 [16], P('map'), may hold values from 128 to 256, as said below
- obs_value: float32 [4096], P('map'), may hold values from -8 to 8
- obs_sigma: float32 [4096], P('map'), may hold values from 0.5 to 2
Outputs:
- analysis: bfloat16 [128, 16, 64, 1440], P('ens', None, 'map')
- factor: float32 [128, 128], replicated
- mean_weights: float32 [128], replicated
Inputs may be any that keep to these rules, and one draw needn't show every extreme that they name: `obs_count`: every draw has a tile with all 256 slots live.
All inputs are finite; a program needn't handle non-finite values.
Results may differ from a plain program's by a relative error of at most 0.0093.
Values may be sent and summed in bfloat16 or wider, within the bound.
No kernel may reach another device: no remote copies, remote signals or barrier semaphores. Data moves between devices by JAX's collectives and lax.ppermute only.
A program may use at most 128 MiB of HBM per device.

v0:
```python
import math

import jax
import jax.numpy as jnp
from jax import lax
from jax.sharding import PartitionSpec as P

MB = 4


def with_halo(block, sides, width):
    for axis, dim in sides:
        count = lax.axis_size(axis)
        forward = [(i, i + 1) for i in range(count - 1)]
        backward = [(target, source) for source, target in forward]
        low = lax.ppermute(
            lax.slice_in_dim(block, block.shape[dim] - width, None, axis=dim), axis, forward
        )
        high = lax.ppermute(lax.slice_in_dim(block, 0, width, axis=dim), axis, backward)
        block = jnp.concatenate([low, block, high], axis=dim)
    return block


def for_sending(value):

    def short(part):
        return part.astype(jnp.bfloat16) if part.dtype == jnp.float32 else part

    return jax.tree.map(short, value)


def convolve(padded, kernel):
    wrapped = jnp.concatenate([padded[..., -1:], padded, padded[..., :1]], axis=-1)
    return lax.conv_general_dilated(
        wrapped,
        kernel,
        (1, 1),
        "VALID",
        dimension_numbers=("NCHW", "OIHW", "NCHW"),
        preferred_element_type=jnp.float32,
    )


def on_device(
    ensemble_weather,
    conv_in,
    bias_in,
    conv_out,
    bias_out,
    observed_entry_index,
    obs_count,
    obs_value,
    obs_sigma,
):
    members_per_tile, field_planes, latitude_tile_rows, longitude_count = ensemble_weather.shape
    n_ens = lax.axis_size("ens")
    members = members_per_tile * n_ens
    realization_groups = ensemble_weather.reshape(
        members_per_tile // MB, MB, field_planes, latitude_tile_rows, longitude_count
    )

    def predicted_realization_group(realization_group):
        padded = with_halo(realization_group, (("map", 2),), 1)
        inner = convolve(padded, conv_in) + bias_in[None, :, None, None]
        hidden = jax.nn.silu(inner).astype(jnp.bfloat16)
        hidden_pad = with_halo(hidden, (("map", 2),), 1)
        outer = convolve(hidden_pad, conv_out) + bias_out[None, :, None, None]
        return (realization_group.astype(jnp.float32) + outer).astype(jnp.bfloat16)

    predicted_weather = lax.map(predicted_realization_group, realization_groups).reshape(
        members_per_tile, field_planes, latitude_tile_rows, longitude_count
    )
    p_dev = observed_entry_index.shape[0]
    measurement_vector = jnp.take(
        predicted_weather.reshape(
            members_per_tile, field_planes * latitude_tile_rows * longitude_count
        ),
        observed_entry_index,
        axis=1,
    ).astype(jnp.float32)
    mean_obs = lax.psum(jnp.sum(measurement_vector, axis=0), "ens") / members
    live = (jnp.arange(p_dev, dtype=jnp.int32) < obs_count[0]).astype(jnp.float32)
    anomalies = (measurement_vector - mean_obs[None, :]) * (
        live / (obs_sigma * math.sqrt(members - 1))
    )[None, :]
    innov = live * (obs_value - mean_obs) / obs_sigma
    regrouped = lax.all_to_all(anomalies, "ens", split_axis=1, concat_axis=0, tiled=True)
    share = p_dev // n_ens
    innov_part = lax.dynamic_slice_in_dim(innov, lax.axis_index("ens") * share, share)
    gram_part = jnp.dot(regrouped, regrouped.T, precision=lax.Precision.HIGHEST)
    proj_part = jnp.dot(regrouped, innov_part, precision=lax.Precision.HIGHEST)
    eye = jnp.eye(members, dtype=jnp.float32)
    gram, proj = lax.psum((gram_part, proj_part), ("ens", "map"))
    factor = jnp.linalg.cholesky(gram + eye)
    middle = jax.scipy.linalg.solve_triangular(factor, proj, lower=True)
    mean_weights = jax.scipy.linalg.solve_triangular(
        factor, middle, lower=True, trans="T"
    ) / math.sqrt(members - 1)
    inverse_t = jax.scipy.linalg.solve_triangular(factor, eye, lower=True, trans="T")
    coeff = mean_weights[:, None] + inverse_t
    transform = (coeff - jnp.mean(coeff, axis=0, keepdims=True) + 1.0 / members).astype(
        jnp.bfloat16
    )
    mixed = jnp.einsum(
        "jc,jfrx->cfrx",
        transform,
        lax.all_to_all(
            for_sending(predicted_weather), "ens", split_axis=1, concat_axis=0, tiled=True
        ).astype(predicted_weather.dtype),
        preferred_element_type=jnp.float32,
    ).astype(jnp.bfloat16)
    analysis = lax.all_to_all(mixed, "ens", split_axis=0, concat_axis=1, tiled=True)
    return (analysis, factor, mean_weights)


def solution(mesh):
    placed = (
        P("ens", None, "map", None),
        P(),
        P(),
        P(),
        P(),
        P("map"),
        P("map"),
        P("map"),
        P("map"),
    )
    return jax.shard_map(
        on_device,
        mesh=mesh,
        in_specs=placed,
        out_specs=(P("ens", None, "map", None), P(), P()),
        check_vma=False,
    )
```

profile of v0, /device:TPU:1, one launch (start us, length us, event | category | flops | bytes accessed | tf_op | source)
XLA Modules:
  0.0 1250.8 jit_solution(5925860040036641962)
XLA Ops:
  9.7 912.8 %while.10 = (s32[]{:T(128)}, bf16[4,4,16,4,1440]{4,1,2,3,0:T(4,128)(2,1)}, bf16[4,4,16,4,1440]{4,3,2,1,0:T(4,128)(2,1)}, bf16[128,16,3,3]{0,1,3,2:T(8,128)(2,1)}...) while((s32[]{:T(128)}, ...), condition=%wide.region_1.2_spmd, body=%wide.region_0.1_spmd.sunk | while | flops 1771046912 | bytes 278889696 | solution.py:70
  40.2 13.2 %multiply_convert_fusion.2 = bf16[4,32,181,128]{3,1,2,0:T(8,128)(2,1)S(1)} fusion(f32[128]{0:T(128)S(1)} %copy-done.13, pred[32,181]{0,1:T(8,128)(4,1)S(1)} %copy-done.14, bf16[16,6,32,183]{2,0,3,1:T(8,128)(2,1)} %copy.128, bf16[128,16,3,3]{0,1,3,2:T(8,128)(2,1)S(1)} %copy-done.11), kind=kOutput, calls=%fused_computation.3.clone.1 | convolution fusion | flops 874823680 | bytes 7098528 | tf_op jit(solution)/shard_map/while/body/eval_jaxpr/conv_general_dilated | solution.py:34
  73.0 7.6 copy.130
  80.6 8.3 reshape.124
  92.0 5.7 collective-permute-done.2
  109.5 42.5 %concatenate.17 = bf16[4,128,6,1442]{1,3,0,2:T(8,128)(2,1)} concatenate(bf16[4,128,6,1]{1,3,0,2:T(2,128)(2,1)S(1)} %get-tuple-element.157, bf16[4,128,6,1440]{1,3,0,2:T(8,128)(2,1)} %copy-done, bf16[4,128,6,1]{1,3,0,2:T(2,128)(2,1)S(1)} %get-tuple-element.158), dimensions={3} | concatenate | bytes 17719296 | tf_op jit(solution)/shard_map/while/body/eval_jaxpr/concatenate | solution.py:33
  152.0 7.6 pad.51
  159.6 12.0 reshape.126
  172.6 9.4 fusion.61
  182.0 42.5 %fusion.62 = f32[4,32,181,16]{1,3,2,0:T(8,128)} fusion(bf16[16,128,3,3]{1,0,3,2:T(8,128)(2,1)S(1)} %copy-done.12, bf16[128,6,4,8,183]{0,4,3,2,1:T(8,128)(2,1)} %fusion.61), kind=kOutput, calls=%fused_computation.5.clone.1 | convolution fusion | flops 854065152 | bytes 10514432 | tf_op jit(solution)/shard_map/while/body/eval_jaxpr/conv_general_dilated | solution.py:34
  267.2 13.2 %multiply_convert_fusion.2 = bf16[4,32,181,128]{3,1,2,0:T(8,128)(2,1)S(1)} fusion(f32[128]{0:T(128)S(1)} %copy-done.13, pred[32,181]{0,1:T(8,128)(4,1)S(1)} %copy-done.14, bf16[16,6,32,183]{2,0,3,1:T(8,128)(2,1)} %copy.128, bf16[128,16,3,3]{0,1,3,2:T(8,128)(2,1)S(1)} %copy-done.11), kind=kOutput, calls=%fused_computation.3.clone.1 | convolution fusion | flops 874823680 | bytes 7098528 | tf_op jit(solution)/shard_map/while/body/eval_jaxpr/conv_general_dilated | solution.py:34
  300.1 7.6 copy.130
  307.6 8.3 reshape.124
  334.8 42.5 %concatenate.17 = bf16[4,128,6,1442]{1,3,0,2:T(8,128)(2,1)} concatenate(bf16[4,128,6,1]{1,3,0,2:T(2,128)(2,1)S(1)} %get-tuple-element.157, bf16[4,128,6,1440]{1,3,0,2:T(8,128)(2,1)} %copy-done, bf16[4,128,6,1]{1,3,0,2:T(2,128)(2,1)S(1)} %get-tuple-element.158), dimensions={3} | concatenate | bytes 17719296 | tf_op jit(solution)/shard_map/while/body/eval_jaxpr/concatenate | solution.py:33
  377.3 7.6 pad.51
  384.9 12.0 reshape.126
  397.9 9.4 fusion.61
  407.3 42.5 %fusion.62 = f32[4,32,181,16]{1,3,2,0:T(8,128)} fusion(bf16[16,128,3,3]{1,0,3,2:T(8,128)(2,1)S(1)} %copy-done.12, bf16[128,6,4,8,183]{0,4,3,2,1:T(8,128)(2,1)} %fusion.61), kind=kOutput, calls=%fused_computation.5.clone.1 | convolution fusion | flops 854065152 | bytes 10514432 | tf_op jit(solution)/shard_map/while/body/eval_jaxpr/conv_general_dilated | solution.py:34
  466.8 6.0 collective-permute-start.1
  493.9 13.2 %multiply_convert_fusion.2 = bf16[4,32,181,128]{3,1,2,0:T(8,128)(2,1)S(1)} fusion(f32[128]{0:T(128)S(1)} %copy-done.13, pred[32,181]{0,1:T(8,128)(4,1)S(1)} %copy-done.14, bf16[16,6,32,183]{2,0,3,1:T(8,128)(2,1)} %copy.128, bf16[128,16,3,3]{0,1,3,2:T(8,128)(2,1)S(1)} %copy-done.11), kind=kOutput, calls=%fused_computation.3.clone.1 | convolution fusion | flops 874823680 | bytes 7098528 | tf_op jit(solution)/shard_map/while/body/eval_jaxpr/conv_general_dilated | solution.py:34
  521.9 6.8 collective-permute-start.3
  528.7 7.6 copy.130
  536.3 8.3 reshape.124
  561.3 42.5 %concatenate.17 = bf16[4,128,6,1442]{1,3,0,2:T(8,128)(2,1)} concatenate(bf16[4,128,6,1]{1,3,0,2:T(2,128)(2,1)S(1)} %get-tuple-element.157, bf16[4,128,6,1440]{1,3,0,2:T(8,128)(2,1)} %copy-done, bf16[4,128,6,1]{1,3,0,2:T(2,128)(2,1)S(1)} %get-tuple-element.158), dimensions={3} | concatenate | bytes 17719296 | tf_op jit(solution)/shard_map/while/body/eval_jaxpr/concatenate | solution.py:33
  603.9 7.6 pad.51
  611.4 12.0 reshape.126
  624.5 9.4 fusion.61
  633.9 42.5 %fusion.62 = f32[4,32,181,16]{1,3,2,0:T(8,128)} fusion(bf16[16,128,3,3]{1,0,3,2:T(8,128)(2,1)S(1)} %copy-done.12, bf16[128,6,4,8,183]{0,4,3,2,1:T(8,128)(2,1)} %fusion.61), kind=kOutput, calls=%fused_computation.5.clone.1 | convolution fusion | flops 854065152 | bytes 10514432 | tf_op jit(solution)/shard_map/while/body/eval_jaxpr/conv_general_dilated | solution.py:34
  693.4 6.0 collective-permute-start.1
  720.4 13.2 %multiply_convert_fusion.2 = bf16[4,32,181,128]{3,1,2,0:T(8,128)(2,1)S(1)} fusion(f32[128]{0:T(128)S(1)} %copy-done.13, pred[32,181]{0,1:T(8,128)(4,1)S(1)} %copy-done.14, bf16[16,6,32,183]{2,0,3,1:T(8,128)(2,1)} %copy.128, bf16[128,16,3,3]{0,1,3,2:T(8,128)(2,1)S(1)} %copy-done.11), kind=kOutput, calls=%fused_computation.3.clone.1 | convolution fusion | flops 874823680 | bytes 7098528 | tf_op jit(solution)/shard_map/while/body/eval_jaxpr/conv_general_dilated | solution.py:34
  748.4 6.8 collective-permute-start.3
  755.3 7.6 copy.130
  762.8 8.3 reshape.124
  785.8 42.5 %concatenate.17 = bf16[4,128,6,1442]{1,3,0,2:T(8,128)(2,1)} concatenate(bf16[4,128,6,1]{1,3,0,2:T(2,128)(2,1)S(1)} %get-tuple-element.157, bf16[4,128,6,1440]{1,3,0,2:T(8,128)(2,1)} %copy-done, bf16[4,128,6,1]{1,3,0,2:T(2,128)(2,1)S(1)} %get-tuple-element.158), dimensions={3} | concatenate | bytes 17719296 | tf_op jit(solution)/shard_map/while/body/eval_jaxpr/concatenate | solution.py:33
  828.3 7.6 pad.51
  835.9 12.0 reshape.126
  848.9 9.4 fusion.61
  858.3 42.5 %fusion.62 = f32[4,32,181,16]{1,3,2,0:T(8,128)} fusion(bf16[16,128,3,3]{1,0,3,2:T(8,128)(2,1)S(1)} %copy-done.12, bf16[128,6,4,8,183]{0,4,3,2,1:T(8,128)(2,1)} %fusion.61), kind=kOutput, calls=%fused_computation.5.clone.1 | convolution fusion | flops 854065152 | bytes 10514432 | tf_op jit(solution)/shard_map/while/body/eval_jaxpr/conv_general_dilated | solution.py:34
  926.8 5.8 reshape_reshape.3
  932.6 16.9 %copy.87 = bf16[16,92160]{0,1:T(8,128)(2,1)} copy(bf16[16,92160]{1,0:T(8,128)(2,1)} %reshape_reshape.3) | data formatting | bytes 5898240 | tf_op jit(solution)/shard_map/reshape;reshape | solution.py:75
  949.7 11.5 gather_fusion
  961.3 20.2 %psum.21 = f32[256]{0:T(256)S(1)} all-reduce(f32[256]{0:T(256)S(1)} %convert_reduce_fusion), channel_id=1, replica_groups=mesh['ens'=8,'map'=16] {'ens'}, use_global_device_ids=true, to_apply=%region_3.4 | all-reduce | flops 256 | bytes 2048 | tf_op jit(solution)/shard_map/psum | solution.py:81
  990.5 5.9 reshape.71
  1003.6 102.7 %psum.23 = f32[128]{0:T(128)S(1)} all-reduce(f32[128]{0:T(128)S(1)} %convolution_bitcast_fusion.2), channel_id=1, replica_groups=mesh['ens'=8,'map'=16] {'ens','map'}, use_global_device_ids=true, to_apply=%region_7.8 | all-reduce | flops 128 | bytes 1024 | tf_op jit(solution)/shard_map/psum | solution.py:93
  1106.3 56.2 %all-reduce.2.cloned.1.call-done = f32[128,128]{1,0:T(8,128)} async-done(((f32[128,128]{1,0:T(8,128)}), f32[128,128]{1,0:T(8,128)}) %all-reduce.2.cloned.1.call-update) | async-done | bytes 65552 | tf_op jit(solution)/shard_map/psum | solution.py:93
  1164.4 11.7 cholesky.18
  1178.0 9.8 custom-call.13
  1196.5 41.8 %all_to_all.52 = bf16[128,2,4,1440]{3,2,1,0:T(4,128)(2,1)S(1)} all-to-all(bf16[128,2,4,1440]{3,2,1,0:T(4,128)(2,1)S(1)} %copy.93), channel_id=1, replica_groups=mesh['ens'=8,'map'=16] {'ens'}, dimensions={0} | all-to-all | bytes 5898240 | tf_op jit(solution)/shard_map/all_to_all | solution.py:112
  (268 shorter events, 340.8 us)
Async XLA Ops:
  11.8 9.0 collective-permute-start
  13.1 8.5 collective-permute-start.1
  34.8 5.4 copy-start.11
  34.8 5.4 copy-start.13
  34.8 5.4 copy-start.14
  62.3 35.4 %collective-permute-start.2 = (bf16[4,128,1,1440]{1,3,0,2:T(8,128)(2,1)}, bf16[4,128,1,1440]{1,3,0,2:T(8,128)(2,1)}, u32[]{:S(2)}, u32[]{:S(2)}) collective-permute-start(bf16[4,128,1,1440]{1,3,0,2:T(8,128)(2,1)} %slice_bitcast_fusion.7), channel_id=1, source_target_pairs={{1,0},{2,1},{3,2},{4,3},{5,4},{6,5},{7,6},{8,7},{9,8},{10,9},{11,1... | collective-permute-start | bytes 4423688 | tf_op jit(solution)/shard_map/while/body/eval_jaxpr/ppermute | solution.py:19
  64.2 8.8 copy-start.4
  68.2 35.0 %collective-permute-start.3 = (bf16[4,128,1,1440]{1,3,0,2:T(8,128)(2,1)}, bf16[4,128,1,1440]{1,3,0,2:T(8,128)(2,1)S(1)}, u32[]{:S(2)}, u32[]{:S(2)}) collective-permute-start(bf16[4,128,1,1440]{1,3,0,2:T(8,128)(2,1)} %slice_bitcast_fusion.9), channel_id=1, source_target_pairs={{0,1},{1,2},{2,3},{3,4},{4,5},{5,6},{6,7},{7,8},{8,9},{9,10},{10,1... | collective-permute-start | bytes 4423688 | tf_op jit(solution)/shard_map/while/body/eval_jaxpr/ppermute | solution.py:16
  172.6 9.4 copy-start.12
  224.5 5.7 copy-start.5
  240.2 7.1 collective-permute-start
  241.5 7.2 collective-permute-start.1
  261.8 5.4 copy-start.11
  261.8 5.4 copy-start.13
  261.8 5.4 copy-start.14
  289.4 33.7 %collective-permute-start.2 = (bf16[4,128,1,1440]{1,3,0,2:T(8,128)(2,1)}, bf16[4,128,1,1440]{1,3,0,2:T(8,128)(2,1)}, u32[]{:S(2)}, u32[]{:S(2)}) collective-permute-start(bf16[4,128,1,1440]{1,3,0,2:T(8,128)(2,1)} %slice_bitcast_fusion.7), channel_id=1, source_target_pairs={{1,0},{2,1},{3,2},{4,3},{5,4},{6,5},{7,6},{8,7},{9,8},{10,9},{11,1... | collective-permute-start | bytes 4423688 | tf_op jit(solution)/shard_map/while/body/eval_jaxpr/ppermute | solution.py:19
  291.2 8.8 copy-start.4
  295.2 33.3 %collective-permute-start.3 = (bf16[4,128,1,1440]{1,3,0,2:T(8,128)(2,1)}, bf16[4,128,1,1440]{1,3,0,2:T(8,128)(2,1)S(1)}, u32[]{:S(2)}, u32[]{:S(2)}) collective-permute-start(bf16[4,128,1,1440]{1,3,0,2:T(8,128)(2,1)} %slice_bitcast_fusion.9), channel_id=1, source_target_pairs={{0,1},{1,2},{2,3},{3,4},{4,5},{5,6},{6,7},{7,8},{8,9},{9,10},{10,1... | collective-permute-start | bytes 4423688 | tf_op jit(solution)/shard_map/while/body/eval_jaxpr/ppermute | solution.py:16
  397.9 9.4 copy-start.12
  449.8 5.7 copy-start.5
  465.5 8.4 collective-permute-start
  466.8 8.6 collective-permute-start.1
  488.5 5.4 copy-start.11
  488.5 5.4 copy-start.13
  488.5 5.4 copy-start.14
  516.0 33.6 %collective-permute-start.2 = (bf16[4,128,1,1440]{1,3,0,2:T(8,128)(2,1)}, bf16[4,128,1,1440]{1,3,0,2:T(8,128)(2,1)}, u32[]{:S(2)}, u32[]{:S(2)}) collective-permute-start(bf16[4,128,1,1440]{1,3,0,2:T(8,128)(2,1)} %slice_bitcast_fusion.7), channel_id=1, source_target_pairs={{1,0},{2,1},{3,2},{4,3},{5,4},{6,5},{7,6},{8,7},{9,8},{10,9},{11,1... | collective-permute-start | bytes 4423688 | tf_op jit(solution)/shard_map/while/body/eval_jaxpr/ppermute | solution.py:19
  517.9 10.8 copy-start.4
  521.9 33.2 %collective-permute-start.3 = (bf16[4,128,1,1440]{1,3,0,2:T(8,128)(2,1)}, bf16[4,128,1,1440]{1,3,0,2:T(8,128)(2,1)S(1)}, u32[]{:S(2)}, u32[]{:S(2)}) collective-permute-start(bf16[4,128,1,1440]{1,3,0,2:T(8,128)(2,1)} %slice_bitcast_fusion.9), channel_id=1, source_target_pairs={{0,1},{1,2},{2,3},{3,4},{4,5},{5,6},{6,7},{7,8},{8,9},{9,10},{10,1... | collective-permute-start | bytes 4423688 | tf_op jit(solution)/shard_map/while/body/eval_jaxpr/ppermute | solution.py:16
  624.5 9.4 copy-start.12
  676.4 5.7 copy-start.5
  692.1 8.4 collective-permute-start
  693.4 8.6 collective-permute-start.1
  715.0 5.4 copy-start.11
  715.0 5.4 copy-start.13
  715.0 5.4 copy-start.14
  742.5 31.7 %collective-permute-start.2 = (bf16[4,128,1,1440]{1,3,0,2:T(8,128)(2,1)}, bf16[4,128,1,1440]{1,3,0,2:T(8,128)(2,1)}, u32[]{:S(2)}, u32[]{:S(2)}) collective-permute-start(bf16[4,128,1,1440]{1,3,0,2:T(8,128)(2,1)} %slice_bitcast_fusion.7), channel_id=1, source_target_pairs={{1,0},{2,1},{3,2},{4,3},{5,4},{6,5},{7,6},{8,7},{9,8},{10,9},{11,1... | collective-permute-start | bytes 4423688 | tf_op jit(solution)/shard_map/while/body/eval_jaxpr/ppermute | solution.py:19
  744.4 10.8 copy-start.4
  748.4 31.1 %collective-permute-start.3 = (bf16[4,128,1,1440]{1,3,0,2:T(8,128)(2,1)}, bf16[4,128,1,1440]{1,3,0,2:T(8,128)(2,1)S(1)}, u32[]{:S(2)}, u32[]{:S(2)}) collective-permute-start(bf16[4,128,1,1440]{1,3,0,2:T(8,128)(2,1)} %slice_bitcast_fusion.9), channel_id=1, source_target_pairs={{0,1},{1,2},{2,3},{3,4},{4,5},{5,6},{6,7},{7,8},{8,9},{9,10},{10,1... | collective-permute-start | bytes 4423688 | tf_op jit(solution)/shard_map/while/body/eval_jaxpr/ppermute | solution.py:16
  848.9 9.4 copy-start.12
  900.8 5.7 copy-start.5
  932.6 16.9 %copy-start.6 = (s32[256]{0:T(256)S(1)}, s32[256]{0:T(256)}, u32[]{:S(2)}) copy-start(s32[256]{0:T(256)} %compare_select_fusion) | copy-start | bytes 3076
  932.6 17.0 %copy-start.10 = (pred[256]{0:T(512)(128)(4,1)S(1)}, pred[256]{0:T(512)(128)(4,1)}, u32[]{:S(2)}) copy-start(pred[256]{0:T(512)(128)(4,1)} %compare_and_fusion) | copy-start | bytes 772
  932.6 49.5 %copy-start.8 = (f32[256]{0:T(256)S(1)}, f32[256]{0:T(256)}, u32[]{:S(2)}) copy-start(f32[256]{0:T(256)} %param.19) | copy-start | bytes 3076
  932.6 49.6 %copy-start.9 = (f32[256]{0:T(256)S(1)}, f32[256]{0:T(256)}, u32[]{:S(2)}) copy-start(f32[256]{0:T(256)} %param.18) | copy-start | bytes 3076
  932.6 54.4 %copy-start.3 = (bf16[4,4,16,4,1440]{4,1,2,3,0:T(4,128)(2,1)S(1)}, bf16[4,4,16,4,1440]{4,1,2,3,0:T(4,128)(2,1)}, u32[]{:S(2)}) copy-start(bf16[4,4,16,4,1440]{4,1,2,3,0:T(4,128)(2,1)} %get-tuple-element.40) | copy-start | bytes 8847364
  983.2 13.2 %all-to-all-start = ((f32[8,1,512]{2,1,0:T(1,128)}), f32[8,1,512]{2,1,0:T(1,128)S(1)}, u32[]{:S(2)}, u32[]{:S(2)}) async-start(f32[8,1,512]{2,1,0:T(1,128)} %reshape.114), calls=%async_computation | async-start | bytes 32768 | tf_op jit(solution)/shard_map/all_to_all | solution.py:87
  996.4 192.1 %all-to-all-start.1 = ((bf16[16,16,4,1440]{3,0,2,1:T(8,128)(2,1)}), bf16[16,16,4,1440]{3,0,2,1:T(8,128)(2,1)S(1)}, u32[]{:S(2)}, u32[]{:S(2)}) async-start(bf16[16,16,4,1440]{3,0,2,1:T(8,128)(2,1)} %reshape.71), calls=%async_computation.1 | async-start | bytes 6291456 | tf_op jit(solution)/shard_map/all_to_all | solution.py:107
  1001.2 161.4 %all-reduce.2.cloned.1.call-start = ((), (), s32[]{:S(2)}) async-start(), calls=%async_computation.3 | async-start | bytes 131072 | tf_op jit(solution)/shard_map/psum | solution.py:93
  (13 other events, 40.8 us)
Sparse Core Ops, SparseCore 0:
  1007.3 155.1 all-reduce.1
where the time goes:
time: 1260 us; the launch traced here: 1250 us
  local copies, waits for them, and re-layouts  568 us (45%)
  matrix products  227 us (18%)
  blocking collectives  165 us (13%)
  other arithmetic  102 us (8%)
  waiting for transfers between devices  101 us (8%)
  starting transfers between devices  63.9 us (5%)
  between operations  15.2 us (1%)
    conv_general_dilated x8, matrix products, convolve(): lax.conv_general_dilated(wrapped, kernel, (1, 1), 'VALID', dimension_numb...  223 us
    concatenate x16, local copies, waits for them, and re-layouts, convolve(): jnp.concatenate([padded[..., -1:], padded, padded[..., :1]], axis=-1)  220 us
    conv_general_dilated x24, local copies, waits for them, and re-layouts, convolve(): lax.conv_general_dilated(wrapped, kernel, (1, 1), 'VALID', dimension_numb...  112 us
    psum x1, blocking collectives, on_device(): gram, proj = lax.psum((gram_part, proj_part), ('ens', 'map'))  103 us
    convert_element_type x32, local copies, waits for them, and re-layouts, predicted_realization_group(): hidden = jax.nn.silu(inner).astype(jnp.bfloat16)  98.2 us
    psum x1, waiting for transfers between devices, on_device(): gram, proj = lax.psum((gram_part, proj_part), ('ens', 'map'))  56.2 us
    ppermute x8, starting transfers between devices, with_halo(): lax.ppermute(lax.slice_in_dim(block, block.shape[dim] - width, None, axis...  44.9 us
    conv_general_dilated x8, other arithmetic, convolve(): lax.conv_general_dilated(wrapped, kernel, (1, 1), 'VALID', dimension_numb...  44.6 us
  transfers between devices with their start and end apart: 19, of which 16 were waited for; matrix products, arithmetic and copies ran while one was open for 11% of the time, Pallas kernels for 0%

commit v1 on v0

v1 whole, which is shorter than its diff:
```python
import math

import jax
import jax.numpy as jnp
from jax import lax
from jax.experimental import pallas as pl
from jax.experimental.pallas import tpu as pltpu
from jax.sharding import PartitionSpec as P

FIELDS = 16
HID = 128
ROWS = 4
LON = 1440
RING = 1536
SLOTS = 256
GROUP = 16
PLANES = ROWS * FIELDS * GROUP
N_ENS = 8
MEMBERS = 128
VMEM_LIMIT = 56 * 1024 * 1024


def forecast_kernel(
    index_ref,
    x_ref,
    top_ref,
    bottom_ref,
    first_top_ref,
    first_bottom_ref,
    second_ref,
    bias_ref,
    fields_ref,
    observed_ref,
    held_ref,
):
    member = pl.program_id(0)
    main = x_ref[0].reshape(ROWS * FIELDS, LON)
    stack = jnp.concatenate(
        [top_ref[0].reshape(2 * FIELDS, LON), main, bottom_ref[0].reshape(2 * FIELDS, LON)],
        axis=0,
    )
    ring = jnp.concatenate([stack, stack[:, :64], stack[:, LON - 32 :]], axis=1)
    left = pltpu.roll(ring, 1, 1)
    right = pltpu.roll(ring, RING - 1, 1)
    ones = jnp.ones((16, RING), jnp.bfloat16)

    def hidden_rows(low, weights_ref):
        high = low + 5 * FIELDS
        taps = jnp.concatenate([left[low:high], ring[low:high], right[low:high], ones], axis=0)
        half = jnp.dot(weights_ref[...], taps, preferred_element_type=jnp.float32)
        return (half * jnp.tanh(half) + half).astype(jnp.bfloat16)

    hidden = jnp.concatenate(
        [hidden_rows(0, first_top_ref), hidden_rows(3 * FIELDS, first_bottom_ref)], axis=0
    )
    outer = jnp.dot(second_ref[...], hidden, preferred_element_type=jnp.float32)
    count = ROWS * FIELDS
    change = (
        pltpu.roll(outer[:count], 1, 1)
        + outer[count : 2 * count]
        + pltpu.roll(outer[2 * count :], RING - 1, 1)
    )
    base = main.astype(jnp.float32) + bias_ref[...]
    own = jnp.concatenate([base, base[:, : RING - LON]], axis=1) + change
    for tile in range(RING // 128):
        held_ref[pl.ds(tile * PLANES + member, count, stride=GROUP), :] = own[
            :, tile * 128 : (tile + 1) * 128
        ]

    @pl.when(member == pl.num_programs(0) - 1)
    def _():
        for field in range(FIELDS):
            for row in range(ROWS):
                at = (row * FIELDS + field) * GROUP
                for tile in range(RING // 128):
                    low, high = tile * 128, min(tile * 128 + 128, LON)
                    fields_ref[field // 2, (field % 2) * ROWS + row, :, low:high] = held_ref[
                        tile * PLANES + at : tile * PLANES + at + GROUP, : high - low
                    ].astype(jnp.bfloat16)
        lane = lax.broadcasted_iota(jnp.int32, (GROUP, 128), 1)
        for part in range(SLOTS // 128):

            def pick(slot, total):
                entry = index_ref[part * 128 + slot]
                plane = entry // LON
                column = entry - plane * LON
                at = (column // 128) * PLANES
                at += ((plane % ROWS) * FIELDS + plane // ROWS) * GROUP
                block = held_ref[pl.ds(pl.multiple_of(at, GROUP), GROUP), :]
                moved = pltpu.roll(block, (slot - column + 128 * 16) % 128, 1)
                return jnp.where(lane == slot, moved, total)

            total = lax.fori_loop(
                0, 128, pick, jnp.zeros((GROUP, 128), jnp.float32), unroll=8
            )
            observed_ref[:, part * 128 : (part + 1) * 128] = total.astype(jnp.bfloat16)


def forecast(index, own, top, bottom, first_top, first_bottom, second, bias):
    whole = lambda *shape: pl.BlockSpec(shape, lambda m, *_: (0,) * len(shape))
    return pl.pallas_call(
        forecast_kernel,
        grid_spec=pltpu.PrefetchScalarGridSpec(
            num_scalar_prefetch=1,
            grid=(GROUP,),
            in_specs=[
                pl.BlockSpec((1, ROWS, FIELDS, LON), lambda m, *_: (m, 0, 0, 0)),
                pl.BlockSpec((1, 2, FIELDS, LON), lambda m, *_: (m, 0, 0, 0)),
                pl.BlockSpec((1, 2, FIELDS, LON), lambda m, *_: (m, 0, 0, 0)),
                whole(*first_top.shape),
                whole(*first_bottom.shape),
                whole(*second.shape),
                whole(*bias.shape),
            ],
            out_specs=[whole(N_ENS, 8, GROUP, LON), whole(GROUP, SLOTS)],
            scratch_shapes=[pltpu.VMEM((RING // 128 * PLANES, 128), jnp.float32)],
        ),
        out_shape=[
            jax.ShapeDtypeStruct((N_ENS, 8, GROUP, LON), jnp.bfloat16),
            jax.ShapeDtypeStruct((GROUP, SLOTS), jnp.bfloat16),
        ],
        compiler_params=pltpu.CompilerParams(vmem_limit_bytes=VMEM_LIMIT),
    )(index, own, top, bottom, first_top, first_bottom, second, bias)


def products_kernel(observed_ref, count_ref, value_ref, sigma_ref, out_ref):
    observed = observed_ref[...].astype(jnp.float32)
    mean = jnp.sum(observed, axis=0, keepdims=True) / MEMBERS
    slot = lax.broadcasted_iota(jnp.int32, (1, SLOTS), 1)
    live = (slot < count_ref[0]).astype(jnp.float32)
    sigma = sigma_ref[...]
    anomalies = (observed - mean) * (live / (sigma * math.sqrt(MEMBERS - 1)))
    innov = live * (value_ref[...] - mean) / sigma
    left = jnp.concatenate([anomalies, jnp.broadcast_to(innov, (8, SLOTS))], axis=0)
    out_ref[...] = lax.dot_general(
        left,
        anomalies,
        (((1,), (1,)), ((), ())),
        precision=lax.Precision.HIGHEST,
        preferred_element_type=jnp.float32,
    )


def products(observed, count, value, sigma):
    vmem = pl.BlockSpec(memory_space=pltpu.VMEM)
    return pl.pallas_call(
        products_kernel,
        in_specs=[vmem, pl.BlockSpec(memory_space=pltpu.SMEM), vmem, vmem],
        out_specs=vmem,
        out_shape=jax.ShapeDtypeStruct((MEMBERS + 8, MEMBERS), jnp.float32),
    )(observed, count, value.reshape(1, SLOTS), sigma.reshape(1, SLOTS))


def transform_kernel(products_ref, factor_ref, weights_ref, transform_ref):
    n = MEMBERS
    row = lax.broadcasted_iota(jnp.int32, (n, n), 0)
    column = lax.broadcasted_iota(jnp.int32, (n, n), 1)
    eye = (row == column).astype(jnp.float32)
    gram = products_ref[0:n, :] + eye
    blocks = [
        [gram[b : b + 8], eye[b : b + 8]] for b in range(0, n, 8)
    ]
    within = lax.broadcasted_iota(jnp.int32, (8, n), 0)
    for b in range(n // 8):
        upper, inverse = blocks[b]
        for k in range(8):
            j = 8 * b + k
            scale = lax.rsqrt(upper[k : k + 1, j : j + 1])
            share = upper[:, j : j + 1] * scale
            upper_row = upper[k : k + 1] * scale
            inverse_row = inverse[k : k + 1] * scale
            share = jnp.where(within > k, share, 0.0)
            upper = jnp.where(within == k, upper_row, upper - share * upper_row)
            inverse = jnp.where(within == k, inverse_row, inverse - share * inverse_row)
        blocks[b] = [upper, inverse]
        turned = upper.T
        for t in range(b + 1, n // 8):
            later_upper, later_inverse = blocks[t]
            for k in range(8):
                share = turned[8 * t : 8 * t + 8, k : k + 1]
                later_upper = later_upper - share * upper[k : k + 1]
                later_inverse = later_inverse - share * inverse[k : k + 1]
            blocks[t] = [later_upper, later_inverse]
    upper = jnp.concatenate([pair[0] for pair in blocks], axis=0)
    inverse = jnp.concatenate([pair[1] for pair in blocks], axis=0)
    factor_ref[...] = jnp.where(row <= column, upper, 0.0).T
    proj = products_ref[n : n + 1, :]
    middle = jnp.sum(inverse * proj, axis=1, keepdims=True)
    weights = jnp.sum(inverse * middle, axis=0, keepdims=True) / math.sqrt(n - 1)
    weights_ref[...] = weights
    coeff = inverse + weights
    transform = coeff - jnp.mean(coeff, axis=1, keepdims=True) + 1.0 / n
    transform_ref[...] = transform.astype(jnp.bfloat16)


def transform_of(summed):
    vmem = pl.BlockSpec(memory_space=pltpu.VMEM)
    return pl.pallas_call(
        transform_kernel,
        in_specs=[vmem],
        out_specs=[vmem, vmem, vmem],
        out_shape=[
            jax.ShapeDtypeStruct((MEMBERS, MEMBERS), jnp.float32),
            jax.ShapeDtypeStruct((1, MEMBERS), jnp.float32),
            jax.ShapeDtypeStruct((MEMBERS, MEMBERS), jnp.bfloat16),
        ],
    )(summed)


def update_kernel(transform_ref, fields_ref, out_ref):
    fields = fields_ref[:, 0].reshape(MEMBERS, LON)
    mixed = jnp.dot(transform_ref[...], fields, preferred_element_type=jnp.float32)
    out_ref[:, 0] = mixed.astype(jnp.bfloat16).reshape(N_ENS, GROUP, LON)


def update(transform, fields):
    block = pl.BlockSpec((N_ENS, 1, GROUP, LON), lambda k: (0, k, 0, 0))
    return pl.pallas_call(
        update_kernel,
        grid=(8,),
        in_specs=[pl.BlockSpec((MEMBERS, MEMBERS), lambda k: (0, 0)), block],
        out_specs=block,
        out_shape=jax.ShapeDtypeStruct((N_ENS, 8, GROUP, LON), jnp.bfloat16),
    )(transform, fields)


def first_weights(conv_in, bias_in, mask):
    kernel = conv_in.astype(jnp.float32) * 0.5
    by_tap = jnp.transpose(kernel, (0, 3, 2, 1))
    placed = [
        jnp.pad(by_tap, ((0, 0), (0, 0), (r, 2 - r), (0, 0))).reshape(HID, 15 * FIELDS)
        for r in range(3)
    ]
    half = bias_in * 0.5
    high = half.astype(jnp.bfloat16).astype(jnp.float32)
    middle = (half - high).astype(jnp.bfloat16).astype(jnp.float32)
    low = half - high - middle
    bias = jnp.pad(jnp.stack([high, middle, low], axis=1), ((0, 0), (0, 13)))
    rows = [jnp.concatenate([part, bias], axis=1) * mask[r] for r, part in enumerate(placed)]
    return jnp.concatenate(rows, axis=0).astype(jnp.bfloat16)


def second_weights(conv_out):
    by_tap = jnp.transpose(conv_out, (3, 0, 2, 1))
    placed = [jnp.pad(by_tap, ((0, 0), (0, 0), (r, 3 - r), (0, 0))) for r in range(ROWS)]
    return jnp.stack(placed, axis=1).reshape(3 * ROWS * FIELDS, 6 * HID)


def on_device(
    ensemble_weather,
    conv_in,
    bias_in,
    conv_out,
    bias_out,
    observed_entry_index,
    obs_count,
    obs_value,
    obs_sigma,
):
    tiles = lax.axis_size("map")
    tile = lax.axis_index("map")
    down = [(i, i + 1) for i in range(tiles - 1)]
    up = [(i + 1, i) for i in range(tiles - 1)]
    own = jnp.transpose(ensemble_weather, (0, 2, 1, 3))
    top = lax.ppermute(own[:, ROWS - 2 :], "map", down)
    bottom = lax.ppermute(own[:, :2], "map", up)
    one = jnp.float32(1.0)
    inner_top = (tile > 0).astype(jnp.float32)
    inner_bottom = (tile < tiles - 1).astype(jnp.float32)
    first_top = first_weights(conv_in, bias_in, [inner_top, one, one])
    first_bottom = first_weights(conv_in, bias_in, [one, one, inner_bottom])
    second = second_weights(conv_out)
    bias = jnp.tile(bias_out, ROWS).reshape(ROWS * FIELDS, 1)
    fields, observed = forecast(
        observed_entry_index, own, top, bottom, first_top, first_bottom, second, bias
    )
    observed = lax.all_gather(observed, "ens", axis=0, tiled=True)
    gathered = lax.all_to_all(fields, "ens", split_axis=0, concat_axis=0, tiled=True)
    summed = lax.psum(products(observed, obs_count, obs_value, obs_sigma), "map")
    factor, mean_weights, transform = transform_of(summed)
    mixed = update(transform, gathered)
    back = lax.all_to_all(mixed, "ens", split_axis=0, concat_axis=0, tiled=True)
    analysis = jnp.transpose(back.reshape(FIELDS, ROWS, GROUP, LON), (2, 0, 1, 3))
    return (analysis, factor, mean_weights.reshape(MEMBERS))


def solution(mesh):
    placed = (
        P("ens", None, "map", None),
        P(),
        P(),
        P(),
        P(),
        P("map"),
        P("map"),
        P("map"),
        P("map"),
    )
    return jax.shard_map(
        on_device,
        mesh=mesh,
        in_specs=placed,
        out_specs=(P("ens", None, "map", None), P(), P()),
        check_vma=False,
    )
```

time: 1260 us -> 305 us (0.24)
  local copies, waits for them, and re-layouts: 568 us -> 18.2 us
  matrix products: 227 us -> 0 us
  other arithmetic: 102 us -> 1.04 us
  blocking collectives: 165 us -> 89.1 us
  Pallas kernels: 0 us -> 59.4 us
  starting transfers between devices: 63.9 us -> 12.1 us
    conv_general_dilated x8 -> x0, matrix products: 223 us -> none  [convolve(): lax.conv_general_dilated(wrapped, kernel, (1, 1), 'VALID', dimension_numb...]
    concatenate x16 -> x0, local copies, waits for them, and re-layouts: 220 us -> none  [convolve(): jnp.concatenate([padded[..., -1:], padded, padded[..., :1]], axis=-1)]
    psum x2 -> x0, blocking collectives: 123 us -> none  [the longest x1 103 us: on_device(): gram, proj = lax.psum((gram_part, proj_part), ('ens', 'map'))]
    conv_general_dilated x24 -> x0, local copies, waits for them, and re-layouts: 112 us -> none  [convolve(): lax.conv_general_dilated(wrapped, kernel, (1, 1), 'VALID', dimension_numb...]
    convert_element_type x33 -> x0, local copies, waits for them, and re-layouts: 103 us -> none  [the longest x32 98.2 us: predicted_realization_group(): hidden = jax.nn.silu(inner).astype(jnp.bfloat16)]
    pallas_call x0 -> x4, Pallas kernels: none -> 59.4 us  [the longest x1 36.4 us: forecast(): pl.pallas_call(forecast_kernel, grid_spec=pltpu.PrefetchScalarGridSpec(nu...]
    ppermute x16 -> x2, starting transfers between devices: 55.2 us -> 5.88 us  [the longest x1 4.59 us: on_device(): top = lax.ppermute(own[:, ROWS - 2:], 'map', down)]
    conv_general_dilated x8 -> x0, other arithmetic: 44.6 us -> none  [convolve(): lax.conv_general_dilated(wrapped, kernel, (1, 1), 'VALID', dimension_numb...]
  transfers between devices with their start and end apart: 19 -> 4, of which waited for: 16 -> 3; matrix products, arithmetic and copies ran while one was open for 11% -> 2% of each run, Pallas kernels for 0% -> 5%
where the time goes in v1:
time: 305 us; the launch traced here: 304 us
  waiting for transfers between devices  109 us (36%)
  blocking collectives  89.1 us (29%)
  Pallas kernels  59.4 us (19%)
  local copies, waits for them, and re-layouts  18.2 us (6%)
  between operations  14.8 us (5%)
  starting transfers between devices  12.1 us (4%)
    psum x1, waiting for transfers between devices, on_device(): lax.psum(products(observed, obs_count, obs_value, obs_sigma), 'map')  80.6 us
    all_to_all x1, blocking collectives, on_device(): back = lax.all_to_all(mixed, 'ens', split_axis=0, concat_axis=0, tiled=True)  44.6 us
    all_gather x1, blocking collectives, on_device(): observed = lax.all_gather(observed, 'ens', axis=0, tiled=True)  44.5 us
    pallas_call x1, Pallas kernels, forecast(): pl.pallas_call(forecast_kernel, grid_spec=pltpu.PrefetchScalarGridSpec(nu...  36.4 us
    ppermute x1, waiting for transfers between devices, on_device(): top = lax.ppermute(own[:, ROWS - 2:], 'map', down)  24.9 us
    pallas_call x1, Pallas kernels, transform_of(): pl.pallas_call(transform_kernel, in_specs=[vmem], out_specs=[vmem, vmem,...  14.3 us
    pallas_call x1, Pallas kernels, update(): pl.pallas_call(update_kernel, grid=(8,), in_specs=[pl.BlockSpec((MEMBERS,...  6.9 us
    unnamed x18, local copies, waits for them, and re-layouts  6.72 us
  transfers between devices with their start and end apart: 4, of which 3 were waited for; matrix products, arithmetic and copies ran while one was open for 2% of the time, Pallas kernels for 5%

profile of v1, /device:TPU:1, one launch (start us, length us, event | category | flops | bytes accessed | tf_op | source)
XLA Modules:
  0.0 304.1 jit_solution(9668686061046106978)
XLA Ops:
  7.2 2.7 copy.48
  9.8 0.0 copy-start
  9.8 0.0 copy-start.7
  9.8 0.0 copy-start.4
  9.9 2.2 fusion.8
  12.1 0.4 copy-done
  12.5 0.0 copy-start.6
  12.5 4.6 %collective-permute-start = (bf16[16,2,16,1440]{3,2,1,0:T(8,128)(2,1)}, bf16[16,2,16,1440]{3,2,1,0:T(8,128)(2,1)S(1)}, u32[]{:S(2)}, u32[]{:S(2)}) collective-permute-start(bf16[16,2,16,1440]{3,2,1,0:T(8,128)(2,1)} %get-tuple-element.14), channel_id=1, source_target_pairs={{0,1},{1,2},{2,3},{3,4},{4,5},{5,6},{6,7},{7,8},{8,9},{9,10},{10,1... | collective-permute-start | bytes 4423688 | tf_op jit(solution)/shard_map/ppermute | solution.py:265
  17.1 1.3 collective-permute-start.1
  18.4 0.0 copy-done.7
  18.4 0.1 copy.35
  18.5 0.0 copy-done.4
  18.6 0.7 fusion.9
  19.2 0.1 copy.36
  19.3 1.0 copy.38
  20.3 0.6 pad.38
  21.0 0.9 copy.37
  21.9 1.0 pad_bitcast_fusion.3
  22.9 0.1 copy.39
  23.0 0.8 copy.49
  23.8 0.0 copy-done.6
  23.8 0.7 reshape_tile.4.bias_ref
  24.5 0.1 multiply_convert_fusion
  24.6 0.1 fusion.7
  24.7 0.8 fusion.1
  25.5 24.9 %collective-permute-done.top_ref = bf16[16,2,16,1440]{3,2,1,0:T(8,128)(2,1)S(1)} collective-permute-done((bf16[16,2,16,1440]{3,2,1,0:T(8,128)(2,1)}, bf16[16,2,16,1440]{3,2,1,0:T(8,128)(2,1)S(1)}, u32[]{:S(2)}, u32[]{:S(2)}) %collective-permute-start) | collective-permute-done | bytes 1474592 | tf_op jit(solution)/shard_map/ppermute | solution.py:265
  50.3 0.0 copy-start.2
  50.3 4.0 %collective-permute-done.1.bottom_ref = bf16[16,2,16,1440]{3,2,1,0:T(8,128)(2,1)S(1)} collective-permute-done((bf16[16,2,16,1440]{3,2,1,0:T(8,128)(2,1)}, bf16[16,2,16,1440]{3,2,1,0:T(8,128)(2,1)S(1)}, u32[]{:S(2)}, u32[]{:S(2)}) %collective-permute-start.1) | collective-permute-done | bytes 1474592 | tf_op jit(solution)/shard_map/ppermute | solution.py:266
  54.3 0.0 copy-start.3
  54.3 0.0 copy-done.2
  54.3 1.2 copy-done.3
  55.5 36.4 %shard_map.112 = (bf16[8,8,16,1440]{3,2,1,0:T(8,128)(2,1)}, bf16[16,256]{1,0:T(8,128)(2,1)}) custom-call(s32[256]{0:T(256)} %index_ref.1, bf16[16,4,16,1440]{3,2,1,0:T(8,128)(2,1)} %bitcast.36, bf16[16,2,16,1440]{3,2,1,0:T(8,128)(2,1)} %copy-done.2, bf16[16,2,16,1440]{3,2,1,0:T(8,128)(2,1)} %copy-done.3, bf16[384,256]{1,0:T(8,128)(2,1)} %get-tuple-element.18.first_top_ref, ...), custom_call_target="tpu_custom_call" | custom-call | tf_op jit(solution)/shard_map/pallas_call | solution.py:101
  91.9 0.0 copy-start.5
  91.9 6.2 %all-to-all-start = ((bf16[8,8,16,1440]{3,2,1,0:T(8,128)(2,1)}), bf16[8,8,16,1440]{3,2,1,0:T(8,128)(2,1)S(1)}, u32[]{:S(2)}, u32[]{:S(2)}) async-start(bf16[8,8,16,1440]{3,2,1,0:T(8,128)(2,1)} %get-tuple-element.10), calls=%async_computation | async-start | bytes 6291456 | tf_op jit(solution)/shard_map/all_to_all | solution.py:278
  98.1 0.0 all-reduce.10.cloned.1.call-start
  98.7 0.0 copy-done.5
  98.8 44.5 %all_gather.3.observed_ref = bf16[128,256]{1,0:T(8,128)(2,1)} all-gather(bf16[16,256]{1,0:T(8,128)(2,1)S(1)} %copy-done.5), channel_id=1, replica_groups=mesh['ens'=8,'map'=16] {'ens'}, dimensions={0}, use_global_device_ids=true | all-gather | bytes 73728 | tf_op jit(solution)/shard_map/all_gather | solution.py:277
  143.3 1.8 shard_map.113
  145.1 0.0 all-reduce.10.cloned.1.call-update
  145.1 80.6 %all-reduce.10.cloned.1.call-done.products_ref = f32[136,128]{1,0:T(8,128)} async-done(((f32[136,128]{1,0:T(8,128)}), f32[136,128]{1,0:T(8,128)}) %all-reduce.10.cloned.1.call-update) | async-done | bytes 69648 | tf_op jit(solution)/shard_map/psum | solution.py:279
  225.7 14.3 %shard_map.114 = (f32[128,128]{1,0:T(8,128)}, f32[1,128]{1,0:T(1,128)}, bf16[128,128]{1,0:T(8,128)(2,1)}) custom-call(f32[136,128]{1,0:T(8,128)} %all-reduce.10.cloned.1.call-done.products_ref), custom_call_target="tpu_custom_call" | custom-call | tf_op jit(solution)/shard_map/pallas_call | solution.py:198
  240.0 0.0 all-to-all-done.fields_ref
  240.0 0.0 copy-start.1
  240.0 1.7 copy-done.1
  241.7 6.9 %shard_map.115 = bf16[8,8,16,1440]{3,2,1,0:T(8,128)(2,1)} custom-call(bf16[128,128]{1,0:T(8,128)(2,1)} %get-tuple-element.9.transform_ref, bf16[8,8,16,1440]{3,2,1,0:T(8,128)(2,1)} %copy-done.1), custom_call_target="tpu_custom_call" | custom-call | tf_op jit(solution)/shard_map/pallas_call | solution.py:218
  248.6 44.6 %all_to_all.10 = bf16[8,8,16,1440]{3,2,1,0:T(8,128)(2,1)S(1)} all-to-all(bf16[8,8,16,1440]{3,2,1,0:T(8,128)(2,1)} %shard_map.115), channel_id=1, replica_groups=mesh['ens'=8,'map'=16] {'ens'}, dimensions={0} | all-to-all | bytes 5898240 | tf_op jit(solution)/shard_map/all_to_all | solution.py:282
  293.2 4.1 %copy.47 = bf16[16,4,16,1440]{3,1,0,2:T(4,128)(2,1)} copy(bf16[16,4,16,1440]{3,2,1,0:T(8,128)(2,1)S(1)} %bitcast.37) | data formatting | bytes 5898240 | tf_op jit(solution)/shard_map/reshape | solution.py:283
  (5 shorter events, 0.1 us)
Async XLA Ops:
  9.8 2.7 copy-start
  9.8 8.6 %copy-start.7 = (f32[128]{0:T(128)S(1)}, f32[128]{0:T(128)}, u32[]{:S(2)}) copy-start(f32[128]{0:T(128)} %param.11) | copy-start | bytes 1540
  9.8 8.7 %copy-start.4 = (bf16[128,16,3,3]{0,1,3,2:T(8,128)(2,1)S(1)}, bf16[128,16,3,3]{0,1,3,2:T(8,128)(2,1)}, u32[]{:S(2)}) copy-start(bf16[128,16,3,3]{0,1,3,2:T(8,128)(2,1)} %param.10) | copy-start | bytes 110596
  12.5 11.3 %copy-start.6 = (f32[16]{0:T(128)S(1)}, f32[16]{0:T(128)}, u32[]{:S(2)}) copy-start(f32[16]{0:T(128)} %param.13) | copy-start | bytes 196
  12.5 37.9 %collective-permute-start = (bf16[16,2,16,1440]{3,2,1,0:T(8,128)(2,1)}, bf16[16,2,16,1440]{3,2,1,0:T(8,128)(2,1)S(1)}, u32[]{:S(2)}, u32[]{:S(2)}) collective-permute-start(bf16[16,2,16,1440]{3,2,1,0:T(8,128)(2,1)} %get-tuple-element.14), channel_id=1, source_target_pairs={{0,1},{1,2},{2,3},{3,4},{4,5},{5,6},{6,7},{7,8},{8,9},{9,10},{10,1... | collective-permute-start | bytes 4423688 | tf_op jit(solution)/shard_map/ppermute | solution.py:265
  17.1 37.2 %collective-permute-start.1 = (bf16[16,2,16,1440]{3,2,1,0:T(8,128)(2,1)}, bf16[16,2,16,1440]{3,2,1,0:T(8,128)(2,1)S(1)}, u32[]{:S(2)}, u32[]{:S(2)}) collective-permute-start(bf16[16,2,16,1440]{3,2,1,0:T(8,128)(2,1)} %get-tuple-element.13), channel_id=1, source_target_pairs={{1,0},{2,1},{3,2},{4,3},{5,4},{6,5},{7,6},{8,7},{9,8},{10,9},{11,1... | collective-permute-start | bytes 4423688 | tf_op jit(solution)/shard_map/ppermute | solution.py:266
  50.3 4.0 %copy-start.2 = (bf16[16,2,16,1440]{3,2,1,0:T(8,128)(2,1)}, bf16[16,2,16,1440]{3,2,1,0:T(8,128)(2,1)S(1)}, u32[]{:S(2)}) copy-start(bf16[16,2,16,1440]{3,2,1,0:T(8,128)(2,1)S(1)} %collective-permute-done.top_ref) | copy-start | bytes 4423684
  54.3 1.2 copy-start.3
  91.9 6.8 %copy-start.5 = (bf16[16,256]{1,0:T(8,128)(2,1)S(1)}, bf16[16,256]{1,0:T(8,128)(2,1)}, u32[]{:S(2)}) copy-start(bf16[16,256]{1,0:T(8,128)(2,1)} %get-tuple-element.8) | copy-start | bytes 24580
  91.9 148.1 %all-to-all-start = ((bf16[8,8,16,1440]{3,2,1,0:T(8,128)(2,1)}), bf16[8,8,16,1440]{3,2,1,0:T(8,128)(2,1)S(1)}, u32[]{:S(2)}, u32[]{:S(2)}) async-start(bf16[8,8,16,1440]{3,2,1,0:T(8,128)(2,1)} %get-tuple-element.10), calls=%async_computation | async-start | bytes 6291456 | tf_op jit(solution)/shard_map/all_to_all | solution.py:278
  98.1 127.6 %all-reduce.10.cloned.1.call-start = ((), (), s32[]{:S(2)}) async-start(), calls=%async_computation.2 | async-start | bytes 139264 | tf_op jit(solution)/shard_map/psum | solution.py:279
  240.0 1.7 copy-start.1
Sparse Core Ops, SparseCore 0:
  145.2 80.4 all-reduce.9

commit v2 on v1

v2 whole, which is shorter than its diff:
```python
import functools
import math

import jax
import jax.numpy as jnp
from jax import lax
from jax.experimental import pallas as pl
from jax.experimental.pallas import tpu as pltpu
from jax.sharding import PartitionSpec as P

FIELDS = 16
HID = 128
ROWS = 4
LON = 1440
RING = 1536
SLOTS = 256
GROUP = 16
PLANES = ROWS * FIELDS
CHUNKS = 4
N_ENS = 8
MEMBERS = 128
VMEM_LIMIT = 56 * 1024 * 1024


def forecast_kernel(
    x_ref,
    top_ref,
    bottom_ref,
    first_top_ref,
    first_bottom_ref,
    second_ref,
    bias_ref,
    column_ref,
    plane_ref,
    earlier_ref,
    held_ref,
    fields_ref,
    observed_ref,
    *,
    start,
):
    del held_ref
    member = pl.program_id(0)
    main = x_ref[0].reshape(PLANES, LON)
    stack = jnp.concatenate(
        [top_ref[0].reshape(2 * FIELDS, LON), main, bottom_ref[0].reshape(2 * FIELDS, LON)],
        axis=0,
    )
    ring = jnp.concatenate([stack, stack[:, :64], stack[:, LON - 32 :]], axis=1)
    left = pltpu.roll(ring, 1, 1)
    right = pltpu.roll(ring, RING - 1, 1)
    ones = jnp.ones((16, RING), jnp.bfloat16)

    def hidden_rows(low, weights_ref):
        high = low + 5 * FIELDS
        taps = jnp.concatenate([left[low:high], ring[low:high], right[low:high], ones], axis=0)
        half = jnp.dot(weights_ref[...], taps, preferred_element_type=jnp.float32)
        return (half * jnp.tanh(half) + half).astype(jnp.bfloat16)

    hidden = jnp.concatenate(
        [hidden_rows(0, first_top_ref), hidden_rows(3 * FIELDS, first_bottom_ref)], axis=0
    )
    outer = jnp.dot(second_ref[...], hidden, preferred_element_type=jnp.float32)
    change = (
        pltpu.roll(outer[:PLANES], 1, 1)
        + outer[PLANES : 2 * PLANES]
        + pltpu.roll(outer[2 * PLANES :], RING - 1, 1)
    )
    base = ring[2 * FIELDS : 2 * FIELDS + PLANES].astype(jnp.float32) + bias_ref[...]
    own = (base + change).astype(jnp.bfloat16)
    fields_ref[:, 0] = own[:, :LON].reshape(N_ENS, 8, LON)
    picked = jnp.dot(own, column_ref[...], preferred_element_type=jnp.float32)
    here = lax.broadcasted_iota(jnp.int32, (PLANES, SLOTS), 0) == plane_ref[...]

    @pl.when(member == 0)
    def _():
        observed_ref[...] = earlier_ref[...]

    observed_ref[pl.ds(start + member, 1), :] = jnp.sum(
        jnp.where(here, picked, 0.0), axis=0, keepdims=True
    )


def cost(microseconds):
    return pl.CostEstimate(
        flops=int(microseconds * 1e9), transcendentals=0, bytes_accessed=int(microseconds * 1e6)
    )


def forecast(start, own, top, bottom, *shared, fields):
    count = top.shape[0]
    whole = lambda array: pl.BlockSpec(array.shape, lambda m: (0,) * array.ndim)
    in_specs = [
        pl.BlockSpec((1, ROWS, FIELDS, LON), lambda m: (start + m, 0, 0, 0)),
        pl.BlockSpec((1, 2, FIELDS, LON), lambda m: (m, 0, 0, 0)),
        pl.BlockSpec((1, 2, FIELDS, LON), lambda m: (m, 0, 0, 0)),
    ]
    in_specs += [whole(array) for array in shared] + [pl.BlockSpec(memory_space=pl.ANY)]
    arrays = [own, top, bottom, *shared, fields]
    kernel = functools.partial(forecast_kernel, start=start)
    aliases = {len(arrays) - 1: 0}
    if fields is None:
        arrays, in_specs, aliases = arrays[:-1], in_specs[:-1], {}
        kernel = lambda *refs: forecast_kernel(*refs[:-2], None, *refs[-2:], start=start)
    return pl.pallas_call(
        kernel,
        grid=(count,),
        in_specs=in_specs,
        out_specs=[
            pl.BlockSpec((N_ENS, 1, 8, LON), lambda m: (0, start + m, 0, 0)),
            pl.BlockSpec((GROUP, SLOTS), lambda m: (0, 0)),
        ],
        out_shape=[
            jax.ShapeDtypeStruct((N_ENS, GROUP, 8, LON), jnp.bfloat16),
            jax.ShapeDtypeStruct((GROUP, SLOTS), jnp.float32),
        ],
        input_output_aliases=aliases,
        cost_estimate=cost(10),
        compiler_params=pltpu.CompilerParams(vmem_limit_bytes=VMEM_LIMIT),
    )(*arrays)


def products_kernel(place_ref, count_ref, value_ref, sigma_ref, *refs):
    pieces, out_ref, held_ref = refs[:N_ENS], refs[N_ENS], refs[N_ENS + 1]
    for step, piece in enumerate(pieces):
        at = pl.multiple_of(place_ref[step] * GROUP, GROUP)
        held_ref[pl.ds(at, GROUP), :] = piece[...]
    observed = held_ref[...]
    mean = jnp.sum(observed, axis=0, keepdims=True) / MEMBERS
    slot = lax.broadcasted_iota(jnp.int32, (1, SLOTS), 1)
    live = (slot < count_ref[0]).astype(jnp.float32)
    sigma = sigma_ref[...]
    anomalies = (observed - mean) * (live / (sigma * math.sqrt(MEMBERS - 1)))
    innov = live * (value_ref[...] - mean) / sigma
    left = jnp.concatenate([anomalies, jnp.broadcast_to(innov, (8, SLOTS))], axis=0)
    out_ref[...] = lax.dot_general(
        left,
        anomalies,
        (((1,), (1,)), ((), ())),
        precision=lax.Precision.HIGHEST,
        preferred_element_type=jnp.float32,
    )


def products(pieces, places, count, value, sigma):
    vmem = pl.BlockSpec(memory_space=pltpu.VMEM)
    smem = pl.BlockSpec(memory_space=pltpu.SMEM)
    return pl.pallas_call(
        products_kernel,
        in_specs=[smem, smem] + [vmem] * (2 + N_ENS),
        out_specs=vmem,
        out_shape=jax.ShapeDtypeStruct((MEMBERS + 8, MEMBERS), jnp.float32),
        cost_estimate=cost(2),
        scratch_shapes=[pltpu.VMEM((MEMBERS, SLOTS), jnp.float32)],
    )(places, count, value.reshape(1, SLOTS), sigma.reshape(1, SLOTS), *pieces)


def transform_kernel(a_ref, b_ref, c_ref, d_ref, factor_ref, weights_ref, transform_ref):
    n = MEMBERS
    total = (a_ref[...] + b_ref[...]) + (c_ref[...] + d_ref[...])
    row = lax.broadcasted_iota(jnp.int32, (n, n), 0)
    column = lax.broadcasted_iota(jnp.int32, (n, n), 1)
    eye = (row == column).astype(jnp.float32)
    gram = total[0:n] + eye
    blocks = [
        [gram[b : b + 8], eye[b : b + 8]] for b in range(0, n, 8)
    ]
    within = lax.broadcasted_iota(jnp.int32, (8, n), 0)
    for b in range(n // 8):
        upper, inverse = blocks[b]
        for k in range(8):
            j = 8 * b + k
            scale = lax.rsqrt(upper[k : k + 1, j : j + 1])
            share = upper[:, j : j + 1] * scale
            upper_row = upper[k : k + 1] * scale
            inverse_row = inverse[k : k + 1] * scale
            share = jnp.where(within > k, share, 0.0)
            upper = jnp.where(within == k, upper_row, upper - share * upper_row)
            inverse = jnp.where(within == k, inverse_row, inverse - share * inverse_row)
        blocks[b] = [upper, inverse]
        turned = upper.T
        for t in range(b + 1, n // 8):
            later_upper, later_inverse = blocks[t]
            for k in range(8):
                share = turned[8 * t : 8 * t + 8, k : k + 1]
                later_upper = later_upper - share * upper[k : k + 1]
                later_inverse = later_inverse - share * inverse[k : k + 1]
            blocks[t] = [later_upper, later_inverse]
    upper = jnp.concatenate([pair[0] for pair in blocks], axis=0)
    inverse = jnp.concatenate([pair[1] for pair in blocks], axis=0)
    factor_ref[...] = jnp.where(row <= column, upper, 0.0).T
    proj = total[n : n + 1]
    middle = jnp.sum(inverse * proj, axis=1, keepdims=True)
    weights = jnp.sum(inverse * middle, axis=0, keepdims=True) / math.sqrt(n - 1)
    weights_ref[...] = weights
    coeff = inverse + weights
    transform = coeff - jnp.mean(coeff, axis=1, keepdims=True) + 1.0 / n
    transform_ref[...] = transform.astype(jnp.bfloat16)


def transform_of(parts):
    vmem = pl.BlockSpec(memory_space=pltpu.VMEM)
    return pl.pallas_call(
        transform_kernel,
        in_specs=[vmem] * 4,
        out_specs=[vmem, vmem, vmem],
        out_shape=[
            jax.ShapeDtypeStruct((MEMBERS, MEMBERS), jnp.float32),
            jax.ShapeDtypeStruct((1, MEMBERS), jnp.float32),
            jax.ShapeDtypeStruct((MEMBERS, MEMBERS), jnp.bfloat16),
        ],
        cost_estimate=cost(12),
    )(*parts)


def update_kernel(transform_ref, fields_ref, out_ref, spread_ref):
    rows = MEMBERS * 8

    @pl.when(pl.program_id(0) == 0)
    def _():
        member = lax.broadcasted_iota(jnp.int32, (rows, MEMBERS), 0) // 8
        column = lax.broadcasted_iota(jnp.int32, (rows, MEMBERS), 1)
        repeat = (member == column).astype(jnp.bfloat16)
        tall = jnp.dot(repeat, transform_ref[...], preferred_element_type=jnp.float32)
        wide = lax.dot_general(
            tall.astype(jnp.bfloat16),
            repeat,
            (((1,), (1,)), ((), ())),
            preferred_element_type=jnp.float32,
        )
        plane = lax.broadcasted_iota(jnp.int32, (rows, rows), 0) % 8
        same = plane == lax.broadcasted_iota(jnp.int32, (rows, rows), 1) % 8
        spread_ref[...] = jnp.where(same, wide, 0.0).astype(jnp.bfloat16)

    mixed = jnp.dot(spread_ref[...], fields_ref[...], preferred_element_type=jnp.float32)
    out_ref[...] = mixed.astype(jnp.bfloat16)


def update(transform, fields):
    rows = MEMBERS * 8
    block = pl.BlockSpec((rows, 256), lambda k: (0, k))
    return pl.pallas_call(
        update_kernel,
        grid=(RING // 256,),
        in_specs=[pl.BlockSpec((MEMBERS, MEMBERS), lambda k: (0, 0)), block],
        out_specs=block,
        out_shape=jax.ShapeDtypeStruct((rows, LON), jnp.bfloat16),
        scratch_shapes=[pltpu.VMEM((rows, rows), jnp.bfloat16)],
        cost_estimate=cost(6),
        compiler_params=pltpu.CompilerParams(vmem_limit_bytes=VMEM_LIMIT),
    )(transform, fields.reshape(rows, LON)).reshape(fields.shape)


def first_weights(conv_in, bias_in, mask):
    kernel = conv_in.astype(jnp.float32) * 0.5
    by_tap = jnp.transpose(kernel, (0, 3, 2, 1))
    placed = [
        jnp.pad(by_tap, ((0, 0), (0, 0), (r, 2 - r), (0, 0))).reshape(HID, 15 * FIELDS)
        for r in range(3)
    ]
    half = bias_in * 0.5
    high = half.astype(jnp.bfloat16).astype(jnp.float32)
    middle = (half - high).astype(jnp.bfloat16).astype(jnp.float32)
    low = half - high - middle
    bias = jnp.pad(jnp.stack([high, middle, low], axis=1), ((0, 0), (0, 13)))
    rows = [jnp.concatenate([part, bias], axis=1) * mask[r] for r, part in enumerate(placed)]
    return jnp.concatenate(rows, axis=0).astype(jnp.bfloat16)


def second_weights(conv_out):
    by_tap = jnp.transpose(conv_out, (3, 0, 2, 1))
    placed = [jnp.pad(by_tap, ((0, 0), (0, 0), (r, 3 - r), (0, 0))) for r in range(ROWS)]
    return jnp.stack(placed, axis=1).reshape(3 * ROWS * FIELDS, 6 * HID)


def on_device(
    ensemble_weather,
    conv_in,
    bias_in,
    conv_out,
    bias_out,
    observed_entry_index,
    obs_count,
    obs_value,
    obs_sigma,
):
    tiles = lax.axis_size("map")
    tile = lax.axis_index("map")
    own_place = lax.axis_index("ens")
    down = [(i, i + 1) for i in range(tiles - 1)]
    up = [(i + 1, i) for i in range(tiles - 1)]

    def swap(value, axis, step):
        pairs = [(i, i ^ step) for i in range(lax.axis_size(axis))]
        return lax.ppermute(value, axis, pairs)

    own = jnp.transpose(ensemble_weather, (0, 2, 1, 3))
    share = GROUP // CHUNKS
    halos = []
    for chunk in range(CHUNKS):
        part = own[chunk * share : (chunk + 1) * share]
        edges = (part[:, ROWS - 2 :], part[:, :2])
        if halos:
            edges, halos[-1] = lax.optimization_barrier((edges, halos[-1]))
        halos.append((lax.ppermute(edges[0], "map", down), lax.ppermute(edges[1], "map", up)))
    one = jnp.float32(1.0)
    inner_top = (tile > 0).astype(jnp.float32)
    inner_bottom = (tile < tiles - 1).astype(jnp.float32)
    first_top = first_weights(conv_in, bias_in, [inner_top, one, one])
    first_bottom = first_weights(conv_in, bias_in, [one, one, inner_bottom])
    second = second_weights(conv_out)
    bias = jnp.tile(bias_out, ROWS).reshape(PLANES, 1)
    plane = observed_entry_index // LON
    column = observed_entry_index - plane * LON
    picks = (jnp.arange(RING)[:, None] == column[None, :]).astype(jnp.bfloat16)
    plane = ((plane % ROWS) * FIELDS + plane // ROWS).reshape(1, SLOTS)

    exchange = lambda value: lax.all_to_all(
        value, "ens", split_axis=0, concat_axis=0, tiled=True
    )
    fields, observed = None, jnp.zeros((GROUP, SLOTS), jnp.float32)
    for chunk, (top, bottom) in enumerate(halos):
        fields, observed = forecast(
            chunk * share,
            own,
            top,
            bottom,
            first_top,
            first_bottom,
            second,
            bias,
            picks,
            plane,
            observed,
            fields=fields,
        )
    pieces = [observed] + [swap(observed, "ens", step) for step in range(1, N_ENS)]
    places = jnp.bitwise_xor(own_place, jnp.arange(N_ENS, dtype=jnp.int32))
    pieces, fields = lax.optimization_barrier((pieces, fields))
    gathered = exchange(fields)
    part = products(pieces, places, obs_count, obs_value, obs_sigma)
    near = [part] + [swap(part, "map", step) for step in (1, 2, 3)]
    row = (near[0] + near[1]) + (near[2] + near[3])
    factor, mean_weights, transform = transform_of(
        [row] + [swap(row, "map", step) for step in (4, 8, 12)]
    )
    back = exchange(update(transform, gathered))
    back = back.reshape(ROWS, 2, GROUP, 8, LON)
    analysis = jnp.transpose(back, (2, 1, 3, 0, 4)).reshape(GROUP, FIELDS, ROWS, LON)
    return (analysis, factor, mean_weights.reshape(MEMBERS))


def solution(mesh):
    placed = (
        P("ens", None, "map", None),
        P(),
        P(),
        P(),
        P(),
        P("map"),
        P("map"),
        P("map"),
        P("map"),
    )
    return jax.shard_map(
        on_device,
        mesh=mesh,
        in_specs=placed,
        out_specs=(P("ens", None, "map", None), P(), P()),
        check_vma=False,
    )
```

time: 305 us -> 199 us (0.65)
  waiting for transfers between devices: 109 us -> 18.7 us
  blocking collectives: 89.1 us -> 44.4 us
  starting transfers between devices: 12.1 us -> 50 us
  between operations: 14.8 us -> 1.74 us
  Pallas kernels: 59.4 us -> 63.8 us
  local copies, waits for them, and re-layouts: 18.2 us -> 14.9 us
  other arithmetic: 1.04 us -> 4.23 us
    psum x1 -> x0, waiting for transfers between devices: 80.6 us -> none  [on_device(): lax.psum(products(observed, obs_count, obs_value, obs_sigma), 'map')]
    all_gather x1 -> x0, blocking collectives: 44.5 us -> none  [on_device(): observed = lax.all_gather(observed, 'ens', axis=0, tiled=True)]
    ppermute x2 -> x21, starting transfers between devices: 5.88 us -> 45.2 us  [the longest x13 23.4 us: swap(): return lax.ppermute(value, axis, pairs)]
    ppermute x2 -> x21, waiting for transfers between devices: 28.8 us -> 18.7 us  [the longest x13 13.3 us: swap(): return lax.ppermute(value, axis, pairs)]
    pallas_call x4 -> x7, Pallas kernels: 59.4 us -> 63.8 us  [the longest x4 39.5 us: forecast(): pl.pallas_call(kernel, grid=(count,), in_specs=in_specs, out_specs=[pl.Bl...]
    unnamed x18 -> x50, local copies, waits for them, and re-layouts: 6.72 us -> 7.7 us
  transfers between devices with their start and end apart: 4 -> 22, of which waited for: 3 -> 8; matrix products, arithmetic and copies ran while one was open for 2% -> 3% of each run, Pallas kernels for 5% -> 23%
where the time goes in v2:
time: 199 us; the launch traced here: 198 us
  Pallas kernels  63.8 us (32%)
  starting transfers between devices  50 us (25%)
  blocking collectives  44.4 us (22%)
  waiting for transfers between devices  18.7 us (9%)
  local copies, waits for them, and re-layouts  14.9 us (7%)
  other arithmetic  4.23 us (2%)
    all_to_all x1, blocking collectives, on_device(): lax.all_to_all(value, 'ens', split_axis=0, concat_axis=0, tiled=True)  44.4 us
    pallas_call x4, Pallas kernels, forecast(): pl.pallas_call(kernel, grid=(count,), in_specs=in_specs, out_specs=[pl.Bl...  39.5 us
    ppermute x13, starting transfers between devices, swap(): return lax.ppermute(value, axis, pairs)  23.4 us
    ppermute x4, starting transfers between devices, on_device(): lax.ppermute(edges[0], 'map', down)  16.7 us
    pallas_call x1, Pallas kernels, transform_of(): pl.pallas_call(transform_kernel, in_specs=[vmem] * 4, out_specs=[vmem, vm...  14.4 us
    ppermute x13, waiting for transfers between devices, swap(): return lax.ppermute(value, axis, pairs)  13.3 us
    pallas_call x1, Pallas kernels, update(): pl.pallas_call(update_kernel, grid=(RING // 256,), in_specs=[pl.BlockSpec...  8.14 us
    unnamed x50, local copies, waits for them, and re-layouts  7.7 us
  transfers between devices with their start and end apart: 22, of which 8 were waited for; matrix products, arithmetic and copies ran while one was open for 3% of the time, Pallas kernels for 23%

profile of v2, /device:TPU:1, one launch (start us, length us, event | category | flops | bytes accessed | tf_op | source)
XLA Modules:
  0.0 197.8 jit_solution(12493128498705175929)
XLA Ops:
  0.6 2.7 %copy.58 = bf16[16,16,4,1440]{3,1,2,0:T(8,128)(2,1)S(1)} copy(bf16[16,16,4,1440]{3,2,1,0:T(4,128)(2,1)} %param.9) | data formatting | bytes 5898240 | tf_op args[0]
  3.3 1.3 fusion.11
  5.1 5.3 %collective-permute-start = (bf16[4,2,16,1440]{3,2,1,0:T(8,128)(2,1)}, bf16[4,2,16,1440]{3,2,1,0:T(8,128)(2,1)}, u32[]{:S(2)}, u32[]{:S(2)}) collective-permute-start(bf16[4,2,16,1440]{3,2,1,0:T(8,128)(2,1)} %get-tuple-element.70), channel_id=1, source_target_pairs={{0,1},{1,2},{2,3},{3,4},{4,5},{5,6},{6,7},{7,8},{8,9},{9,10},{10,1... | collective-permute-start | bytes 1105928 | tf_op jit(solution)/shard_map/ppermute | solution.py:305
  10.4 1.3 collective-permute-start.1
  12.4 0.8 copy.59
  13.2 0.5 fusion.10
  13.7 0.7 reshape_tile.4.refs_6_.bias_ref
  14.6 0.8 fusion.2
  15.4 1.2 fusion.refs_7_.column_ref
  16.6 1.0 collective-permute-done.refs_1_
  17.7 4.3 %collective-permute-done.1.refs_2_ = bf16[4,2,16,1440]{3,2,1,0:T(8,128)(2,1)} collective-permute-done((bf16[4,2,16,1440]{3,2,1,0:T(8,128)(2,1)S(1)}, bf16[4,2,16,1440]{3,2,1,0:T(8,128)(2,1)}, u32[]{:S(2)}, u32[]{:S(2)}) %collective-permute-start.1) | collective-permute-done | bytes 368672 | tf_op jit(solution)/shard_map/ppermute | solution.py:305
  22.0 2.8 %collective-permute-start.2 = (bf16[4,2,16,1440]{3,2,1,0:T(8,128)(2,1)S(1)}, bf16[4,2,16,1440]{3,2,1,0:T(8,128)(2,1)S(1)}, u32[]{:S(2)}, u32[]{:S(2)}) collective-permute-start(bf16[4,2,16,1440]{3,2,1,0:T(8,128)(2,1)S(1)} %get-tuple-element.35), channel_id=1, source_target_pairs={{0,1},{1,2},{2,3},{3,4},{4,5},{5,6},{6,7},{7,8},{8,9},{9,10},{10,1... | collective-permute-start | bytes 1105928 | tf_op jit(solution)/shard_map/ppermute | solution.py:305
  24.8 1.3 collective-permute-start.3
  26.1 0.6 broadcast_in_dim.2.refs_9_
  26.7 9.9 %shard_map.112 = (bf16[8,16,8,1440]{3,2,1,0:T(8,128)(2,1)}, f32[16,256]{1,0:T(8,128)}) custom-call(bf16[16,4,16,1440]{3,2,1,0:T(8,128)(2,1)} %bitcast.39, bf16[4,2,16,1440]{3,2,1,0:T(8,128)(2,1)} %collective-permute-done.refs_1_, bf16[4,2,16,1440]{3,2,1,0:T(8,128)(2,1)} %collective-permute-done.1.refs_2_, ...), custom_call_target="tpu_custom_call" | custom-call | flops 10000000000 | bytes 10000000 | tf_op jit(solution)/shard_map/pallas_call | solution.py:105
  36.6 4.0 %collective-permute-start.4 = (bf16[4,2,16,1440]{3,2,1,0:T(8,128)(2,1)S(1)}, bf16[4,2,16,1440]{3,2,1,0:T(8,128)(2,1)S(1)}, u32[]{:S(2)}, u32[]{:S(2)}) collective-permute-start(bf16[4,2,16,1440]{3,2,1,0:T(8,128)(2,1)S(1)} %get-tuple-element.37), channel_id=1, source_target_pairs={{0,1},{1,2},{2,3},{3,4},{4,5},{5,6},{6,7},{7,8},{8,9},{9,10},{10,1... | collective-permute-start | bytes 1105928 | tf_op jit(solution)/shard_map/ppermute | solution.py:305
  40.7 1.3 collective-permute-start.5
  42.0 9.9 %shard_map.113 = (bf16[8,16,8,1440]{3,2,1,0:T(8,128)(2,1)}, f32[16,256]{1,0:T(8,128)}) custom-call(bf16[16,4,16,1440]{3,2,1,0:T(8,128)(2,1)} %bitcast.40, bf16[4,2,16,1440]{3,2,1,0:T(8,128)(2,1)} %copy-done.8, bf16[4,2,16,1440]{3,2,1,0:T(8,128)(2,1)} %copy-done.10, ...), custom_call_target="tpu_custom_call", output_to_operand_aliasing={{0}: (10, {})} | custom-call | flops 10000000000 | bytes 10000000 | tf_op jit(solution)/shard_map/pallas_call | solution.py:105
  51.9 4.6 %collective-permute-start.6 = (bf16[4,2,16,1440]{3,2,1,0:T(8,128)(2,1)S(1)}, bf16[4,2,16,1440]{3,2,1,0:T(8,128)(2,1)S(1)}, u32[]{:S(2)}, u32[]{:S(2)}) collective-permute-start(bf16[4,2,16,1440]{3,2,1,0:T(8,128)(2,1)S(1)} %get-tuple-element.39), channel_id=1, source_target_pairs={{0,1},{1,2},{2,3},{3,4},{4,5},{5,6},{6,7},{7,8},{8,9},{9,10},{10,1... | collective-permute-start | bytes 1105928 | tf_op jit(solution)/shard_map/ppermute | solution.py:305
  56.5 1.3 collective-permute-start.7
  57.8 9.9 %shard_map.114 = (bf16[8,16,8,1440]{3,2,1,0:T(8,128)(2,1)}, f32[16,256]{1,0:T(8,128)}) custom-call(bf16[16,4,16,1440]{3,2,1,0:T(8,128)(2,1)} %bitcast.41, bf16[4,2,16,1440]{3,2,1,0:T(8,128)(2,1)} %copy-done.9, bf16[4,2,16,1440]{3,2,1,0:T(8,128)(2,1)} %copy-done.12, ...), custom_call_target="tpu_custom_call", output_to_operand_aliasing={{0}: (10, {})} | custom-call | flops 10000000000 | bytes 10000000 | tf_op jit(solution)/shard_map/pallas_call | solution.py:105
  67.8 0.7 copy-done.11
  68.6 9.8 %shard_map.115 = (bf16[8,16,8,1440]{3,2,1,0:T(8,128)(2,1)}, f32[16,256]{1,0:T(8,128)}) custom-call(bf16[16,4,16,1440]{3,2,1,0:T(8,128)(2,1)} %bitcast.42, bf16[4,2,16,1440]{3,2,1,0:T(8,128)(2,1)} %copy-done.11, bf16[4,2,16,1440]{3,2,1,0:T(8,128)(2,1)} %copy-done.13, ...), custom_call_target="tpu_custom_call", output_to_operand_aliasing={{0}: (10, {})} | custom-call | flops 10000000000 | bytes 10000000 | tf_op jit(solution)/shard_map/pallas_call | solution.py:105
  78.5 3.8 %collective-permute-start.10 = (f32[16,256]{1,0:T(8,128)}, f32[16,256]{1,0:T(8,128)S(1)}, u32[]{:S(2)}, u32[]{:S(2)}) collective-permute-start(f32[16,256]{1,0:T(8,128)} %get-tuple-element.55.refs_0_), channel_id=1, source_target_pairs={{0,48},{16,32},{32,16},{48,0},{64,112},{80,96},{96,80},{112,64},{1... | collective-permute-start | bytes 49160 | tf_op jit(solution)/shard_map/ppermute | solution.py:295
  82.2 2.5 %collective-permute-start.11 = (f32[16,256]{1,0:T(8,128)}, f32[16,256]{1,0:T(8,128)S(1)}, u32[]{:S(2)}, u32[]{:S(2)}) collective-permute-start(f32[16,256]{1,0:T(8,128)} %get-tuple-element.55.refs_0_), channel_id=1, source_target_pairs={{0,64},{16,80},{32,96},{48,112},{64,0},{80,16},{96,32},{112,48},{1... | collective-permute-start | bytes 49160 | tf_op jit(solution)/shard_map/ppermute | solution.py:295
  84.7 2.2 %collective-permute-start.13 = (f32[16,256]{1,0:T(8,128)}, f32[16,256]{1,0:T(8,128)S(1)}, u32[]{:S(2)}, u32[]{:S(2)}) collective-permute-start(f32[16,256]{1,0:T(8,128)} %get-tuple-element.55.refs_0_), channel_id=1, source_target_pairs={{0,96},{16,112},{32,64},{48,80},{64,32},{80,48},{96,0},{112,16},{1... | collective-permute-start | bytes 49160 | tf_op jit(solution)/shard_map/ppermute | solution.py:295
  86.9 1.6 collective-permute-start.14
  88.6 1.0 collective-permute-done.12.refs_5_
  89.6 2.2 %collective-permute-done.14.refs_7_ = f32[16,256]{1,0:T(8,128)S(1)} collective-permute-done((f32[16,256]{1,0:T(8,128)}, f32[16,256]{1,0:T(8,128)S(1)}, u32[]{:S(2)}, u32[]{:S(2)}) %collective-permute-start.14) | collective-permute-done | bytes 16416 | tf_op jit(solution)/shard_map/ppermute | solution.py:295
  91.8 0.5 copy-done.21
  92.4 4.7 %all-to-all-start = ((bf16[8,16,8,1440]{3,2,1,0:T(8,128)(2,1)}), bf16[8,16,8,1440]{3,2,1,0:T(8,128)(2,1)S(1)}, u32[]{:S(2)}, u32[]{:S(2)}) async-start(bf16[8,16,8,1440]{3,2,1,0:T(8,128)(2,1)} %get-tuple-element.64), calls=%async_computation | async-start | bytes 6291456 | tf_op jit(solution)/shard_map/all_to_all | solution.py:318
  97.7 0.5 iota_xor_fusion.place_ref
  98.2 1.8 shard_map.116
  100.1 2.4 %collective-permute-start.15 = (f32[136,128]{1,0:T(8,128)}, f32[136,128]{1,0:T(8,128)S(1)}, u32[]{:S(2)}, u32[]{:S(2)}) collective-permute-start(f32[136,128]{1,0:T(8,128)} %shard_map.116), channel_id=1, source_target_pairs={{0,1},{1,0},{2,3},{3,2},{4,5},{5,4},{6,7},{7,6},{8,9},{9,8},{10,11... | collective-permute-start | bytes 208904 | tf_op jit(solution)/shard_map/ppermute | solution.py:295
  102.4 6.6 %collective-permute-start.16 = (f32[136,128]{1,0:T(8,128)}, f32[136,128]{1,0:T(8,128)S(1)}, u32[]{:S(2)}, u32[]{:S(2)}) collective-permute-start(f32[136,128]{1,0:T(8,128)} %shard_map.116), channel_id=1, source_target_pairs={{0,2},{1,3},{2,0},{3,1},{4,6},{5,7},{6,4},{7,5},{8,10},{9,11},{10,... | collective-permute-start | bytes 208904 | tf_op jit(solution)/shard_map/ppermute | solution.py:295
  109.0 3.7 %collective-permute-done.16 = f32[136,128]{1,0:T(8,128)S(1)} collective-permute-done((f32[136,128]{1,0:T(8,128)}, f32[136,128]{1,0:T(8,128)S(1)}, u32[]{:S(2)}, u32[]{:S(2)}) %collective-permute-start.16) | collective-permute-done | bytes 69664 | tf_op jit(solution)/shard_map/ppermute | solution.py:295
  112.7 1.5 collective-permute-done.17
  114.2 0.9 add_add_fusion.a_ref
  115.1 1.4 collective-permute-start.18
  116.5 3.0 %collective-permute-start.19 = (f32[136,128]{1,0:T(8,128)S(1)}, f32[136,128]{1,0:T(8,128)S(1)}, u32[]{:S(2)}, u32[]{:S(2)}) collective-permute-start(f32[136,128]{1,0:T(8,128)S(1)} %add_add_fusion.a_ref), channel_id=1, source_target_pairs={{0,8},{1,9},{2,10},{3,11},{4,12},{5,13},{6,14},{7,15},{8,0},{9,1},... | collective-permute-start | bytes 208904 | tf_op jit(solution)/shard_map/ppermute | solution.py:295
  119.5 2.6 %collective-permute-done.19.c_ref = f32[136,128]{1,0:T(8,128)S(1)} collective-permute-done((f32[136,128]{1,0:T(8,128)S(1)}, f32[136,128]{1,0:T(8,128)S(1)}, u32[]{:S(2)}, u32[]{:S(2)}) %collective-permute-start.19) | collective-permute-done | bytes 69664 | tf_op jit(solution)/shard_map/ppermute | solution.py:295
  122.1 2.4 %collective-permute-done.20.d_ref = f32[136,128]{1,0:T(8,128)S(1)} collective-permute-done((f32[136,128]{1,0:T(8,128)S(1)}, f32[136,128]{1,0:T(8,128)S(1)}, u32[]{:S(2)}, u32[]{:S(2)}) %collective-permute-start.20) | collective-permute-done | bytes 69664 | tf_op jit(solution)/shard_map/ppermute | solution.py:295
  124.5 0.6 copy-done.16
  125.1 14.4 %shard_map.117 = (f32[128,128]{1,0:T(8,128)}, f32[1,128]{1,0:T(1,128)}, bf16[128,128]{1,0:T(8,128)(2,1)}) custom-call(f32[136,128]{1,0:T(8,128)} %copy-done.2, f32[136,128]{1,0:T(8,128)} %copy-done.14, f32[136,128]{1,0:T(8,128)} %copy-done.15, f32[136,128]{1,0:T(8,128)} %copy-done.16), custom_call_target="tpu_custom_call" | custom-call | flops 12000000000 | bytes 12000000 | tf_op jit(solution)/shard_map/pallas_call | solution.py:203
  139.5 1.7 copy-done.1
  141.2 8.1 %shard_map.118 = bf16[1024,1440]{1,0:T(8,128)(2,1)} custom-call(bf16[128,128]{1,0:T(8,128)(2,1)} %get-tuple-element.63.transform_ref, bf16[1024,1440]{1,0:T(8,128)(2,1)} %bitcast.44), custom_call_target="tpu_custom_call" | custom-call | flops 6000000000 | bytes 6000000 | tf_op jit(solution)/shard_map/pallas_call | solution.py:242
  149.3 44.4 %all_to_all.10 = bf16[8,16,8,1440]{3,2,1,0:T(8,128)(2,1)S(1)} all-to-all(bf16[8,16,8,1440]{3,2,1,0:T(8,128)(2,1)} %bitcast.46), channel_id=1, replica_groups=mesh['ens'=8,'map'=16] {'ens'}, dimensions={0} | all-to-all | bytes 5898240 | tf_op jit(solution)/shard_map/all_to_all | solution.py:318
  193.7 4.1 %copy.53 = bf16[4,2,16,8,1440]{4,0,3,1,2:T(4,128)(2,1)} copy(bf16[4,2,16,8,1440]{4,3,2,1,0:T(8,128)(2,1)S(1)} %bitcast.43) | data formatting | bytes 5898240 | tf_op jit(solution)/shard_map/reshape | solution.py:348
  (79 shorter events, 1.7 us)
Async XLA Ops:
  3.3 1.8 copy-start
  3.3 8.3 %copy-start.7 = (f32[128]{0:T(128)S(1)}, f32[128]{0:T(128)}, u32[]{:S(2)}) copy-start(f32[128]{0:T(128)} %param.11) | copy-start | bytes 1540
  3.3 8.5 %copy-start.3 = (bf16[128,16,3,3]{0,1,3,2:T(8,128)(2,1)S(1)}, bf16[128,16,3,3]{0,1,3,2:T(8,128)(2,1)}, u32[]{:S(2)}) copy-start(bf16[128,16,3,3]{0,1,3,2:T(8,128)(2,1)} %param.10) | copy-start | bytes 110596
  3.3 8.9 %copy-start.4 = (bf16[16,128,3,3]{1,0,3,2:T(8,128)(2,1)S(1)}, bf16[16,128,3,3]{1,0,3,2:T(8,128)(2,1)}, u32[]{:S(2)}) copy-start(bf16[16,128,3,3]{1,0,3,2:T(8,128)(2,1)} %param.12) | copy-start | bytes 110596
  5.1 8.1 %copy-start.5 = (s32[256]{0:T(256)S(1)}, s32[256]{0:T(256)}, u32[]{:S(2)}) copy-start(s32[256]{0:T(256)} %param.14) | copy-start | bytes 3076
  5.1 8.6 %copy-start.6 = (f32[16]{0:T(128)S(1)}, f32[16]{0:T(128)}, u32[]{:S(2)}) copy-start(f32[16]{0:T(128)} %param.13) | copy-start | bytes 196
  5.1 12.6 %collective-permute-start = (bf16[4,2,16,1440]{3,2,1,0:T(8,128)(2,1)}, bf16[4,2,16,1440]{3,2,1,0:T(8,128)(2,1)}, u32[]{:S(2)}, u32[]{:S(2)}) collective-permute-start(bf16[4,2,16,1440]{3,2,1,0:T(8,128)(2,1)} %get-tuple-element.70), channel_id=1, source_target_pairs={{0,1},{1,2},{2,3},{3,4},{4,5},{5,6},{6,7},{7,8},{8,9},{9,10},{10,1... | collective-permute-start | bytes 1105928 | tf_op jit(solution)/shard_map/ppermute | solution.py:305
  10.4 11.7 %collective-permute-start.1 = (bf16[4,2,16,1440]{3,2,1,0:T(8,128)(2,1)S(1)}, bf16[4,2,16,1440]{3,2,1,0:T(8,128)(2,1)}, u32[]{:S(2)}, u32[]{:S(2)}) collective-permute-start(bf16[4,2,16,1440]{3,2,1,0:T(8,128)(2,1)S(1)} %get-tuple-element.69), channel_id=1, source_target_pairs={{1,0},{2,1},{3,2},{4,3},{5,4},{6,5},{7,6},{8,7},{9,8},{10,9},{11,1... | collective-permute-start | bytes 1105928 | tf_op jit(solution)/shard_map/ppermute | solution.py:305
  22.0 14.6 %collective-permute-start.2 = (bf16[4,2,16,1440]{3,2,1,0:T(8,128)(2,1)S(1)}, bf16[4,2,16,1440]{3,2,1,0:T(8,128)(2,1)S(1)}, u32[]{:S(2)}, u32[]{:S(2)}) collective-permute-start(bf16[4,2,16,1440]{3,2,1,0:T(8,128)(2,1)S(1)} %get-tuple-element.35), channel_id=1, source_target_pairs={{0,1},{1,2},{2,3},{3,4},{4,5},{5,6},{6,7},{7,8},{8,9},{9,10},{10,1... | collective-permute-start | bytes 1105928 | tf_op jit(solution)/shard_map/ppermute | solution.py:305
  24.8 11.8 %collective-permute-start.3 = (bf16[4,2,16,1440]{3,2,1,0:T(8,128)(2,1)S(1)}, bf16[4,2,16,1440]{3,2,1,0:T(8,128)(2,1)S(1)}, u32[]{:S(2)}, u32[]{:S(2)}) collective-permute-start(bf16[4,2,16,1440]{3,2,1,0:T(8,128)(2,1)S(1)} %get-tuple-element.36), channel_id=1, source_target_pairs={{1,0},{2,1},{3,2},{4,3},{5,4},{6,5},{7,6},{8,7},{9,8},{10,9},{11,1... | collective-permute-start | bytes 1105928 | tf_op jit(solution)/shard_map/ppermute | solution.py:305
  36.6 5.4 %copy-start.8 = (bf16[4,2,16,1440]{3,2,1,0:T(8,128)(2,1)}, bf16[4,2,16,1440]{3,2,1,0:T(8,128)(2,1)S(1)}, u32[]{:S(2)}) copy-start(bf16[4,2,16,1440]{3,2,1,0:T(8,128)(2,1)S(1)} %collective-permute-done.2.top_ref) | copy-start | bytes 1105924
  36.6 5.3 %copy-start.10 = (bf16[4,2,16,1440]{3,2,1,0:T(8,128)(2,1)}, bf16[4,2,16,1440]{3,2,1,0:T(8,128)(2,1)S(1)}, u32[]{:S(2)}) copy-start(bf16[4,2,16,1440]{3,2,1,0:T(8,128)(2,1)S(1)} %collective-permute-done.3.bottom_ref) | copy-start | bytes 1105924
  36.6 15.2 %collective-permute-start.4 = (bf16[4,2,16,1440]{3,2,1,0:T(8,128)(2,1)S(1)}, bf16[4,2,16,1440]{3,2,1,0:T(8,128)(2,1)S(1)}, u32[]{:S(2)}, u32[]{:S(2)}) collective-permute-start(bf16[4,2,16,1440]{3,2,1,0:T(8,128)(2,1)S(1)} %get-tuple-element.37), channel_id=1, source_target_pairs={{0,1},{1,2},{2,3},{3,4},{4,5},{5,6},{6,7},{7,8},{8,9},{9,10},{10,1... | collective-permute-start | bytes 1105928 | tf_op jit(solution)/shard_map/ppermute | solution.py:305
  40.7 11.2 %collective-permute-start.5 = (bf16[4,2,16,1440]{3,2,1,0:T(8,128)(2,1)S(1)}, bf16[4,2,16,1440]{3,2,1,0:T(8,128)(2,1)S(1)}, u32[]{:S(2)}, u32[]{:S(2)}) collective-permute-start(bf16[4,2,16,1440]{3,2,1,0:T(8,128)(2,1)S(1)} %get-tuple-element.38), channel_id=1, source_target_pairs={{1,0},{2,1},{3,2},{4,3},{5,4},{6,5},{7,6},{8,7},{9,8},{10,9},{11,1... | collective-permute-start | bytes 1105928 | tf_op jit(solution)/shard_map/ppermute | solution.py:305
  51.9 6.0 %copy-start.9 = (bf16[4,2,16,1440]{3,2,1,0:T(8,128)(2,1)}, bf16[4,2,16,1440]{3,2,1,0:T(8,128)(2,1)S(1)}, u32[]{:S(2)}) copy-start(bf16[4,2,16,1440]{3,2,1,0:T(8,128)(2,1)S(1)} %collective-permute-done.4.top_ref) | copy-start | bytes 1105924
  51.9 5.9 %copy-start.12 = (bf16[4,2,16,1440]{3,2,1,0:T(8,128)(2,1)}, bf16[4,2,16,1440]{3,2,1,0:T(8,128)(2,1)S(1)}, u32[]{:S(2)}) copy-start(bf16[4,2,16,1440]{3,2,1,0:T(8,128)(2,1)S(1)} %collective-permute-done.5.bottom_ref) | copy-start | bytes 1105924
  51.9 15.8 %collective-permute-start.6 = (bf16[4,2,16,1440]{3,2,1,0:T(8,128)(2,1)S(1)}, bf16[4,2,16,1440]{3,2,1,0:T(8,128)(2,1)S(1)}, u32[]{:S(2)}, u32[]{:S(2)}) collective-permute-start(bf16[4,2,16,1440]{3,2,1,0:T(8,128)(2,1)S(1)} %get-tuple-element.39), channel_id=1, source_target_pairs={{0,1},{1,2},{2,3},{3,4},{4,5},{5,6},{6,7},{7,8},{8,9},{9,10},{10,1... | collective-permute-start | bytes 1105928 | tf_op jit(solution)/shard_map/ppermute | solution.py:305
  56.5 11.2 %collective-permute-start.7 = (bf16[4,2,16,1440]{3,2,1,0:T(8,128)(2,1)S(1)}, bf16[4,2,16,1440]{3,2,1,0:T(8,128)(2,1)S(1)}, u32[]{:S(2)}, u32[]{:S(2)}) collective-permute-start(bf16[4,2,16,1440]{3,2,1,0:T(8,128)(2,1)S(1)} %get-tuple-element.40), channel_id=1, source_target_pairs={{1,0},{2,1},{3,2},{4,3},{5,4},{6,5},{7,6},{8,7},{9,8},{10,9},{11,1... | collective-permute-start | bytes 1105928 | tf_op jit(solution)/shard_map/ppermute | solution.py:305
  67.7 0.8 copy-start.11
  67.8 0.9 copy-start.13
  78.5 10.0 %collective-permute-start.10 = (f32[16,256]{1,0:T(8,128)}, f32[16,256]{1,0:T(8,128)S(1)}, u32[]{:S(2)}, u32[]{:S(2)}) collective-permute-start(f32[16,256]{1,0:T(8,128)} %get-tuple-element.55.refs_0_), channel_id=1, source_target_pairs={{0,48},{16,32},{32,16},{48,0},{64,112},{80,96},{96,80},{112,64},{1... | collective-permute-start | bytes 49160 | tf_op jit(solution)/shard_map/ppermute | solution.py:295
  82.2 6.2 %collective-permute-start.11 = (f32[16,256]{1,0:T(8,128)}, f32[16,256]{1,0:T(8,128)S(1)}, u32[]{:S(2)}, u32[]{:S(2)}) collective-permute-start(f32[16,256]{1,0:T(8,128)} %get-tuple-element.55.refs_0_), channel_id=1, source_target_pairs={{0,64},{16,80},{32,96},{48,112},{64,0},{80,16},{96,32},{112,48},{1... | collective-permute-start | bytes 49160 | tf_op jit(solution)/shard_map/ppermute | solution.py:295
  84.7 4.9 %collective-permute-start.12 = (f32[16,256]{1,0:T(8,128)}, f32[16,256]{1,0:T(8,128)S(1)}, u32[]{:S(2)}, u32[]{:S(2)}) collective-permute-start(f32[16,256]{1,0:T(8,128)} %get-tuple-element.55.refs_0_), channel_id=1, source_target_pairs={{0,80},{16,64},{32,112},{48,96},{64,16},{80,0},{96,48},{112,32},{1... | collective-permute-start | bytes 49160 | tf_op jit(solution)/shard_map/ppermute | solution.py:295
  84.7 4.9 %collective-permute-start.13 = (f32[16,256]{1,0:T(8,128)}, f32[16,256]{1,0:T(8,128)S(1)}, u32[]{:S(2)}, u32[]{:S(2)}) collective-permute-start(f32[16,256]{1,0:T(8,128)} %get-tuple-element.55.refs_0_), channel_id=1, source_target_pairs={{0,96},{16,112},{32,64},{48,80},{64,32},{80,48},{96,0},{112,16},{1... | collective-permute-start | bytes 49160 | tf_op jit(solution)/shard_map/ppermute | solution.py:295
  86.9 4.9 %collective-permute-start.14 = (f32[16,256]{1,0:T(8,128)}, f32[16,256]{1,0:T(8,128)S(1)}, u32[]{:S(2)}, u32[]{:S(2)}) collective-permute-start(f32[16,256]{1,0:T(8,128)} %get-tuple-element.55.refs_0_), channel_id=1, source_target_pairs={{0,112},{16,96},{32,80},{48,64},{64,48},{80,32},{96,16},{112,0},{1... | collective-permute-start | bytes 49160 | tf_op jit(solution)/shard_map/ppermute | solution.py:295
  88.5 3.3 %copy-start.17 = (f32[16,256]{1,0:T(8,128)}, f32[16,256]{1,0:T(8,128)S(1)}, u32[]{:S(2)}) copy-start(f32[16,256]{1,0:T(8,128)S(1)} %collective-permute-done.10.refs_3_) | copy-start | bytes 49156
  88.5 3.3 %collective-permute-start.8 = (f32[16,256]{1,0:T(8,128)}, f32[16,256]{1,0:T(8,128)S(1)}, u32[]{:S(2)}, u32[]{:S(2)}) collective-permute-start(f32[16,256]{1,0:T(8,128)} %get-tuple-element.55.refs_0_), channel_id=1, source_target_pairs={{0,16},{16,0},{32,48},{48,32},{64,80},{80,64},{96,112},{112,96},{1... | collective-permute-start | bytes 49160 | tf_op jit(solution)/shard_map/ppermute | solution.py:295
  88.5 3.3 %copy-start.18 = (f32[16,256]{1,0:T(8,128)}, f32[16,256]{1,0:T(8,128)S(1)}, u32[]{:S(2)}) copy-start(f32[16,256]{1,0:T(8,128)S(1)} %collective-permute-done.11.refs_4_) | copy-start | bytes 49156
  88.5 3.3 %collective-permute-start.9 = (f32[16,256]{1,0:T(8,128)}, f32[16,256]{1,0:T(8,128)S(1)}, u32[]{:S(2)}, u32[]{:S(2)}) collective-permute-start(f32[16,256]{1,0:T(8,128)} %get-tuple-element.55.refs_0_), channel_id=1, source_target_pairs={{0,32},{16,48},{32,0},{48,16},{64,96},{80,112},{96,64},{112,80},{1... | collective-permute-start | bytes 49160 | tf_op jit(solution)/shard_map/ppermute | solution.py:295
  89.6 2.2 %copy-start.19 = (f32[16,256]{1,0:T(8,128)}, f32[16,256]{1,0:T(8,128)S(1)}, u32[]{:S(2)}) copy-start(f32[16,256]{1,0:T(8,128)S(1)} %collective-permute-done.12.refs_5_) | copy-start | bytes 49156
  89.6 2.2 %copy-start.20 = (f32[16,256]{1,0:T(8,128)}, f32[16,256]{1,0:T(8,128)S(1)}, u32[]{:S(2)}) copy-start(f32[16,256]{1,0:T(8,128)S(1)} %collective-permute-done.13.refs_6_) | copy-start | bytes 49156
  91.7 0.6 copy-start.21
  91.8 0.6 copy-start.22
  91.8 0.6 copy-start.23
  92.4 47.1 %all-to-all-start = ((bf16[8,16,8,1440]{3,2,1,0:T(8,128)(2,1)}), bf16[8,16,8,1440]{3,2,1,0:T(8,128)(2,1)S(1)}, u32[]{:S(2)}, u32[]{:S(2)}) async-start(bf16[8,16,8,1440]{3,2,1,0:T(8,128)(2,1)} %get-tuple-element.64), calls=%async_computation | async-start | bytes 6291456 | tf_op jit(solution)/shard_map/all_to_all | solution.py:318
  100.1 8.9 %collective-permute-start.15 = (f32[136,128]{1,0:T(8,128)}, f32[136,128]{1,0:T(8,128)S(1)}, u32[]{:S(2)}, u32[]{:S(2)}) collective-permute-start(f32[136,128]{1,0:T(8,128)} %shard_map.116), channel_id=1, source_target_pairs={{0,1},{1,0},{2,3},{3,2},{4,5},{5,4},{6,7},{7,6},{8,9},{9,8},{10,11... | collective-permute-start | bytes 208904 | tf_op jit(solution)/shard_map/ppermute | solution.py:295
  102.4 10.3 %collective-permute-start.16 = (f32[136,128]{1,0:T(8,128)}, f32[136,128]{1,0:T(8,128)S(1)}, u32[]{:S(2)}, u32[]{:S(2)}) collective-permute-start(f32[136,128]{1,0:T(8,128)} %shard_map.116), channel_id=1, source_target_pairs={{0,2},{1,3},{2,0},{3,1},{4,6},{5,7},{6,4},{7,5},{8,10},{9,11},{10,... | collective-permute-start | bytes 208904 | tf_op jit(solution)/shard_map/ppermute | solution.py:295
  109.0 5.2 %collective-permute-start.17 = (f32[136,128]{1,0:T(8,128)}, f32[136,128]{1,0:T(8,128)S(1)}, u32[]{:S(2)}, u32[]{:S(2)}) collective-permute-start(f32[136,128]{1,0:T(8,128)} %shard_map.116), channel_id=1, source_target_pairs={{0,3},{1,2},{2,1},{3,0},{4,7},{5,6},{6,5},{7,4},{8,11},{9,10},{10,... | collective-permute-start | bytes 208904 | tf_op jit(solution)/shard_map/ppermute | solution.py:295
  115.1 9.4 %copy-start.2 = (f32[136,128]{1,0:T(8,128)}, f32[136,128]{1,0:T(8,128)S(1)}, u32[]{:S(2)}) copy-start(f32[136,128]{1,0:T(8,128)S(1)} %add_add_fusion.a_ref) | copy-start | bytes 208900
  115.1 4.4 %collective-permute-start.18 = (f32[136,128]{1,0:T(8,128)S(1)}, f32[136,128]{1,0:T(8,128)S(1)}, u32[]{:S(2)}, u32[]{:S(2)}) collective-permute-start(f32[136,128]{1,0:T(8,128)S(1)} %add_add_fusion.a_ref), channel_id=1, source_target_pairs={{0,4},{1,5},{2,6},{3,7},{4,0},{5,1},{6,2},{7,3},{8,12},{9,13},{10,... | collective-permute-start | bytes 208904 | tf_op jit(solution)/shard_map/ppermute | solution.py:295
  116.5 5.6 %collective-permute-start.19 = (f32[136,128]{1,0:T(8,128)S(1)}, f32[136,128]{1,0:T(8,128)S(1)}, u32[]{:S(2)}, u32[]{:S(2)}) collective-permute-start(f32[136,128]{1,0:T(8,128)S(1)} %add_add_fusion.a_ref), channel_id=1, source_target_pairs={{0,8},{1,9},{2,10},{3,11},{4,12},{5,13},{6,14},{7,15},{8,0},{9,1},... | collective-permute-start | bytes 208904 | tf_op jit(solution)/shard_map/ppermute | solution.py:295
  119.5 5.0 %collective-permute-start.20 = (f32[136,128]{1,0:T(8,128)S(1)}, f32[136,128]{1,0:T(8,128)S(1)}, u32[]{:S(2)}, u32[]{:S(2)}) collective-permute-start(f32[136,128]{1,0:T(8,128)S(1)} %add_add_fusion.a_ref), channel_id=1, source_target_pairs={{0,12},{1,13},{2,14},{3,15},{4,8},{5,9},{6,10},{7,11},{8,4},{9,5},... | collective-permute-start | bytes 208904 | tf_op jit(solution)/shard_map/ppermute | solution.py:295
  119.5 5.0 %copy-start.14 = (f32[136,128]{1,0:T(8,128)}, f32[136,128]{1,0:T(8,128)S(1)}, u32[]{:S(2)}) copy-start(f32[136,128]{1,0:T(8,128)S(1)} %collective-permute-done.18.b_ref) | copy-start | bytes 208900
  122.1 2.4 %copy-start.15 = (f32[136,128]{1,0:T(8,128)}, f32[136,128]{1,0:T(8,128)S(1)}, u32[]{:S(2)}) copy-start(f32[136,128]{1,0:T(8,128)S(1)} %collective-permute-done.19.c_ref) | copy-start | bytes 208900
  124.5 0.6 copy-start.16
  139.5 1.7 copy-start.1

commit v3 on v2

--- a/solution.py
+++ b/solution.py
@@ -16,7 +16,7 @@
 SLOTS = 256
 GROUP = 16
 PLANES = ROWS * FIELDS
-CHUNKS = 4
+CHUNKS = 2
 N_ENS = 8
 MEMBERS = 128
 VMEM_LIMIT = 56 * 1024 * 1024
@@ -28,18 +28,16 @@
     bottom_ref,
     first_top_ref,
     first_bottom_ref,
-    second_ref,
+    second_low_ref,
+    second_middle_ref,
+    second_high_ref,
     bias_ref,
     column_ref,
     plane_ref,
-    earlier_ref,
-    held_ref,
     fields_ref,
     observed_ref,
-    *,
-    start,
+    held_ref,
 ):
-    del held_ref
     member = pl.program_id(0)
     main = x_ref[0].reshape(PLANES, LON)
     stack = jnp.concatenate(
@@ -60,25 +58,39 @@
     hidden = jnp.concatenate(
         [hidden_rows(0, first_top_ref), hidden_rows(3 * FIELDS, first_bottom_ref)], axis=0
     )
-    outer = jnp.dot(second_ref[...], hidden, preferred_element_type=jnp.float32)
-    change = (
-        pltpu.roll(outer[:PLANES], 1, 1)
-        + outer[PLANES : 2 * PLANES]
-        + pltpu.roll(outer[2 * PLANES :], RING - 1, 1)
+
+    def outer(weights_ref, pair):
+        rows = hidden[2 * HID * pair : 2 * HID * (pair + 1)]
+        return jnp.dot(weights_ref[...], rows, preferred_element_type=jnp.float32)
+
+    both = outer(second_middle_ref, 1)
+    half = 3 * PLANES // 2
+    pairs = [both[:half] + outer(second_low_ref, 0), both[half:] + outer(second_high_ref, 2)]
+    shift = lambda tap, by: pltpu.roll(tap, by, 1)
+    part = PLANES // 2
+    change = jnp.concatenate(
+        [
+            shift(p[:part], 1) + p[part : 2 * part] + shift(p[2 * part :], RING - 1)
+            for p in pairs
+        ],
+        axis=0,
     )
     base = ring[2 * FIELDS : 2 * FIELDS + PLANES].astype(jnp.float32) + bias_ref[...]
     own = (base + change).astype(jnp.bfloat16)
     fields_ref[:, 0] = own[:, :LON].reshape(N_ENS, 8, LON)
-    picked = jnp.dot(own, column_ref[...], preferred_element_type=jnp.float32)
-    here = lax.broadcasted_iota(jnp.int32, (PLANES, SLOTS), 0) == plane_ref[...]
-
-    @pl.when(member == 0)
+    held_ref[pl.ds(pl.multiple_of(member * PLANES, PLANES), PLANES), :] = own
+
+    count = observed_ref.shape[0]
+
+    @pl.when(member == count - 1)
     def _():
-        observed_ref[...] = earlier_ref[...]
-
-    observed_ref[pl.ds(start + member, 1), :] = jnp.sum(
-        jnp.where(here, picked, 0.0), axis=0, keepdims=True
-    )
+        picked = jnp.dot(held_ref[...], column_ref[...], preferred_element_type=jnp.float32)
+        here = lax.broadcasted_iota(jnp.int32, (PLANES, SLOTS), 0) == plane_ref[...]
+        for m in range(count):
+            mine = picked[m * PLANES : (m + 1) * PLANES]
+            observed_ref[m : m + 1, :] = jnp.sum(
+                jnp.where(here, mine, 0.0), axis=0, keepdims=True
+            )
 
 
 def cost(microseconds):
@@ -87,37 +99,30 @@
     )
 
 
-def forecast(start, own, top, bottom, *shared, fields):
+def forecast(start, own, top, bottom, *shared):
     count = top.shape[0]
     whole = lambda array: pl.BlockSpec(array.shape, lambda m: (0,) * array.ndim)
-    in_specs = [
-        pl.BlockSpec((1, ROWS, FIELDS, LON), lambda m: (start + m, 0, 0, 0)),
-        pl.BlockSpec((1, 2, FIELDS, LON), lambda m: (m, 0, 0, 0)),
-        pl.BlockSpec((1, 2, FIELDS, LON), lambda m: (m, 0, 0, 0)),
-    ]
-    in_specs += [whole(array) for array in shared] + [pl.BlockSpec(memory_space=pl.ANY)]
-    arrays = [own, top, bottom, *shared, fields]
-    kernel = functools.partial(forecast_kernel, start=start)
-    aliases = {len(arrays) - 1: 0}
-    if fields is None:
-        arrays, in_specs, aliases = arrays[:-1], in_specs[:-1], {}
-        kernel = lambda *refs: forecast_kernel(*refs[:-2], None, *refs[-2:], start=start)
     return pl.pallas_call(
-        kernel,
+        forecast_kernel,
         grid=(count,),
-        in_specs=in_specs,
+        in_specs=[
+            pl.BlockSpec((1, ROWS, FIELDS, LON), lambda m: (start + m, 0, 0, 0)),
+            pl.BlockSpec((1, 2, FIELDS, LON), lambda m: (m, 0, 0, 0)),
+            pl.BlockSpec((1, 2, FIELDS, LON), lambda m: (m, 0, 0, 0)),
+        ]
+        + [whole(array) for array in shared],
         out_specs=[
-            pl.BlockSpec((N_ENS, 1, 8, LON), lambda m: (0, start + m, 0, 0)),
-            pl.BlockSpec((GROUP, SLOTS), lambda m: (0, 0)),
+            pl.BlockSpec((N_ENS, 1, 8, LON), lambda m: (0, m, 0, 0)),
+            pl.BlockSpec((count, SLOTS), lambda m: (0, 0)),
         ],
         out_shape=[
-            jax.ShapeDtypeStruct((N_ENS, GROUP, 8, LON), jnp.bfloat16),
-            jax.ShapeDtypeStruct((GROUP, SLOTS), jnp.float32),
+            jax.ShapeDtypeStruct((N_ENS, count, 8, LON), jnp.bfloat16),
+            jax.ShapeDtypeStruct((count, SLOTS), jnp.float32),
         ],
-        input_output_aliases=aliases,
-        cost_estimate=cost(10),
+        scratch_shapes=[pltpu.VMEM((count * PLANES, RING), jnp.bfloat16)],
+        cost_estimate=cost(2 * count),
         compiler_params=pltpu.CompilerParams(vmem_limit_bytes=VMEM_LIMIT),
-    )(*arrays)
+    )(own, top, bottom, *shared)
 
 
 def products_kernel(place_ref, count_ref, value_ref, sigma_ref, *refs):
@@ -162,30 +167,39 @@
     column = lax.broadcasted_iota(jnp.int32, (n, n), 1)
     eye = (row == column).astype(jnp.float32)
     gram = total[0:n] + eye
-    blocks = [
-        [gram[b : b + 8], eye[b : b + 8]] for b in range(0, n, 8)
-    ]
+    blocks = [[gram[b : b + 8], eye[b : b + 8]] for b in range(0, n, 8)]
     within = lax.broadcasted_iota(jnp.int32, (8, n), 0)
+    wide = lambda value: jnp.broadcast_to(value, (8, n))
     for b in range(n // 8):
         upper, inverse = blocks[b]
+        columns = [wide(upper[:, 8 * b + k : 8 * b + k + 1]) for k in range(8)]
+        scales, steps, rows = [], [], []
         for k in range(8):
-            j = 8 * b + k
-            scale = lax.rsqrt(upper[k : k + 1, j : j + 1])
-            share = upper[:, j : j + 1] * scale
-            upper_row = upper[k : k + 1] * scale
-            inverse_row = inverse[k : k + 1] * scale
+            scale = lax.rsqrt(wide(columns[k][k : k + 1]))
+            share = columns[k] * scale
+            step = {}
+            for later in range(k + 1, 8):
+                step[later] = wide(share[later : later + 1])
+                columns[later] = columns[later] - share * step[later]
+            upper_row = wide(upper[k : k + 1]) * scale
+            inverse_row = wide(inverse[k : k + 1]) * scale
             share = jnp.where(within > k, share, 0.0)
             upper = jnp.where(within == k, upper_row, upper - share * upper_row)
             inverse = jnp.where(within == k, inverse_row, inverse - share * inverse_row)
-        blocks[b] = [upper, inverse]
-        turned = upper.T
+            scales.append(scale)
+            steps.append(step)
+            rows.append((upper_row, inverse_row))
         for t in range(b + 1, n // 8):
             later_upper, later_inverse = blocks[t]
+            columns = [wide(later_upper[:, 8 * b + k : 8 * b + k + 1]) for k in range(8)]
             for k in range(8):
-                share = turned[8 * t : 8 * t + 8, k : k + 1]
-                later_upper = later_upper - share * upper[k : k + 1]
-                later_inverse = later_inverse - share * inverse[k : k + 1]
+                share = columns[k] * scales[k]
+                for later in range(k + 1, 8):
+                    columns[later] = columns[later] - share * steps[k][later]
+                later_upper = later_upper - share * rows[k][0]
+                later_inverse = later_inverse - share * rows[k][1]
             blocks[t] = [later_upper, later_inverse]
+        blocks[b] = [upper, inverse]
     upper = jnp.concatenate([pair[0] for pair in blocks], axis=0)
     inverse = jnp.concatenate([pair[1] for pair in blocks], axis=0)
     factor_ref[...] = jnp.where(row <= column, upper, 0.0).T
@@ -213,18 +227,22 @@
     )(*parts)
 
 
-def update_kernel(transform_ref, fields_ref, out_ref, spread_ref):
+def update_kernel(transform_ref, early_ref, late_ref, out_ref, spread_ref):
     rows = MEMBERS * 8
+    half = rows // 2
 
     @pl.when(pl.program_id(0) == 0)
     def _():
-        member = lax.broadcasted_iota(jnp.int32, (rows, MEMBERS), 0) // 8
-        column = lax.broadcasted_iota(jnp.int32, (rows, MEMBERS), 1)
-        repeat = (member == column).astype(jnp.bfloat16)
+        shape = (rows, MEMBERS)
+        row = lax.broadcasted_iota(jnp.int32, shape, 0)
+        column = lax.broadcasted_iota(jnp.int32, shape, 1)
+        held = row % half // 64 * GROUP + row // half * 8 + row % 64 // 8
+        repeat = (row // 8 == column).astype(jnp.bfloat16)
+        placed = (held == column).astype(jnp.bfloat16)
         tall = jnp.dot(repeat, transform_ref[...], preferred_element_type=jnp.float32)
         wide = lax.dot_general(
             tall.astype(jnp.bfloat16),
-            repeat,
+            placed,
             (((1,), (1,)), ((), ())),
             preferred_element_type=jnp.float32,
         )
@@ -232,23 +250,25 @@
         same = plane == lax.broadcasted_iota(jnp.int32, (rows, rows), 1) % 8
         spread_ref[...] = jnp.where(same, wide, 0.0).astype(jnp.bfloat16)
 
-    mixed = jnp.dot(spread_ref[...], fields_ref[...], preferred_element_type=jnp.float32)
+    fields = jnp.concatenate([early_ref[...], late_ref[...]], axis=0)
+    mixed = jnp.dot(spread_ref[...], fields, preferred_element_type=jnp.float32)
     out_ref[...] = mixed.astype(jnp.bfloat16)
 
 
-def update(transform, fields):
+def update(transform, early, late):
     rows = MEMBERS * 8
-    block = pl.BlockSpec((rows, 256), lambda k: (0, k))
-    return pl.pallas_call(
+    half = pl.BlockSpec((rows // 2, 256), lambda k: (0, k))
+    mixed = pl.pallas_call(
         update_kernel,
         grid=(RING // 256,),
-        in_specs=[pl.BlockSpec((MEMBERS, MEMBERS), lambda k: (0, 0)), block],
-        out_specs=block,
+        in_specs=[pl.BlockSpec((MEMBERS, MEMBERS), lambda k: (0, 0)), half, half],
+        out_specs=pl.BlockSpec((rows, 256), lambda k: (0, k)),
         out_shape=jax.ShapeDtypeStruct((rows, LON), jnp.bfloat16),
         scratch_shapes=[pltpu.VMEM((rows, rows), jnp.bfloat16)],
         cost_estimate=cost(6),
         compiler_params=pltpu.CompilerParams(vmem_limit_bytes=VMEM_LIMIT),
-    )(transform, fields.reshape(rows, LON)).reshape(fields.shape)
+    )(transform, early.reshape(rows // 2, LON), late.reshape(rows // 2, LON))
+    return mixed.reshape(N_ENS, GROUP, 8, LON)
 
 
 def first_weights(conv_in, bias_in, mask):
@@ -270,7 +290,12 @@
 def second_weights(conv_out):
     by_tap = jnp.transpose(conv_out, (3, 0, 2, 1))
     placed = [jnp.pad(by_tap, ((0, 0), (0, 0), (r, 3 - r), (0, 0))) for r in range(ROWS)]
-    return jnp.stack(placed, axis=1).reshape(3 * ROWS * FIELDS, 6 * HID)
+    whole = jnp.stack(placed, axis=1).reshape(3, 2, 2 * FIELDS, 6 * HID)
+    low = whole[:, 0].reshape(6 * FIELDS, 6 * HID)
+    high = whole[:, 1].reshape(6 * FIELDS, 6 * HID)
+    pair = 2 * HID
+    middle = jnp.concatenate([low[:, pair : 2 * pair], high[:, pair : 2 * pair]], axis=0)
+    return low[:, :pair], middle, high[:, 2 * pair :]
 
 
 def on_device(
@@ -308,7 +333,7 @@
     inner_bottom = (tile < tiles - 1).astype(jnp.float32)
     first_top = first_weights(conv_in, bias_in, [inner_top, one, one])
     first_bottom = first_weights(conv_in, bias_in, [one, one, inner_bottom])
-    second = second_weights(conv_out)
+    second_low, second_middle, second_high = second_weights(conv_out)
     bias = jnp.tile(bias_out, ROWS).reshape(PLANES, 1)
     plane = observed_entry_index // LON
     column = observed_entry_index - plane * LON
@@ -318,33 +343,37 @@
     exchange = lambda value: lax.all_to_all(
         value, "ens", split_axis=0, concat_axis=0, tiled=True
     )
-    fields, observed = None, jnp.zeros((GROUP, SLOTS), jnp.float32)
+    fields, observed = [], []
     for chunk, (top, bottom) in enumerate(halos):
-        fields, observed = forecast(
+        moved, seen = forecast(
             chunk * share,
             own,
             top,
             bottom,
             first_top,
             first_bottom,
-            second,
+            second_low,
+            second_middle,
+            second_high,
             bias,
             picks,
             plane,
-            observed,
-            fields=fields,
         )
+        fields.append(moved)
+        observed.append(seen)
+    early = exchange(fields[0])
+    observed = jnp.concatenate(observed, axis=0)
     pieces = [observed] + [swap(observed, "ens", step) for step in range(1, N_ENS)]
     places = jnp.bitwise_xor(own_place, jnp.arange(N_ENS, dtype=jnp.int32))
-    pieces, fields = lax.optimization_barrier((pieces, fields))
-    gathered = exchange(fields)
+    pieces, late = lax.optimization_barrier((pieces, fields[1]))
+    late = exchange(late)
     part = products(pieces, places, obs_count, obs_value, obs_sigma)
     near = [part] + [swap(part, "map", step) for step in (1, 2, 3)]
     row = (near[0] + near[1]) + (near[2] + near[3])
     factor, mean_weights, transform = transform_of(
         [row] + [swap(row, "map", step) for step in (4, 8, 12)]
     )
-    back = exchange(update(transform, gathered))
+    back = exchange(update(transform, early, late))
     back = back.reshape(ROWS, 2, GROUP, 8, LON)
     analysis = jnp.transpose(back, (2, 1, 3, 0, 4)).reshape(GROUP, FIELDS, ROWS, LON)
     return (analysis, factor, mean_weights.reshape(MEMBERS))

time: 199 us -> 177 us (0.89)
  Pallas kernels: 63.8 us -> 46 us
  starting transfers between devices: 50 us -> 42.5 us
  waiting for transfers between devices: 18.7 us -> 24.3 us
  blocking collectives: 44.4 us -> 42.3 us
    pallas_call x4 -> x2, Pallas kernels: 39.5 us -> 30.4 us  [forecast(): pl.pallas_call(forecast_kernel, grid=(count,), in_specs=[pl.BlockSpec((1,...]
    pallas_call x1, Pallas kernels: 14.4 us -> 5.66 us  [transform_of(): pl.pallas_call(transform_kernel, in_specs=[vmem] * 4, out_specs=[vmem, vm...]
    ppermute x4 -> x2, waiting for transfers between devices: 1.04 us -> 9.13 us  [on_device(): lax.ppermute(edges[0], 'map', down)]
    ppermute x4 -> x2, starting transfers between devices: 16.7 us -> 8.67 us  [on_device(): lax.ppermute(edges[0], 'map', down)]
    all_to_all x1 -> x2, starting transfers between devices: 4.72 us -> 12.1 us  [on_device(): lax.all_to_all(value, 'ens', split_axis=0, concat_axis=0, tiled=True)]
    ppermute x13, waiting for transfers between devices: 13.3 us -> 7.02 us  [swap(): return lax.ppermute(value, axis, pairs)]
    ppermute x13, starting transfers between devices: 23.4 us -> 19.2 us  [swap(): return lax.ppermute(value, axis, pairs)]
    all_to_all x1 -> x2, waiting for transfers between devices: 0.01 us -> 3.96 us  [on_device(): lax.all_to_all(value, 'ens', split_axis=0, concat_axis=0, tiled=True)]
  transfers between devices with their start and end apart: 22 -> 19, of which waited for: 8 -> 7; matrix products, arithmetic and copies ran while one was open for 3% -> 4% of each run, Pallas kernels for 23% -> 22%
where the time goes in v3:
time: 177 us; the launch traced here: 175 us
  Pallas kernels  46 us (26%)
  starting transfers between devices  42.5 us (24%)
  blocking collectives  42.3 us (24%)
  waiting for transfers between devices  24.3 us (14%)
  local copies, waits for them, and re-layouts  14.3 us (8%)
  other arithmetic  4.09 us (2%)
    all_to_all x1, blocking collectives, on_device(): lax.all_to_all(value, 'ens', split_axis=0, concat_axis=0, tiled=True)  42.3 us
    pallas_call x2, Pallas kernels, forecast(): pl.pallas_call(forecast_kernel, grid=(count,), in_specs=[pl.BlockSpec((1,...  30.4 us
    ppermute x13, starting transfers between devices, swap(): return lax.ppermute(value, axis, pairs)  19.2 us
    all_to_all x2, starting transfers between devices, on_device(): lax.all_to_all(value, 'ens', split_axis=0, concat_axis=0, tiled=True)  12.1 us
    ppermute x2, waiting for transfers between devices, on_device(): lax.ppermute(edges[0], 'map', down)  9.13 us
    ppermute x2, starting transfers between devices, on_device(): lax.ppermute(edges[0], 'map', down)  8.67 us
    pallas_call x1, Pallas kernels, update(): pl.pallas_call(update_kernel, grid=(RING // 256,), in_specs=[pl.BlockSpec...  8.09 us
    ppermute x13, waiting for transfers between devices, swap(): return lax.ppermute(value, axis, pairs)  7.02 us
  transfers between devices with their start and end apart: 19, of which 7 were waited for; matrix products, arithmetic and copies ran while one was open for 4% of the time, Pallas kernels for 22%

profile of v3, /device:TPU:1, one launch (start us, length us, event | category | flops | bytes accessed | tf_op | source)
XLA Modules:
  0.0 175.1 jit_solution(12982598619710876800)
XLA Ops:
  0.6 2.7 %copy.46 = bf16[16,16,4,1440]{3,1,2,0:T(8,128)(2,1)S(1)} copy(bf16[16,16,4,1440]{3,2,1,0:T(4,128)(2,1)} %param.9) | data formatting | bytes 5898240 | tf_op args[0]
  3.3 1.7 fusion.11
  5.1 0.4 copy-done
  5.5 4.5 %collective-permute-start = (bf16[8,2,16,1440]{3,2,1,0:T(8,128)(2,1)}, bf16[8,2,16,1440]{3,2,1,0:T(8,128)(2,1)S(1)}, u32[]{:S(2)}, u32[]{:S(2)}) collective-permute-start(bf16[8,2,16,1440]{3,2,1,0:T(8,128)(2,1)} %get-tuple-element.46), channel_id=1, source_target_pairs={{0,1},{1,2},{2,3},{3,4},{4,5},{5,6},{6,7},{7,8},{8,9},{9,10},{10,1... | collective-permute-start | bytes 2211848 | tf_op jit(solution)/shard_map/ppermute | solution.py:330
  10.0 1.3 collective-permute-start.1
  11.4 0.1 copy.36
  11.8 0.1 copy.38
  12.0 0.1 copy.40
  12.1 0.4 reshape.55
  12.5 0.6 fusion.10
  13.3 0.6 fusion.13
  14.0 0.8 fusion.2
  14.7 0.7 pad_maximum_fusion.3.second_middle_ref
  15.4 0.7 reshape_tile.4.bias_ref
  16.1 1.3 fusion.column_ref
  17.4 9.1 %collective-permute-done.top_ref = bf16[8,2,16,1440]{3,2,1,0:T(8,128)(2,1)S(1)} collective-permute-done((bf16[8,2,16,1440]{3,2,1,0:T(8,128)(2,1)}, bf16[8,2,16,1440]{3,2,1,0:T(8,128)(2,1)S(1)}, u32[]{:S(2)}, u32[]{:S(2)}) %collective-permute-start) | collective-permute-done | bytes 737312 | tf_op jit(solution)/shard_map/ppermute | solution.py:330
  26.5 4.1 %collective-permute-done.1.bottom_ref = bf16[8,2,16,1440]{3,2,1,0:T(8,128)(2,1)} collective-permute-done((bf16[8,2,16,1440]{3,2,1,0:T(8,128)(2,1)}, bf16[8,2,16,1440]{3,2,1,0:T(8,128)(2,1)}, u32[]{:S(2)}, u32[]{:S(2)}) %collective-permute-start.1) | collective-permute-done | bytes 737312 | tf_op jit(solution)/shard_map/ppermute | solution.py:330
  30.6 4.1 %collective-permute-start.2 = (bf16[8,2,16,1440]{3,2,1,0:T(8,128)(2,1)S(1)}, bf16[8,2,16,1440]{3,2,1,0:T(8,128)(2,1)}, u32[]{:S(2)}, u32[]{:S(2)}) collective-permute-start(bf16[8,2,16,1440]{3,2,1,0:T(8,128)(2,1)S(1)} %get-tuple-element.26), channel_id=1, source_target_pairs={{0,1},{1,2},{2,3},{3,4},{4,5},{5,6},{6,7},{7,8},{8,9},{9,10},{10,1... | collective-permute-start | bytes 2211848 | tf_op jit(solution)/shard_map/ppermute | solution.py:330
  34.8 1.3 collective-permute-start.3
  36.0 15.2 %shard_map.112 = (bf16[8,8,8,1440]{3,2,1,0:T(8,128)(2,1)}, f32[8,256]{1,0:T(8,128)}) custom-call(bf16[16,4,16,1440]{3,2,1,0:T(8,128)(2,1)} %bitcast.37, bf16[8,2,16,1440]{3,2,1,0:T(8,128)(2,1)} %copy-done.12, bf16[8,2,16,1440]{3,2,1,0:T(8,128)(2,1)} %collective-permute-done.1.bottom_ref, bf16[384,256]{1,0:T(8,128)(2,1)} %get-tuple-element.58.first_top_ref, ...), custom_call_target="tpu_custom_call" | custom-call | flops 16000000000 | bytes 16000000 | tf_op jit(solution)/shard_map/pallas_call | solution.py:105
  51.2 6.6 %all-to-all-start = ((bf16[8,8,8,1440]{3,2,1,0:T(8,128)(2,1)}), bf16[8,8,8,1440]{3,2,1,0:T(8,128)(2,1)S(1)}, u32[]{:S(2)}, u32[]{:S(2)}) async-start(bf16[8,8,8,1440]{3,2,1,0:T(8,128)(2,1)} %get-tuple-element.39), calls=%async_computation | async-start | bytes 3145728 | tf_op jit(solution)/shard_map/all_to_all | solution.py:343
  57.8 15.2 %shard_map.113 = (bf16[8,8,8,1440]{3,2,1,0:T(8,128)(2,1)}, f32[8,256]{1,0:T(8,128)}) custom-call(bf16[16,4,16,1440]{3,2,1,0:T(8,128)(2,1)} %bitcast.38, bf16[8,2,16,1440]{3,2,1,0:T(8,128)(2,1)} %collective-permute-done.2.top_ref, bf16[8,2,16,1440]{3,2,1,0:T(8,128)(2,1)} %collective-permute-done.3.bottom_ref, ...), custom_call_target="tpu_custom_call" | custom-call | flops 16000000000 | bytes 16000000 | tf_op jit(solution)/shard_map/pallas_call | solution.py:105
  73.0 0.7 constant_dynamic-update-slice_fusion.refs_0_
  73.8 2.8 %collective-permute-start.10 = (f32[16,256]{1,0:T(8,128)S(1)}, f32[16,256]{1,0:T(8,128)S(1)}, u32[]{:S(2)}, u32[]{:S(2)}) collective-permute-start(f32[16,256]{1,0:T(8,128)S(1)} %constant_dynamic-update-slice_fusion.refs_0_), channel_id=1, source_target_pairs={{0,112},{16,96},{32,80},{48,64},{64,48},{80,32},{96,16},{112,0},{1... | collective-permute-start | bytes 49160 | tf_op jit(solution)/shard_map/ppermute | solution.py:320
  76.6 0.2 collective-permute-start.4
  76.7 2.0 %collective-permute-start.6 = (f32[16,256]{1,0:T(8,128)S(1)}, f32[16,256]{1,0:T(8,128)S(1)}, u32[]{:S(2)}, u32[]{:S(2)}) collective-permute-start(f32[16,256]{1,0:T(8,128)S(1)} %constant_dynamic-update-slice_fusion.refs_0_), channel_id=1, source_target_pairs={{0,48},{16,32},{32,16},{48,0},{64,112},{80,96},{96,80},{112,64},{1... | collective-permute-start | bytes 49160 | tf_op jit(solution)/shard_map/ppermute | solution.py:320
  78.7 0.5 collective-permute-start.7
  79.3 2.5 %collective-permute-start.8 = (f32[16,256]{1,0:T(8,128)S(1)}, f32[16,256]{1,0:T(8,128)S(1)}, u32[]{:S(2)}, u32[]{:S(2)}) collective-permute-start(f32[16,256]{1,0:T(8,128)S(1)} %constant_dynamic-update-slice_fusion.refs_0_), channel_id=1, source_target_pairs={{0,80},{16,64},{32,112},{48,96},{64,16},{80,0},{96,48},{112,32},{1... | collective-permute-start | bytes 49160 | tf_op jit(solution)/shard_map/ppermute | solution.py:320
  81.8 0.6 collective-permute-start.9
  82.3 0.5 iota_xor_fusion.place_ref
  83.6 0.4 collective-permute-done.8.refs_5_
  84.0 1.6 collective-permute-done.9.refs_6_
  85.6 0.5 copy-done.22
  86.2 1.8 %shard_map.114 = f32[136,128]{1,0:T(8,128)} custom-call(s32[8]{0:T(128)} %iota_xor_fusion.place_ref, s32[1]{0:T(128)S(6)} %copy.48.count_ref, f32[1,256]{1,0:T(1,128)} %bitcast.52, f32[1,256]{1,0:T(1,128)} %bitcast.53, f32[16,256]{1,0:T(8,128)} %copy-done.9, f32[16,256]{1,0:T(8,128)} %copy-done.17, f32[16,256]{1,0:T(8,128)} %copy-done.18, ...), custom_call_target="tpu_custom_call" | custom-call | flops 2000000000 | bytes 2000000 | tf_op jit(solution)/shard_map/pallas_call | solution.py:153
  88.0 2.3 %collective-permute-start.11 = (f32[136,128]{1,0:T(8,128)}, f32[136,128]{1,0:T(8,128)S(1)}, u32[]{:S(2)}, u32[]{:S(2)}) collective-permute-start(f32[136,128]{1,0:T(8,128)} %shard_map.114), channel_id=1, source_target_pairs={{0,1},{1,0},{2,3},{3,2},{4,5},{5,4},{6,7},{7,6},{8,9},{9,8},{10,11... | collective-permute-start | bytes 208904 | tf_op jit(solution)/shard_map/ppermute | solution.py:320
  90.3 2.9 %collective-permute-start.12 = (f32[136,128]{1,0:T(8,128)}, f32[136,128]{1,0:T(8,128)S(1)}, u32[]{:S(2)}, u32[]{:S(2)}) collective-permute-start(f32[136,128]{1,0:T(8,128)} %shard_map.114), channel_id=1, source_target_pairs={{0,2},{1,3},{2,0},{3,1},{4,6},{5,7},{6,4},{7,5},{8,10},{9,11},{10,... | collective-permute-start | bytes 208904 | tf_op jit(solution)/shard_map/ppermute | solution.py:320
  93.2 5.5 %all-to-all-start.1 = ((bf16[8,8,8,1440]{3,2,1,0:T(8,128)(2,1)}), bf16[8,8,8,1440]{3,2,1,0:T(8,128)(2,1)S(1)}, u32[]{:S(2)}, u32[]{:S(2)}) async-start(bf16[8,8,8,1440]{3,2,1,0:T(8,128)(2,1)} %get-tuple-element.40), calls=%async_computation.1 | async-start | bytes 3145728 | tf_op jit(solution)/shard_map/all_to_all | solution.py:343
  98.8 2.5 %collective-permute-start.14 = (f32[136,128]{1,0:T(8,128)S(1)}, f32[136,128]{1,0:T(8,128)S(1)}, u32[]{:S(2)}, u32[]{:S(2)}) collective-permute-start(f32[136,128]{1,0:T(8,128)S(1)} %add_add_fusion.a_ref), channel_id=1, source_target_pairs={{0,4},{1,5},{2,6},{3,7},{4,0},{5,1},{6,2},{7,3},{8,12},{9,13},{10,... | collective-permute-start | bytes 208904 | tf_op jit(solution)/shard_map/ppermute | solution.py:320
  101.3 2.9 %collective-permute-start.15 = (f32[136,128]{1,0:T(8,128)S(1)}, f32[136,128]{1,0:T(8,128)S(1)}, u32[]{:S(2)}, u32[]{:S(2)}) collective-permute-start(f32[136,128]{1,0:T(8,128)S(1)} %add_add_fusion.a_ref), channel_id=1, source_target_pairs={{0,8},{1,9},{2,10},{3,11},{4,12},{5,13},{6,14},{7,15},{8,0},{9,1},... | collective-permute-start | bytes 208904 | tf_op jit(solution)/shard_map/ppermute | solution.py:320
  104.2 3.7 %collective-permute-done.15.c_ref = f32[136,128]{1,0:T(8,128)S(1)} collective-permute-done((f32[136,128]{1,0:T(8,128)S(1)}, f32[136,128]{1,0:T(8,128)S(1)}, u32[]{:S(2)}, u32[]{:S(2)}) %collective-permute-start.15) | collective-permute-done | bytes 69664 | tf_op jit(solution)/shard_map/ppermute | solution.py:320
  107.9 1.3 collective-permute-done.16.d_ref
  109.2 0.6 copy-done.15
  109.8 5.7 %shard_map.115 = (f32[128,128]{1,0:T(8,128)}, f32[1,128]{1,0:T(1,128)}, bf16[128,128]{1,0:T(8,128)(2,1)}) custom-call(f32[136,128]{1,0:T(8,128)} %copy-done.4, f32[136,128]{1,0:T(8,128)} %copy-done.13, f32[136,128]{1,0:T(8,128)} %copy-done.14, f32[136,128]{1,0:T(8,128)} %copy-done.15), custom_call_target="tpu_custom_call" | custom-call | flops 12000000000 | bytes 12000000 | tf_op jit(solution)/shard_map/pallas_call | solution.py:217
  115.5 4.0 %all-to-all-done.1 = bf16[8,8,8,1440]{3,2,1,0:T(8,128)(2,1)S(1)} async-done(((bf16[8,8,8,1440]{3,2,1,0:T(8,128)(2,1)}), bf16[8,8,8,1440]{3,2,1,0:T(8,128)(2,1)S(1)}, u32[]{:S(2)}, u32[]{:S(2)}) %all-to-all-start.1) | async-done | bytes 1474592 | tf_op jit(solution)/shard_map/all_to_all | solution.py:343
  119.5 1.2 copy-done.2
  120.6 8.1 %shard_map.116 = bf16[1024,1440]{1,0:T(8,128)(2,1)} custom-call(bf16[128,128]{1,0:T(8,128)(2,1)} %get-tuple-element.38.transform_ref, bf16[512,1440]{1,0:T(8,128)(2,1)} %bitcast.42, bf16[512,1440]{1,0:T(8,128)(2,1)} %bitcast.43), custom_call_target="tpu_custom_call" | custom-call | flops 6000000000 | bytes 6000000 | tf_op jit(solution)/shard_map/pallas_call | solution.py:261
  128.7 42.3 %all_to_all.15 = bf16[8,16,8,1440]{3,2,1,0:T(8,128)(2,1)S(1)} all-to-all(bf16[8,16,8,1440]{3,2,1,0:T(8,128)(2,1)} %bitcast.41), channel_id=1, replica_groups=mesh['ens'=8,'map'=16] {'ens'}, dimensions={0} | all-to-all | bytes 5898240 | tf_op jit(solution)/shard_map/all_to_all | solution.py:343
  171.0 4.1 %copy.43 = bf16[4,2,16,8,1440]{4,0,3,1,2:T(4,128)(2,1)} copy(bf16[4,2,16,8,1440]{4,3,2,1,0:T(8,128)(2,1)S(1)} %bitcast.39) | data formatting | bytes 5898240 | tf_op jit(solution)/shard_map/reshape | solution.py:377
  (73 shorter events, 0.7 us)
Async XLA Ops:
  3.3 2.2 %copy-start = (bf16[16,16,4,1440]{3,1,2,0:T(8,128)(2,1)}, bf16[16,16,4,1440]{3,1,2,0:T(8,128)(2,1)S(1)}, u32[]{:S(2)}) copy-start(bf16[16,16,4,1440]{3,1,2,0:T(8,128)(2,1)S(1)} %copy.46) | copy-start | bytes 8847364
  3.3 8.0 %copy-start.11 = (f32[128]{0:T(128)S(1)}, f32[128]{0:T(128)}, u32[]{:S(2)}) copy-start(f32[128]{0:T(128)} %param.11) | copy-start | bytes 1540
  3.3 8.2 %copy-start.5 = (bf16[128,16,3,3]{0,1,3,2:T(8,128)(2,1)S(1)}, bf16[128,16,3,3]{0,1,3,2:T(8,128)(2,1)}, u32[]{:S(2)}) copy-start(bf16[128,16,3,3]{0,1,3,2:T(8,128)(2,1)} %param.10) | copy-start | bytes 110596
  3.3 8.6 %copy-start.6 = (bf16[16,128,3,3]{1,0,3,2:T(8,128)(2,1)S(1)}, bf16[16,128,3,3]{1,0,3,2:T(8,128)(2,1)}, u32[]{:S(2)}) copy-start(bf16[16,128,3,3]{1,0,3,2:T(8,128)(2,1)} %param.12) | copy-start | bytes 110596
  5.5 7.0 %copy-start.8 = (s32[256]{0:T(256)S(1)}, s32[256]{0:T(256)}, u32[]{:S(2)}) copy-start(s32[256]{0:T(256)} %param.14) | copy-start | bytes 3076
  5.5 21.0 %collective-permute-start = (bf16[8,2,16,1440]{3,2,1,0:T(8,128)(2,1)}, bf16[8,2,16,1440]{3,2,1,0:T(8,128)(2,1)S(1)}, u32[]{:S(2)}, u32[]{:S(2)}) collective-permute-start(bf16[8,2,16,1440]{3,2,1,0:T(8,128)(2,1)} %get-tuple-element.46), channel_id=1, source_target_pairs={{0,1},{1,2},{2,3},{3,4},{4,5},{5,6},{6,7},{7,8},{8,9},{9,10},{10,1... | collective-permute-start | bytes 2211848 | tf_op jit(solution)/shard_map/ppermute | solution.py:330
  10.0 20.6 %collective-permute-start.1 = (bf16[8,2,16,1440]{3,2,1,0:T(8,128)(2,1)}, bf16[8,2,16,1440]{3,2,1,0:T(8,128)(2,1)}, u32[]{:S(2)}, u32[]{:S(2)}) collective-permute-start(bf16[8,2,16,1440]{3,2,1,0:T(8,128)(2,1)} %get-tuple-element.45), channel_id=1, source_target_pairs={{1,0},{2,1},{3,2},{4,3},{5,4},{6,5},{7,6},{8,7},{9,8},{10,9},{11,1... | collective-permute-start | bytes 2211848 | tf_op jit(solution)/shard_map/ppermute | solution.py:330
  11.5 3.9 %copy-start.10 = (f32[16]{0:T(128)S(1)}, f32[16]{0:T(128)}, u32[]{:S(2)}) copy-start(f32[16]{0:T(128)} %param.13) | copy-start | bytes 196
  26.5 9.6 %copy-start.12 = (bf16[8,2,16,1440]{3,2,1,0:T(8,128)(2,1)}, bf16[8,2,16,1440]{3,2,1,0:T(8,128)(2,1)S(1)}, u32[]{:S(2)}) copy-start(bf16[8,2,16,1440]{3,2,1,0:T(8,128)(2,1)S(1)} %collective-permute-done.top_ref) | copy-start | bytes 2211844
  30.6 27.2 %collective-permute-start.2 = (bf16[8,2,16,1440]{3,2,1,0:T(8,128)(2,1)S(1)}, bf16[8,2,16,1440]{3,2,1,0:T(8,128)(2,1)}, u32[]{:S(2)}, u32[]{:S(2)}) collective-permute-start(bf16[8,2,16,1440]{3,2,1,0:T(8,128)(2,1)S(1)} %get-tuple-element.26), channel_id=1, source_target_pairs={{0,1},{1,2},{2,3},{3,4},{4,5},{5,6},{6,7},{7,8},{8,9},{9,10},{10,1... | collective-permute-start | bytes 2211848 | tf_op jit(solution)/shard_map/ppermute | solution.py:330
  34.8 23.1 %collective-permute-start.3 = (bf16[8,2,16,1440]{3,2,1,0:T(8,128)(2,1)S(1)}, bf16[8,2,16,1440]{3,2,1,0:T(8,128)(2,1)}, u32[]{:S(2)}, u32[]{:S(2)}) collective-permute-start(bf16[8,2,16,1440]{3,2,1,0:T(8,128)(2,1)S(1)} %get-tuple-element.27), channel_id=1, source_target_pairs={{1,0},{2,1},{3,2},{4,3},{5,4},{6,5},{7,6},{8,7},{9,8},{10,9},{11,1... | collective-permute-start | bytes 2211848 | tf_op jit(solution)/shard_map/ppermute | solution.py:330
  51.2 6.6 %copy-start.7 = (f32[8,256]{1,0:T(8,128)S(1)}, f32[8,256]{1,0:T(8,128)}, u32[]{:S(2)}) copy-start(f32[8,256]{1,0:T(8,128)} %get-tuple-element.25) | copy-start | bytes 24580
  51.2 41.9 %all-to-all-start = ((bf16[8,8,8,1440]{3,2,1,0:T(8,128)(2,1)}), bf16[8,8,8,1440]{3,2,1,0:T(8,128)(2,1)S(1)}, u32[]{:S(2)}, u32[]{:S(2)}) async-start(bf16[8,8,8,1440]{3,2,1,0:T(8,128)(2,1)} %get-tuple-element.39), calls=%async_computation | async-start | bytes 3145728 | tf_op jit(solution)/shard_map/all_to_all | solution.py:343
  73.7 11.8 %copy-start.9 = (f32[16,256]{1,0:T(8,128)}, f32[16,256]{1,0:T(8,128)S(1)}, u32[]{:S(2)}) copy-start(f32[16,256]{1,0:T(8,128)S(1)} %constant_dynamic-update-slice_fusion.refs_0_) | copy-start | bytes 49156
  73.8 5.6 %collective-permute-start.10 = (f32[16,256]{1,0:T(8,128)S(1)}, f32[16,256]{1,0:T(8,128)S(1)}, u32[]{:S(2)}, u32[]{:S(2)}) collective-permute-start(f32[16,256]{1,0:T(8,128)S(1)} %constant_dynamic-update-slice_fusion.refs_0_), channel_id=1, source_target_pairs={{0,112},{16,96},{32,80},{48,64},{64,48},{80,32},{96,16},{112,0},{1... | collective-permute-start | bytes 49160 | tf_op jit(solution)/shard_map/ppermute | solution.py:320
  76.6 5.2 %collective-permute-start.4 = (f32[16,256]{1,0:T(8,128)S(1)}, f32[16,256]{1,0:T(8,128)S(1)}, u32[]{:S(2)}, u32[]{:S(2)}) collective-permute-start(f32[16,256]{1,0:T(8,128)S(1)} %constant_dynamic-update-slice_fusion.refs_0_), channel_id=1, source_target_pairs={{0,16},{16,0},{32,48},{48,32},{64,80},{80,64},{96,112},{112,96},{1... | collective-permute-start | bytes 49160 | tf_op jit(solution)/shard_map/ppermute | solution.py:320
  76.7 6.8 %collective-permute-start.5 = (f32[16,256]{1,0:T(8,128)S(1)}, f32[16,256]{1,0:T(8,128)S(1)}, u32[]{:S(2)}, u32[]{:S(2)}) collective-permute-start(f32[16,256]{1,0:T(8,128)S(1)} %constant_dynamic-update-slice_fusion.refs_0_), channel_id=1, source_target_pairs={{0,32},{16,48},{32,0},{48,16},{64,96},{80,112},{96,64},{112,80},{1... | collective-permute-start | bytes 49160 | tf_op jit(solution)/shard_map/ppermute | solution.py:320
  76.7 6.8 %collective-permute-start.6 = (f32[16,256]{1,0:T(8,128)S(1)}, f32[16,256]{1,0:T(8,128)S(1)}, u32[]{:S(2)}, u32[]{:S(2)}) collective-permute-start(f32[16,256]{1,0:T(8,128)S(1)} %constant_dynamic-update-slice_fusion.refs_0_), channel_id=1, source_target_pairs={{0,48},{16,32},{32,16},{48,0},{64,112},{80,96},{96,80},{112,64},{1... | collective-permute-start | bytes 49160 | tf_op jit(solution)/shard_map/ppermute | solution.py:320
  78.7 4.8 %collective-permute-start.7 = (f32[16,256]{1,0:T(8,128)S(1)}, f32[16,256]{1,0:T(8,128)S(1)}, u32[]{:S(2)}, u32[]{:S(2)}) collective-permute-start(f32[16,256]{1,0:T(8,128)S(1)} %constant_dynamic-update-slice_fusion.refs_0_), channel_id=1, source_target_pairs={{0,64},{16,80},{32,96},{48,112},{64,0},{80,16},{96,32},{112,48},{1... | collective-permute-start | bytes 49160 | tf_op jit(solution)/shard_map/ppermute | solution.py:320
  79.3 6.3 %copy-start.16 = (f32[16,256]{1,0:T(8,128)}, f32[16,256]{1,0:T(8,128)S(1)}, u32[]{:S(2)}) copy-start(f32[16,256]{1,0:T(8,128)S(1)} %collective-permute-done.10.refs_7_) | copy-start | bytes 49156
  79.3 4.7 %collective-permute-start.8 = (f32[16,256]{1,0:T(8,128)S(1)}, f32[16,256]{1,0:T(8,128)S(1)}, u32[]{:S(2)}, u32[]{:S(2)}) collective-permute-start(f32[16,256]{1,0:T(8,128)S(1)} %constant_dynamic-update-slice_fusion.refs_0_), channel_id=1, source_target_pairs={{0,80},{16,64},{32,112},{48,96},{64,16},{80,0},{96,48},{112,32},{1... | collective-permute-start | bytes 49160 | tf_op jit(solution)/shard_map/ppermute | solution.py:320
  81.8 3.8 %copy-start.17 = (f32[16,256]{1,0:T(8,128)}, f32[16,256]{1,0:T(8,128)S(1)}, u32[]{:S(2)}) copy-start(f32[16,256]{1,0:T(8,128)S(1)} %collective-permute-done.4.refs_1_) | copy-start | bytes 49156
  81.8 3.8 %collective-permute-start.9 = (f32[16,256]{1,0:T(8,128)S(1)}, f32[16,256]{1,0:T(8,128)S(1)}, u32[]{:S(2)}, u32[]{:S(2)}) collective-permute-start(f32[16,256]{1,0:T(8,128)S(1)} %constant_dynamic-update-slice_fusion.refs_0_), channel_id=1, source_target_pairs={{0,96},{16,112},{32,64},{48,80},{64,32},{80,48},{96,0},{112,16},{1... | collective-permute-start | bytes 49160 | tf_op jit(solution)/shard_map/ppermute | solution.py:320
  83.5 2.1 %copy-start.18 = (f32[16,256]{1,0:T(8,128)}, f32[16,256]{1,0:T(8,128)S(1)}, u32[]{:S(2)}) copy-start(f32[16,256]{1,0:T(8,128)S(1)} %collective-permute-done.5.refs_2_) | copy-start | bytes 49156
  83.5 2.1 %copy-start.19 = (f32[16,256]{1,0:T(8,128)}, f32[16,256]{1,0:T(8,128)S(1)}, u32[]{:S(2)}) copy-start(f32[16,256]{1,0:T(8,128)S(1)} %collective-permute-done.6.refs_3_) | copy-start | bytes 49156
  83.5 2.1 %copy-start.20 = (f32[16,256]{1,0:T(8,128)}, f32[16,256]{1,0:T(8,128)S(1)}, u32[]{:S(2)}) copy-start(f32[16,256]{1,0:T(8,128)S(1)} %collective-permute-done.7.refs_4_) | copy-start | bytes 49156
  84.0 1.6 copy-start.21
  85.6 0.6 copy-start.22
  88.0 10.8 %copy-start.3 = (f32[136,128]{1,0:T(8,128)S(1)}, f32[136,128]{1,0:T(8,128)}, u32[]{:S(2)}) copy-start(f32[136,128]{1,0:T(8,128)} %shard_map.114) | copy-start | bytes 208900
  88.0 10.7 %collective-permute-start.11 = (f32[136,128]{1,0:T(8,128)}, f32[136,128]{1,0:T(8,128)S(1)}, u32[]{:S(2)}, u32[]{:S(2)}) collective-permute-start(f32[136,128]{1,0:T(8,128)} %shard_map.114), channel_id=1, source_target_pairs={{0,1},{1,0},{2,3},{3,2},{4,5},{5,4},{6,7},{7,6},{8,9},{9,8},{10,11... | collective-permute-start | bytes 208904 | tf_op jit(solution)/shard_map/ppermute | solution.py:320
  90.3 8.4 %collective-permute-start.12 = (f32[136,128]{1,0:T(8,128)}, f32[136,128]{1,0:T(8,128)S(1)}, u32[]{:S(2)}, u32[]{:S(2)}) collective-permute-start(f32[136,128]{1,0:T(8,128)} %shard_map.114), channel_id=1, source_target_pairs={{0,2},{1,3},{2,0},{3,1},{4,6},{5,7},{6,4},{7,5},{8,10},{9,11},{10,... | collective-permute-start | bytes 208904 | tf_op jit(solution)/shard_map/ppermute | solution.py:320
  93.2 5.6 %collective-permute-start.13 = (f32[136,128]{1,0:T(8,128)}, f32[136,128]{1,0:T(8,128)S(1)}, u32[]{:S(2)}, u32[]{:S(2)}) collective-permute-start(f32[136,128]{1,0:T(8,128)} %shard_map.114), channel_id=1, source_target_pairs={{0,3},{1,2},{2,1},{3,0},{4,7},{5,6},{6,5},{7,4},{8,11},{9,10},{10,... | collective-permute-start | bytes 208904 | tf_op jit(solution)/shard_map/ppermute | solution.py:320
  93.2 22.3 %copy-start.1 = (bf16[8,8,8,1440]{3,2,1,0:T(8,128)(2,1)}, bf16[8,8,8,1440]{3,2,1,0:T(8,128)(2,1)S(1)}, u32[]{:S(2)}) copy-start(bf16[8,8,8,1440]{3,2,1,0:T(8,128)(2,1)S(1)} %all-to-all-done) | copy-start | bytes 4423684
  93.2 26.3 %all-to-all-start.1 = ((bf16[8,8,8,1440]{3,2,1,0:T(8,128)(2,1)}), bf16[8,8,8,1440]{3,2,1,0:T(8,128)(2,1)S(1)}, u32[]{:S(2)}, u32[]{:S(2)}) async-start(bf16[8,8,8,1440]{3,2,1,0:T(8,128)(2,1)} %get-tuple-element.40), calls=%async_computation.1 | async-start | bytes 3145728 | tf_op jit(solution)/shard_map/all_to_all | solution.py:343
  98.8 10.4 %copy-start.4 = (f32[136,128]{1,0:T(8,128)}, f32[136,128]{1,0:T(8,128)S(1)}, u32[]{:S(2)}) copy-start(f32[136,128]{1,0:T(8,128)S(1)} %add_add_fusion.a_ref) | copy-start | bytes 208900
  98.8 5.5 %collective-permute-start.14 = (f32[136,128]{1,0:T(8,128)S(1)}, f32[136,128]{1,0:T(8,128)S(1)}, u32[]{:S(2)}, u32[]{:S(2)}) collective-permute-start(f32[136,128]{1,0:T(8,128)S(1)} %add_add_fusion.a_ref), channel_id=1, source_target_pairs={{0,4},{1,5},{2,6},{3,7},{4,0},{5,1},{6,2},{7,3},{8,12},{9,13},{10,... | collective-permute-start | bytes 208904 | tf_op jit(solution)/shard_map/ppermute | solution.py:320
  101.3 6.6 %collective-permute-start.15 = (f32[136,128]{1,0:T(8,128)S(1)}, f32[136,128]{1,0:T(8,128)S(1)}, u32[]{:S(2)}, u32[]{:S(2)}) collective-permute-start(f32[136,128]{1,0:T(8,128)S(1)} %add_add_fusion.a_ref), channel_id=1, source_target_pairs={{0,8},{1,9},{2,10},{3,11},{4,12},{5,13},{6,14},{7,15},{8,0},{9,1},... | collective-permute-start | bytes 208904 | tf_op jit(solution)/shard_map/ppermute | solution.py:320
  104.2 5.0 %collective-permute-start.16 = (f32[136,128]{1,0:T(8,128)S(1)}, f32[136,128]{1,0:T(8,128)S(1)}, u32[]{:S(2)}, u32[]{:S(2)}) collective-permute-start(f32[136,128]{1,0:T(8,128)S(1)} %add_add_fusion.a_ref), channel_id=1, source_target_pairs={{0,12},{1,13},{2,14},{3,15},{4,8},{5,9},{6,10},{7,11},{8,4},{9,5},... | collective-permute-start | bytes 208904 | tf_op jit(solution)/shard_map/ppermute | solution.py:320
  104.2 5.0 %copy-start.13 = (f32[136,128]{1,0:T(8,128)}, f32[136,128]{1,0:T(8,128)S(1)}, u32[]{:S(2)}) copy-start(f32[136,128]{1,0:T(8,128)S(1)} %collective-permute-done.14.b_ref) | copy-start | bytes 208900
  107.9 1.3 copy-start.14
  109.2 0.6 copy-start.15
  119.5 1.2 copy-start.2

commit v4 on v3

--- a/solution.py
+++ b/solution.py
@@ -155,7 +155,7 @@
         in_specs=[smem, smem] + [vmem] * (2 + N_ENS),
         out_specs=vmem,
         out_shape=jax.ShapeDtypeStruct((MEMBERS + 8, MEMBERS), jnp.float32),
-        cost_estimate=cost(2),
+        cost_estimate=cost(1),
         scratch_shapes=[pltpu.VMEM((MEMBERS, SLOTS), jnp.float32)],
     )(places, count, value.reshape(1, SLOTS), sigma.reshape(1, SLOTS), *pieces)
 
@@ -223,7 +223,7 @@
             jax.ShapeDtypeStruct((1, MEMBERS), jnp.float32),
             jax.ShapeDtypeStruct((MEMBERS, MEMBERS), jnp.bfloat16),
         ],
-        cost_estimate=cost(12),
+        cost_estimate=cost(1),
     )(*parts)
 
 
@@ -319,15 +319,20 @@
         pairs = [(i, i ^ step) for i in range(lax.axis_size(axis))]
         return lax.ppermute(value, axis, pairs)
 
+    share = GROUP // CHUNKS
+
+    def edges(chunk):
+        part = ensemble_weather[chunk * share : (chunk + 1) * share]
+        rows = lambda low: jnp.transpose(part[:, :, low : low + 2], (0, 2, 1, 3))
+        return rows(ROWS - 2), rows(0)
+
+    def halo(rows):
+        return lax.ppermute(rows[0], "map", down), lax.ppermute(rows[1], "map", up)
+
+    own_edges = edges(0)
+    halos = [halo(own_edges)]
+    own_edges, ensemble_weather = lax.optimization_barrier((own_edges, ensemble_weather))
     own = jnp.transpose(ensemble_weather, (0, 2, 1, 3))
-    share = GROUP // CHUNKS
-    halos = []
-    for chunk in range(CHUNKS):
-        part = own[chunk * share : (chunk + 1) * share]
-        edges = (part[:, ROWS - 2 :], part[:, :2])
-        if halos:
-            edges, halos[-1] = lax.optimization_barrier((edges, halos[-1]))
-        halos.append((lax.ppermute(edges[0], "map", down), lax.ppermute(edges[1], "map", up)))
     one = jnp.float32(1.0)
     inner_top = (tile > 0).astype(jnp.float32)
     inner_bottom = (tile < tiles - 1).astype(jnp.float32)
@@ -339,10 +344,12 @@
     column = observed_entry_index - plane * LON
     picks = (jnp.arange(RING)[:, None] == column[None, :]).astype(jnp.bfloat16)
     plane = ((plane % ROWS) * FIELDS + plane // ROWS).reshape(1, SLOTS)
-
     exchange = lambda value: lax.all_to_all(
         value, "ens", split_axis=0, concat_axis=0, tiled=True
     )
+    next_edges, picks = lax.optimization_barrier((edges(1), picks))
+    halos.append(halo(next_edges))
+
     fields, observed = [], []
     for chunk, (top, bottom) in enumerate(halos):
         moved, seen = forecast(
@@ -365,7 +372,7 @@
     observed = jnp.concatenate(observed, axis=0)
     pieces = [observed] + [swap(observed, "ens", step) for step in range(1, N_ENS)]
     places = jnp.bitwise_xor(own_place, jnp.arange(N_ENS, dtype=jnp.int32))
-    pieces, late = lax.optimization_barrier((pieces, fields[1]))
+    pieces, late, early = lax.optimization_barrier((pieces, fields[1], early))
     late = exchange(late)
     part = products(pieces, places, obs_count, obs_value, obs_sigma)
     near = [part] + [swap(part, "map", step) for step in (1, 2, 3)]

time: 177 us -> 175 us (0.989)
  waiting for transfers between devices: 24.3 us -> 13.1 us
  local copies, waits for them, and re-layouts: 14.3 us -> 21.8 us
  blocking collectives: 42.3 us -> 44.9 us
    ppermute x4, waiting for transfers between devices: 13.3 us -> 0.01 us  [the longest x2 0.01 us: halo(): lax.ppermute(rows[1], 'map', up)]
    ppermute x13, waiting for transfers between devices: 7.02 us -> 13.1 us  [swap(): return lax.ppermute(value, axis, pairs)]
    all_to_all x2, waiting for transfers between devices: 3.96 us -> 0.01 us  [on_device(): lax.all_to_all(value, 'ens', split_axis=0, concat_axis=0, tiled=True)]
    all_to_all x1, blocking collectives: 42.3 us -> 44.9 us  [on_device(): lax.all_to_all(value, 'ens', split_axis=0, concat_axis=0, tiled=True)]
    ppermute x13, starting transfers between devices: 19.2 us -> 17.1 us  [swap(): return lax.ppermute(value, axis, pairs)]
    slice x1, local copies, waits for them, and re-layouts: 1.75 us -> 3.66 us  [edges(): rows = lambda low: jnp.transpose(part[:, :, low:low + 2], (0, 2, 1, 3))]
    reshape x3, local copies, waits for them, and re-layouts: 0.3 us -> 2.1 us  [first_weights(): jnp.pad(by_tap, ((0, 0), (0, 0), (r, 2 - r), (0, 0)))]
    unnamed x48 -> x49, local copies, waits for them, and re-layouts: 5.48 us -> 3.9 us
  transfers between devices with their start and end apart: 19 -> 19, of which waited for: 7 -> 7; matrix products, arithmetic and copies ran while one was open for 4% -> 9% of each run, Pallas kernels for 22% -> 22%
where the time goes in v4:
time: 175 us; the launch traced here: 174 us
  Pallas kernels  45.9 us (26%)
  blocking collectives  44.9 us (26%)
  starting transfers between devices  42.2 us (24%)
  local copies, waits for them, and re-layouts  21.8 us (12%)
  waiting for transfers between devices  13.1 us (7%)
  other arithmetic  4.92 us (3%)
    all_to_all x1, blocking collectives, on_device(): lax.all_to_all(value, 'ens', split_axis=0, concat_axis=0, tiled=True)  44.9 us
    pallas_call x2, Pallas kernels, forecast(): pl.pallas_call(forecast_kernel, grid=(count,), in_specs=[pl.BlockSpec((1,...  30.3 us
    ppermute x13, starting transfers between devices, swap(): return lax.ppermute(value, axis, pairs)  17.1 us
    ppermute x13, waiting for transfers between devices, swap(): return lax.ppermute(value, axis, pairs)  13.1 us
    all_to_all x2, starting transfers between devices, on_device(): lax.all_to_all(value, 'ens', split_axis=0, concat_axis=0, tiled=True)  12.3 us
    ppermute x2, starting transfers between devices, halo(): lax.ppermute(rows[0], 'map', down)  10.2 us
    pallas_call x1, Pallas kernels, update(): pl.pallas_call(update_kernel, grid=(RING // 256,), in_specs=[pl.BlockSpec...  8.1 us
    pallas_call x1, Pallas kernels, transform_of(): pl.pallas_call(transform_kernel, in_specs=[vmem] * 4, out_specs=[vmem, vm...  5.67 us
  transfers between devices with their start and end apart: 19, of which 7 were waited for; matrix products, arithmetic and copies ran while one was open for 9% of the time, Pallas kernels for 22%

profile of v4, /device:TPU:1, one launch (start us, length us, event | category | flops | bytes accessed | tf_op | source)
XLA Modules:
  0.0 174.5 jit_solution(13344828110773241480)
XLA Ops:
  0.6 3.7 %fusion.12 = (bf16[8,16,2,1440]{3,2,1,0:T(2,128)(2,1)S(1)}, bf16[8,16,2,1440]{3,2,1,0:T(2,128)(2,1)S(1)}) fusion(bf16[16,16,4,1440]{3,2,1,0:T(4,128)(2,1)} %param.9), kind=kLoop, calls=%fused_computation.48 | loop fusion | bytes 2949120 | tf_op jit(solution)/shard_map/slice | solution.py:326
  4.3 1.0 copy.64
  5.3 5.3 %collective-permute-start = (bf16[8,2,16,1440]{3,2,1,0:T(8,128)(2,1)}, bf16[8,2,16,1440]{3,2,1,0:T(8,128)(2,1)}, u32[]{:S(2)}, u32[]{:S(2)}) collective-permute-start(bf16[8,2,16,1440]{3,2,1,0:T(8,128)(2,1)} %bitcast.44), channel_id=1, source_target_pairs={{0,1},{1,2},{2,3},{3,4},{4,5},{5,6},{6,7},{7,8},{8,9},{9,10},{10,1... | collective-permute-start | bytes 2211848 | tf_op jit(solution)/shard_map/ppermute | solution.py:330
  10.6 1.0 copy.63
  11.6 1.3 collective-permute-start.1
  12.9 0.8 copy.65
  13.7 1.3 slice_bitcast_fusion
  15.6 1.2 fusion.column_ref
  16.8 4.9 %collective-permute-start.2 = (bf16[8,2,16,1440]{3,2,1,0:T(8,128)(2,1)}, bf16[8,2,16,1440]{3,2,1,0:T(8,128)(2,1)}, u32[]{:S(2)}, u32[]{:S(2)}) collective-permute-start(bf16[8,2,16,1440]{3,2,1,0:T(8,128)(2,1)} %get-tuple-element.27), channel_id=1, source_target_pairs={{0,1},{1,2},{2,3},{3,4},{4,5},{5,6},{6,7},{7,8},{8,9},{9,10},{10,1... | collective-permute-start | bytes 2211848 | tf_op jit(solution)/shard_map/ppermute | solution.py:330
  21.7 1.3 collective-permute-start.3
  23.1 0.8 fusion.16
  24.1 1.1 reshape.55
  25.1 1.0 fusion.13
  26.3 1.0 copy.47
  27.3 1.0 copy.49
  28.3 0.9 pad.38
  29.3 0.7 reshape_tile.4.bias_ref
  30.0 0.6 fusion.14
  30.7 0.6 pad_maximum_fusion.3.second_middle_ref
  31.5 0.8 fusion.2
  32.3 15.2 %shard_map.112 = (bf16[8,8,8,1440]{3,2,1,0:T(8,128)(2,1)}, f32[8,256]{1,0:T(8,128)}) custom-call(bf16[16,4,16,1440]{3,2,1,0:T(8,128)(2,1)} %bitcast.46, bf16[8,2,16,1440]{3,2,1,0:T(8,128)(2,1)} %collective-permute-done.top_ref, bf16[8,2,16,1440]{3,2,1,0:T(8,128)(2,1)} %collective-permute-done.1.bottom_ref, bf16[384,256]{1,0:T(8,128)(2,1)} %get-tuple-element.62.first_top_ref, ...), custom_call_target="tpu_custom_call" | custom-call | flops 16000000000 | bytes 16000000 | tf_op jit(solution)/shard_map/pallas_call | solution.py:105
  47.5 7.3 %all-to-all-start = ((bf16[8,8,8,1440]{3,2,1,0:T(8,128)(2,1)}), bf16[8,8,8,1440]{3,2,1,0:T(8,128)(2,1)S(1)}, u32[]{:S(2)}, u32[]{:S(2)}) async-start(bf16[8,8,8,1440]{3,2,1,0:T(8,128)(2,1)} %get-tuple-element.31), calls=%async_computation | async-start | bytes 3145728 | tf_op jit(solution)/shard_map/all_to_all | solution.py:347
  54.8 15.1 %shard_map.113 = (bf16[8,8,8,1440]{3,2,1,0:T(8,128)(2,1)}, f32[8,256]{1,0:T(8,128)}) custom-call(bf16[16,4,16,1440]{3,2,1,0:T(8,128)(2,1)} %bitcast.47, bf16[8,2,16,1440]{3,2,1,0:T(8,128)(2,1)} %collective-permute-done.2.top_ref, bf16[8,2,16,1440]{3,2,1,0:T(8,128)(2,1)} %collective-permute-done.3.bottom_ref, ...), custom_call_target="tpu_custom_call" | custom-call | flops 16000000000 | bytes 16000000 | tf_op jit(solution)/shard_map/pallas_call | solution.py:105
  70.0 0.7 constant_dynamic-update-slice_fusion.refs_0_
  70.7 2.9 %collective-permute-start.10 = (f32[16,256]{1,0:T(8,128)S(1)}, f32[16,256]{1,0:T(8,128)S(1)}, u32[]{:S(2)}, u32[]{:S(2)}) collective-permute-start(f32[16,256]{1,0:T(8,128)S(1)} %constant_dynamic-update-slice_fusion.refs_0_), channel_id=1, source_target_pairs={{0,112},{16,96},{32,80},{48,64},{64,48},{80,32},{96,16},{112,0},{1... | collective-permute-start | bytes 49160 | tf_op jit(solution)/shard_map/ppermute | solution.py:320
  73.7 2.0 %collective-permute-start.6 = (f32[16,256]{1,0:T(8,128)S(1)}, f32[16,256]{1,0:T(8,128)S(1)}, u32[]{:S(2)}, u32[]{:S(2)}) collective-permute-start(f32[16,256]{1,0:T(8,128)S(1)} %constant_dynamic-update-slice_fusion.refs_0_), channel_id=1, source_target_pairs={{0,48},{16,32},{32,16},{48,0},{64,112},{80,96},{96,80},{112,64},{1... | collective-permute-start | bytes 49160 | tf_op jit(solution)/shard_map/ppermute | solution.py:320
  75.7 0.6 collective-permute-start.7
  76.3 2.4 %collective-permute-start.8 = (f32[16,256]{1,0:T(8,128)S(1)}, f32[16,256]{1,0:T(8,128)S(1)}, u32[]{:S(2)}, u32[]{:S(2)}) collective-permute-start(f32[16,256]{1,0:T(8,128)S(1)} %constant_dynamic-update-slice_fusion.refs_0_), channel_id=1, source_target_pairs={{0,80},{16,64},{32,112},{48,96},{64,16},{80,0},{96,48},{112,32},{1... | collective-permute-start | bytes 49160 | tf_op jit(solution)/shard_map/ppermute | solution.py:320
  78.7 0.6 collective-permute-start.9
  79.8 1.2 collective-permute-done.8.refs_5_
  81.0 1.6 collective-permute-done.9.refs_6_
  82.5 5.0 %all-to-all-start.1 = ((bf16[8,8,8,1440]{3,2,1,0:T(8,128)(2,1)}), bf16[8,8,8,1440]{3,2,1,0:T(8,128)(2,1)S(1)}, u32[]{:S(2)}, u32[]{:S(2)}) async-start(bf16[8,8,8,1440]{3,2,1,0:T(8,128)(2,1)} %get-tuple-element.42), calls=%async_computation.1 | async-start | bytes 3145728 | tf_op jit(solution)/shard_map/all_to_all | solution.py:347
  88.7 1.8 %shard_map.114 = f32[136,128]{1,0:T(8,128)} custom-call(s32[8]{0:T(128)} %iota_xor_fusion.place_ref, s32[1]{0:T(128)S(6)} %copy.67.count_ref, f32[1,256]{1,0:T(1,128)} %bitcast.60, f32[1,256]{1,0:T(1,128)} %bitcast.61, f32[16,256]{1,0:T(8,128)} %copy-done.10, f32[16,256]{1,0:T(8,128)} %copy-done.17, f32[16,256]{1,0:T(8,128)} %copy-done.18, ...), custom_call_target="tpu_custom_call" | custom-call | flops 1000000000 | bytes 1000000 | tf_op jit(solution)/shard_map/pallas_call | solution.py:153
  90.6 1.0 collective-permute-start.11
  91.6 3.4 %collective-permute-start.12 = (f32[136,128]{1,0:T(8,128)}, f32[136,128]{1,0:T(8,128)S(1)}, u32[]{:S(2)}, u32[]{:S(2)}) collective-permute-start(f32[136,128]{1,0:T(8,128)} %shard_map.114), channel_id=1, source_target_pairs={{0,2},{1,3},{2,0},{3,1},{4,6},{5,7},{6,4},{7,5},{8,10},{9,11},{10,... | collective-permute-start | bytes 208904 | tf_op jit(solution)/shard_map/ppermute | solution.py:320
  95.0 4.0 %collective-permute-done.12 = f32[136,128]{1,0:T(8,128)S(1)} collective-permute-done((f32[136,128]{1,0:T(8,128)}, f32[136,128]{1,0:T(8,128)S(1)}, u32[]{:S(2)}, u32[]{:S(2)}) %collective-permute-start.12) | collective-permute-done | bytes 69664 | tf_op jit(solution)/shard_map/ppermute | solution.py:320
  99.0 1.2 collective-permute-done.13
  100.2 0.9 add_add_fusion.a_ref
  101.1 1.4 collective-permute-start.14
  102.5 2.4 %collective-permute-start.15 = (f32[136,128]{1,0:T(8,128)S(1)}, f32[136,128]{1,0:T(8,128)S(1)}, u32[]{:S(2)}, u32[]{:S(2)}) collective-permute-start(f32[136,128]{1,0:T(8,128)S(1)} %add_add_fusion.a_ref), channel_id=1, source_target_pairs={{0,8},{1,9},{2,10},{3,11},{4,12},{5,13},{6,14},{7,15},{8,0},{9,1},... | collective-permute-start | bytes 208904 | tf_op jit(solution)/shard_map/ppermute | solution.py:320
  105.2 2.5 %collective-permute-done.15.c_ref = f32[136,128]{1,0:T(8,128)S(1)} collective-permute-done((f32[136,128]{1,0:T(8,128)S(1)}, f32[136,128]{1,0:T(8,128)S(1)}, u32[]{:S(2)}, u32[]{:S(2)}) %collective-permute-start.15) | collective-permute-done | bytes 69664 | tf_op jit(solution)/shard_map/ppermute | solution.py:320
  107.7 2.2 %collective-permute-done.16.d_ref = f32[136,128]{1,0:T(8,128)S(1)} collective-permute-done((f32[136,128]{1,0:T(8,128)S(1)}, f32[136,128]{1,0:T(8,128)S(1)}, u32[]{:S(2)}, u32[]{:S(2)}) %collective-permute-start.16) | collective-permute-done | bytes 69664 | tf_op jit(solution)/shard_map/ppermute | solution.py:320
  109.9 0.6 copy-done.15
  110.5 5.7 %shard_map.115 = (f32[128,128]{1,0:T(8,128)}, f32[1,128]{1,0:T(1,128)}, bf16[128,128]{1,0:T(8,128)(2,1)}) custom-call(f32[136,128]{1,0:T(8,128)} %copy-done.5, f32[136,128]{1,0:T(8,128)} %copy-done.13, f32[136,128]{1,0:T(8,128)} %copy-done.14, f32[136,128]{1,0:T(8,128)} %copy-done.15), custom_call_target="tpu_custom_call" | custom-call | flops 1000000000 | bytes 1000000 | tf_op jit(solution)/shard_map/pallas_call | solution.py:217
  116.1 1.2 copy-done.3
  117.3 8.1 %shard_map.116 = bf16[1024,1440]{1,0:T(8,128)(2,1)} custom-call(bf16[128,128]{1,0:T(8,128)(2,1)} %get-tuple-element.40.transform_ref, bf16[512,1440]{1,0:T(8,128)(2,1)} %bitcast.50, bf16[512,1440]{1,0:T(8,128)(2,1)} %bitcast.51), custom_call_target="tpu_custom_call" | custom-call | flops 6000000000 | bytes 6000000 | tf_op jit(solution)/shard_map/pallas_call | solution.py:261
  125.4 44.9 %all_to_all.15 = bf16[8,16,8,1440]{3,2,1,0:T(8,128)(2,1)S(1)} all-to-all(bf16[8,16,8,1440]{3,2,1,0:T(8,128)(2,1)} %bitcast.49), channel_id=1, replica_groups=mesh['ens'=8,'map'=16] {'ens'}, dimensions={0} | all-to-all | bytes 5898240 | tf_op jit(solution)/shard_map/all_to_all | solution.py:347
  170.4 4.1 %copy.55 = bf16[4,2,16,8,1440]{4,0,3,1,2:T(4,128)(2,1)} copy(bf16[4,2,16,8,1440]{4,3,2,1,0:T(8,128)(2,1)S(1)} %bitcast.45) | data formatting | bytes 5898240 | tf_op jit(solution)/shard_map/reshape | solution.py:384
  (76 shorter events, 2.7 us)
Async XLA Ops:
  0.6 12.3 %copy-start = (bf16[16,16,4,1440]{3,2,1,0:T(4,128)(2,1)S(1)}, bf16[16,16,4,1440]{3,2,1,0:T(4,128)(2,1)}, u32[]{:S(2)}) copy-start(bf16[16,16,4,1440]{3,2,1,0:T(4,128)(2,1)} %param.9) | copy-start | bytes 8847364
  5.3 27.0 %collective-permute-start = (bf16[8,2,16,1440]{3,2,1,0:T(8,128)(2,1)}, bf16[8,2,16,1440]{3,2,1,0:T(8,128)(2,1)}, u32[]{:S(2)}, u32[]{:S(2)}) collective-permute-start(bf16[8,2,16,1440]{3,2,1,0:T(8,128)(2,1)} %bitcast.44), channel_id=1, source_target_pairs={{0,1},{1,2},{2,3},{3,4},{4,5},{5,6},{6,7},{7,8},{8,9},{9,10},{10,1... | collective-permute-start | bytes 2211848 | tf_op jit(solution)/shard_map/ppermute | solution.py:330
  11.6 20.7 %collective-permute-start.1 = (bf16[8,2,16,1440]{3,2,1,0:T(8,128)(2,1)}, bf16[8,2,16,1440]{3,2,1,0:T(8,128)(2,1)}, u32[]{:S(2)}, u32[]{:S(2)}) collective-permute-start(bf16[8,2,16,1440]{3,2,1,0:T(8,128)(2,1)} %bitcast.43), channel_id=1, source_target_pairs={{1,0},{2,1},{3,2},{4,3},{5,4},{6,5},{7,6},{8,7},{9,8},{10,9},{11,1... | collective-permute-start | bytes 2211848 | tf_op jit(solution)/shard_map/ppermute | solution.py:330
  13.7 11.5 %copy-start.1 = (bf16[16,16,4,1440]{3,1,2,0:T(8,128)(2,1)}, bf16[16,16,4,1440]{3,1,2,0:T(8,128)(2,1)S(1)}, u32[]{:S(2)}) copy-start(bf16[16,16,4,1440]{3,1,2,0:T(8,128)(2,1)S(1)} %copy.65) | copy-start | bytes 8847364
  13.7 1.3 copy-start.9
  13.7 9.3 %copy-start.12 = (f32[128]{0:T(128)S(1)}, f32[128]{0:T(128)}, u32[]{:S(2)}) copy-start(f32[128]{0:T(128)} %param.11) | copy-start | bytes 1540
  13.7 9.3 %copy-start.6 = (bf16[128,16,3,3]{0,1,3,2:T(8,128)(2,1)S(1)}, bf16[128,16,3,3]{0,1,3,2:T(8,128)(2,1)}, u32[]{:S(2)}) copy-start(bf16[128,16,3,3]{0,1,3,2:T(8,128)(2,1)} %param.10) | copy-start | bytes 110596
  13.7 10.1 %copy-start.7 = (bf16[16,128,3,3]{1,0,3,2:T(8,128)(2,1)S(1)}, bf16[16,128,3,3]{1,0,3,2:T(8,128)(2,1)}, u32[]{:S(2)}) copy-start(bf16[16,128,3,3]{1,0,3,2:T(8,128)(2,1)} %param.12) | copy-start | bytes 110596
  15.0 14.3 %copy-start.11 = (f32[16]{0:T(128)S(1)}, f32[16]{0:T(128)}, u32[]{:S(2)}) copy-start(f32[16]{0:T(128)} %param.13) | copy-start | bytes 196
  16.8 38.0 %collective-permute-start.2 = (bf16[8,2,16,1440]{3,2,1,0:T(8,128)(2,1)}, bf16[8,2,16,1440]{3,2,1,0:T(8,128)(2,1)}, u32[]{:S(2)}, u32[]{:S(2)}) collective-permute-start(bf16[8,2,16,1440]{3,2,1,0:T(8,128)(2,1)} %get-tuple-element.27), channel_id=1, source_target_pairs={{0,1},{1,2},{2,3},{3,4},{4,5},{5,6},{6,7},{7,8},{8,9},{9,10},{10,1... | collective-permute-start | bytes 2211848 | tf_op jit(solution)/shard_map/ppermute | solution.py:330
  21.7 33.1 %collective-permute-start.3 = (bf16[8,2,16,1440]{3,2,1,0:T(8,128)(2,1)}, bf16[8,2,16,1440]{3,2,1,0:T(8,128)(2,1)}, u32[]{:S(2)}, u32[]{:S(2)}) collective-permute-start(bf16[8,2,16,1440]{3,2,1,0:T(8,128)(2,1)} %get-tuple-element.28), channel_id=1, source_target_pairs={{1,0},{2,1},{3,2},{4,3},{5,4},{6,5},{7,6},{8,7},{9,8},{10,9},{11,1... | collective-permute-start | bytes 2211848 | tf_op jit(solution)/shard_map/ppermute | solution.py:330
  23.1 0.8 copy-start.4
  47.5 7.3 %copy-start.8 = (f32[8,256]{1,0:T(8,128)S(1)}, f32[8,256]{1,0:T(8,128)}, u32[]{:S(2)}) copy-start(f32[8,256]{1,0:T(8,128)} %get-tuple-element.26) | copy-start | bytes 24580
  47.5 35.0 %all-to-all-start = ((bf16[8,8,8,1440]{3,2,1,0:T(8,128)(2,1)}), bf16[8,8,8,1440]{3,2,1,0:T(8,128)(2,1)S(1)}, u32[]{:S(2)}, u32[]{:S(2)}) async-start(bf16[8,8,8,1440]{3,2,1,0:T(8,128)(2,1)} %get-tuple-element.31), calls=%async_computation | async-start | bytes 3145728 | tf_op jit(solution)/shard_map/all_to_all | solution.py:347
  70.7 18.0 %copy-start.10 = (f32[16,256]{1,0:T(8,128)}, f32[16,256]{1,0:T(8,128)S(1)}, u32[]{:S(2)}) copy-start(f32[16,256]{1,0:T(8,128)S(1)} %constant_dynamic-update-slice_fusion.refs_0_) | copy-start | bytes 49156
  70.7 5.6 %collective-permute-start.10 = (f32[16,256]{1,0:T(8,128)S(1)}, f32[16,256]{1,0:T(8,128)S(1)}, u32[]{:S(2)}, u32[]{:S(2)}) collective-permute-start(f32[16,256]{1,0:T(8,128)S(1)} %constant_dynamic-update-slice_fusion.refs_0_), channel_id=1, source_target_pairs={{0,112},{16,96},{32,80},{48,64},{64,48},{80,32},{96,16},{112,0},{1... | collective-permute-start | bytes 49160 | tf_op jit(solution)/shard_map/ppermute | solution.py:320
  73.6 5.2 %collective-permute-start.4 = (f32[16,256]{1,0:T(8,128)S(1)}, f32[16,256]{1,0:T(8,128)S(1)}, u32[]{:S(2)}, u32[]{:S(2)}) collective-permute-start(f32[16,256]{1,0:T(8,128)S(1)} %constant_dynamic-update-slice_fusion.refs_0_), channel_id=1, source_target_pairs={{0,16},{16,0},{32,48},{48,32},{64,80},{80,64},{96,112},{112,96},{1... | collective-permute-start | bytes 49160 | tf_op jit(solution)/shard_map/ppermute | solution.py:320
  73.7 5.6 %collective-permute-start.5 = (f32[16,256]{1,0:T(8,128)S(1)}, f32[16,256]{1,0:T(8,128)S(1)}, u32[]{:S(2)}, u32[]{:S(2)}) collective-permute-start(f32[16,256]{1,0:T(8,128)S(1)} %constant_dynamic-update-slice_fusion.refs_0_), channel_id=1, source_target_pairs={{0,32},{16,48},{32,0},{48,16},{64,96},{80,112},{96,64},{112,80},{1... | collective-permute-start | bytes 49160 | tf_op jit(solution)/shard_map/ppermute | solution.py:320
  73.7 5.6 %collective-permute-start.6 = (f32[16,256]{1,0:T(8,128)S(1)}, f32[16,256]{1,0:T(8,128)S(1)}, u32[]{:S(2)}, u32[]{:S(2)}) collective-permute-start(f32[16,256]{1,0:T(8,128)S(1)} %constant_dynamic-update-slice_fusion.refs_0_), channel_id=1, source_target_pairs={{0,48},{16,32},{32,16},{48,0},{64,112},{80,96},{96,80},{112,64},{1... | collective-permute-start | bytes 49160 | tf_op jit(solution)/shard_map/ppermute | solution.py:320
  75.7 4.1 %collective-permute-start.7 = (f32[16,256]{1,0:T(8,128)S(1)}, f32[16,256]{1,0:T(8,128)S(1)}, u32[]{:S(2)}, u32[]{:S(2)}) collective-permute-start(f32[16,256]{1,0:T(8,128)S(1)} %constant_dynamic-update-slice_fusion.refs_0_), channel_id=1, source_target_pairs={{0,64},{16,80},{32,96},{48,112},{64,0},{80,16},{96,32},{112,48},{1... | collective-permute-start | bytes 49160 | tf_op jit(solution)/shard_map/ppermute | solution.py:320
  76.3 12.4 %copy-start.16 = (f32[16,256]{1,0:T(8,128)}, f32[16,256]{1,0:T(8,128)S(1)}, u32[]{:S(2)}) copy-start(f32[16,256]{1,0:T(8,128)S(1)} %collective-permute-done.10.refs_7_) | copy-start | bytes 49156
  76.3 4.7 %collective-permute-start.8 = (f32[16,256]{1,0:T(8,128)S(1)}, f32[16,256]{1,0:T(8,128)S(1)}, u32[]{:S(2)}, u32[]{:S(2)}) collective-permute-start(f32[16,256]{1,0:T(8,128)S(1)} %constant_dynamic-update-slice_fusion.refs_0_), channel_id=1, source_target_pairs={{0,80},{16,64},{32,112},{48,96},{64,16},{80,0},{96,48},{112,32},{1... | collective-permute-start | bytes 49160 | tf_op jit(solution)/shard_map/ppermute | solution.py:320
  78.7 10.0 %copy-start.17 = (f32[16,256]{1,0:T(8,128)}, f32[16,256]{1,0:T(8,128)S(1)}, u32[]{:S(2)}) copy-start(f32[16,256]{1,0:T(8,128)S(1)} %collective-permute-done.4.refs_1_) | copy-start | bytes 49156
  78.7 3.8 %collective-permute-start.9 = (f32[16,256]{1,0:T(8,128)S(1)}, f32[16,256]{1,0:T(8,128)S(1)}, u32[]{:S(2)}, u32[]{:S(2)}) collective-permute-start(f32[16,256]{1,0:T(8,128)S(1)} %constant_dynamic-update-slice_fusion.refs_0_), channel_id=1, source_target_pairs={{0,96},{16,112},{32,64},{48,80},{64,32},{80,48},{96,0},{112,16},{1... | collective-permute-start | bytes 49160 | tf_op jit(solution)/shard_map/ppermute | solution.py:320
  79.3 9.4 %copy-start.18 = (f32[16,256]{1,0:T(8,128)}, f32[16,256]{1,0:T(8,128)S(1)}, u32[]{:S(2)}) copy-start(f32[16,256]{1,0:T(8,128)S(1)} %collective-permute-done.5.refs_2_) | copy-start | bytes 49156
  79.3 9.4 %copy-start.19 = (f32[16,256]{1,0:T(8,128)}, f32[16,256]{1,0:T(8,128)S(1)}, u32[]{:S(2)}) copy-start(f32[16,256]{1,0:T(8,128)S(1)} %collective-permute-done.6.refs_3_) | copy-start | bytes 49156
  79.8 8.9 %copy-start.20 = (f32[16,256]{1,0:T(8,128)}, f32[16,256]{1,0:T(8,128)S(1)}, u32[]{:S(2)}) copy-start(f32[16,256]{1,0:T(8,128)S(1)} %collective-permute-done.7.refs_4_) | copy-start | bytes 49156
  81.0 7.8 %copy-start.21 = (f32[16,256]{1,0:T(8,128)}, f32[16,256]{1,0:T(8,128)S(1)}, u32[]{:S(2)}) copy-start(f32[16,256]{1,0:T(8,128)S(1)} %collective-permute-done.8.refs_5_) | copy-start | bytes 49156
  82.5 6.2 %copy-start.22 = (f32[16,256]{1,0:T(8,128)}, f32[16,256]{1,0:T(8,128)S(1)}, u32[]{:S(2)}) copy-start(f32[16,256]{1,0:T(8,128)S(1)} %collective-permute-done.9.refs_6_) | copy-start | bytes 49156
  82.5 8.0 %copy-start.2 = (bf16[8,8,8,1440]{3,2,1,0:T(8,128)(2,1)}, bf16[8,8,8,1440]{3,2,1,0:T(8,128)(2,1)S(1)}, u32[]{:S(2)}) copy-start(bf16[8,8,8,1440]{3,2,1,0:T(8,128)(2,1)S(1)} %all-to-all-done) | copy-start | bytes 4423684
  82.5 33.6 %all-to-all-start.1 = ((bf16[8,8,8,1440]{3,2,1,0:T(8,128)(2,1)}), bf16[8,8,8,1440]{3,2,1,0:T(8,128)(2,1)S(1)}, u32[]{:S(2)}, u32[]{:S(2)}) async-start(bf16[8,8,8,1440]{3,2,1,0:T(8,128)(2,1)} %get-tuple-element.42), calls=%async_computation.1 | async-start | bytes 3145728 | tf_op jit(solution)/shard_map/all_to_all | solution.py:347
  90.6 4.5 %collective-permute-start.11 = (f32[136,128]{1,0:T(8,128)}, f32[136,128]{1,0:T(8,128)S(1)}, u32[]{:S(2)}, u32[]{:S(2)}) collective-permute-start(f32[136,128]{1,0:T(8,128)} %shard_map.114), channel_id=1, source_target_pairs={{0,1},{1,0},{2,3},{3,2},{4,5},{5,4},{6,7},{7,6},{8,9},{9,8},{10,11... | collective-permute-start | bytes 208904 | tf_op jit(solution)/shard_map/ppermute | solution.py:320
  91.6 7.4 %collective-permute-start.12 = (f32[136,128]{1,0:T(8,128)}, f32[136,128]{1,0:T(8,128)S(1)}, u32[]{:S(2)}, u32[]{:S(2)}) collective-permute-start(f32[136,128]{1,0:T(8,128)} %shard_map.114), channel_id=1, source_target_pairs={{0,2},{1,3},{2,0},{3,1},{4,6},{5,7},{6,4},{7,5},{8,10},{9,11},{10,... | collective-permute-start | bytes 208904 | tf_op jit(solution)/shard_map/ppermute | solution.py:320
  95.0 5.2 %collective-permute-start.13 = (f32[136,128]{1,0:T(8,128)}, f32[136,128]{1,0:T(8,128)S(1)}, u32[]{:S(2)}, u32[]{:S(2)}) collective-permute-start(f32[136,128]{1,0:T(8,128)} %shard_map.114), channel_id=1, source_target_pairs={{0,3},{1,2},{2,1},{3,0},{4,7},{5,6},{6,5},{7,4},{8,11},{9,10},{10,... | collective-permute-start | bytes 208904 | tf_op jit(solution)/shard_map/ppermute | solution.py:320
  101.1 8.7 %copy-start.5 = (f32[136,128]{1,0:T(8,128)}, f32[136,128]{1,0:T(8,128)S(1)}, u32[]{:S(2)}) copy-start(f32[136,128]{1,0:T(8,128)S(1)} %add_add_fusion.a_ref) | copy-start | bytes 208900
  101.1 4.0 %collective-permute-start.14 = (f32[136,128]{1,0:T(8,128)S(1)}, f32[136,128]{1,0:T(8,128)S(1)}, u32[]{:S(2)}, u32[]{:S(2)}) collective-permute-start(f32[136,128]{1,0:T(8,128)S(1)} %add_add_fusion.a_ref), channel_id=1, source_target_pairs={{0,4},{1,5},{2,6},{3,7},{4,0},{5,1},{6,2},{7,3},{8,12},{9,13},{10,... | collective-permute-start | bytes 208904 | tf_op jit(solution)/shard_map/ppermute | solution.py:320
  102.5 5.2 %collective-permute-start.15 = (f32[136,128]{1,0:T(8,128)S(1)}, f32[136,128]{1,0:T(8,128)S(1)}, u32[]{:S(2)}, u32[]{:S(2)}) collective-permute-start(f32[136,128]{1,0:T(8,128)S(1)} %add_add_fusion.a_ref), channel_id=1, source_target_pairs={{0,8},{1,9},{2,10},{3,11},{4,12},{5,13},{6,14},{7,15},{8,0},{9,1},... | collective-permute-start | bytes 208904 | tf_op jit(solution)/shard_map/ppermute | solution.py:320
  104.9 4.9 %collective-permute-start.16 = (f32[136,128]{1,0:T(8,128)S(1)}, f32[136,128]{1,0:T(8,128)S(1)}, u32[]{:S(2)}, u32[]{:S(2)}) collective-permute-start(f32[136,128]{1,0:T(8,128)S(1)} %add_add_fusion.a_ref), channel_id=1, source_target_pairs={{0,12},{1,13},{2,14},{3,15},{4,8},{5,9},{6,10},{7,11},{8,4},{9,5},... | collective-permute-start | bytes 208904 | tf_op jit(solution)/shard_map/ppermute | solution.py:320
  105.2 4.7 %copy-start.13 = (f32[136,128]{1,0:T(8,128)}, f32[136,128]{1,0:T(8,128)S(1)}, u32[]{:S(2)}) copy-start(f32[136,128]{1,0:T(8,128)S(1)} %collective-permute-done.14.b_ref) | copy-start | bytes 208900
  107.7 2.2 %copy-start.14 = (f32[136,128]{1,0:T(8,128)}, f32[136,128]{1,0:T(8,128)S(1)}, u32[]{:S(2)}) copy-start(f32[136,128]{1,0:T(8,128)S(1)} %collective-permute-done.15.c_ref) | copy-start | bytes 208900
  109.9 0.6 copy-start.15
  116.1 1.2 copy-start.3

commit v5 on v4

v5 whole, which is shorter than its diff:
```python
import functools
import math

import jax
import jax.numpy as jnp
from jax import lax
from jax.experimental import pallas as pl
from jax.experimental.pallas import tpu as pltpu
from jax.sharding import PartitionSpec as P

FIELDS = 16
HID = 128
ROWS = 4
LON = 1440
RING = 1536
SLOTS = 256
GROUP = 16
PLANES = ROWS * FIELDS
CHUNKS = 2
STEP = 4
N_ENS = 8
MEMBERS = 128
VMEM_LIMIT = 56 * 1024 * 1024


def prepare_kernel(
    tile_ref,
    first_ref,
    bias_in_ref,
    second_ref,
    bias_out_ref,
    index_ref,
    top_ref,
    bottom_ref,
    low_ref,
    middle_ref,
    high_ref,
    bias_ref,
    picks_ref,
    plane_ref,
    *,
    tiles,
):
    tap = lambda ref, row, column: ref[(3 * row + column) * 16 : (3 * row + column + 1) * 16]
    half = bias_in_ref[...] * 0.5
    high = half.astype(jnp.bfloat16).astype(jnp.float32)
    middle = (half - high).astype(jnp.bfloat16).astype(jnp.float32)
    low = half - high - middle
    zeros = jnp.zeros((16, HID), jnp.float32)
    bias = jnp.concatenate([high, middle, low, zeros[:13]], axis=0)
    parts = []
    for r in range(3):
        pieces = []
        for column in range(3):
            for row in range(5):
                known = 0 <= row - r <= 2
                piece = tap(first_ref, row - r, column).astype(jnp.float32) if known else zeros
                pieces.append(piece * 0.5)
        parts.append(jnp.concatenate(pieces + [bias], axis=0).T)
    tile = tile_ref[0]
    inner_top = jnp.where(tile > 0, 1.0, 0.0)
    inner_bottom = jnp.where(tile < tiles - 1, 1.0, 0.0)
    top = jnp.concatenate([parts[0] * inner_top, parts[1], parts[2]], axis=0)
    bottom = jnp.concatenate([parts[0], parts[1], parts[2] * inner_bottom], axis=0)
    top_ref[...] = top.astype(jnp.bfloat16)
    bottom_ref[...] = bottom.astype(jnp.bfloat16)

    rows = 6 * FIELDS
    to = lax.broadcasted_iota(jnp.int32, (rows, rows), 0)
    source = to // 32 * 32 + to % 2 * 16 + to % 32 // 2
    turn = (source == lax.broadcasted_iota(jnp.int32, (rows, rows), 1)).astype(jnp.bfloat16)

    def placed(taps):
        blank = jnp.zeros((16, HID), jnp.bfloat16)
        lines = []
        for column in range(3):
            for line in taps:
                cells = [blank if d is None else tap(second_ref, d, column) for d in line]
                lines.append(jnp.concatenate(cells, axis=1))
        whole = jnp.concatenate(lines, axis=0)
        return jnp.dot(turn, whole, preferred_element_type=jnp.float32).astype(jnp.bfloat16)

    upper = placed(((0, 1), (None, 0)))
    lower = placed(((2, None), (1, 2)))
    low_ref[...] = upper
    middle_ref[...] = jnp.concatenate([lower, upper], axis=0)
    high_ref[...] = lower

    group = 16 * FIELDS
    field = lax.broadcasted_iota(jnp.int32, (group, FIELDS), 0) // 16
    mine = field == lax.broadcasted_iota(jnp.int32, (group, FIELDS), 1)
    bias_ref[...] = jnp.sum(jnp.where(mine, bias_out_ref[...], 0.0), axis=1, keepdims=True)

    entry = index_ref[...]
    bound = (lax.broadcasted_iota(jnp.int32, (PLANES, SLOTS), 0) + 1) * LON
    plane = jnp.sum(jnp.where(entry >= bound, 1, 0), axis=0, keepdims=True)
    plane_ref[...] = plane
    column = entry - plane * LON
    for at in range(0, RING, 256):
        place = lax.broadcasted_iota(jnp.int32, (256, SLOTS), 0) + at
        picks_ref[at : at + 256, :] = jnp.where(place == column, 1.0, 0.0).astype(jnp.bfloat16)


def prepare(tile, tiles, conv_in, bias_in, conv_out, bias_out, index):
    vmem = pl.BlockSpec(memory_space=pltpu.VMEM)
    shape = jax.ShapeDtypeStruct
    return pl.pallas_call(
        functools.partial(prepare_kernel, tiles=tiles),
        in_specs=[pl.BlockSpec(memory_space=pltpu.SMEM)] + [vmem] * 5,
        out_specs=[vmem] * 8,
        out_shape=[
            shape((3 * HID, 256), jnp.bfloat16),
            shape((3 * HID, 256), jnp.bfloat16),
            shape((6 * FIELDS, 2 * HID), jnp.bfloat16),
            shape((12 * FIELDS, 2 * HID), jnp.bfloat16),
            shape((6 * FIELDS, 2 * HID), jnp.bfloat16),
            shape((16 * FIELDS, 1), jnp.float32),
            shape((RING, SLOTS), jnp.bfloat16),
            shape((1, SLOTS), jnp.int32),
        ],
        cost_estimate=cost(3),
    )(
        tile.astype(jnp.int32).reshape(1),
        jnp.transpose(conv_in, (2, 3, 1, 0)).reshape(9 * FIELDS, HID),
        bias_in.reshape(1, HID),
        jnp.transpose(conv_out, (2, 3, 0, 1)).reshape(9 * FIELDS, HID),
        bias_out.reshape(1, FIELDS),
        index.reshape(1, SLOTS),
    )


def forecast_kernel(
    x_ref,
    base_ref,
    top_ref,
    bottom_ref,
    first_top_ref,
    first_bottom_ref,
    low_ref,
    middle_ref,
    high_ref,
    bias_ref,
    picks_ref,
    plane_ref,
    earlier_ref,
    fields_ref,
    observed_ref,
    held_ref,
):
    step = pl.program_id(0)
    ones = jnp.ones((16, RING), jnp.bfloat16)
    part = PLANES // 2

    def changes(member):
        stack = jnp.concatenate(
            [
                top_ref[member].reshape(2 * FIELDS, LON),
                x_ref[member].reshape(PLANES, LON),
                bottom_ref[member].reshape(2 * FIELDS, LON),
            ],
            axis=0,
        )
        ring = jnp.concatenate([stack, stack[:, :64], stack[:, LON - 32 :]], axis=1)
        left = pltpu.roll(ring, 1, 1)
        right = pltpu.roll(ring, RING - 1, 1)

        def hidden_rows(at, weights_ref):
            to = at + 5 * FIELDS
            taps = jnp.concatenate([left[at:to], ring[at:to], right[at:to], ones], axis=0)
            half = jnp.dot(weights_ref[...], taps, preferred_element_type=jnp.float32)
            return (half * jnp.tanh(half) + half).astype(jnp.bfloat16)

        hidden = jnp.concatenate(
            [hidden_rows(0, first_top_ref), hidden_rows(3 * FIELDS, first_bottom_ref)], axis=0
        )

        def outer(weights_ref, pair):
            rows = hidden[2 * HID * pair : 2 * HID * (pair + 1)]
            return jnp.dot(weights_ref[...], rows, preferred_element_type=jnp.float32)

        both = outer(middle_ref, 1)
        for taps in (both[: 3 * part] + outer(low_ref, 0), both[3 * part :] + outer(high_ref, 2)):
            yield (
                pltpu.roll(taps[:part], 1, 1)
                + taps[part : 2 * part]
                + pltpu.roll(taps[2 * part :], RING - 1, 1)
            )

    sub = lax.broadcasted_iota(jnp.int32, (8, RING), 0)
    pairs = []
    for pair in range(STEP // 2):
        sources = [*changes(2 * pair), *changes(2 * pair + 1)]
        blocks = []
        for field in range(FIELDS):
            at, by = field // 4 * 8, field % 4 * 2
            moved = [
                pltpu.roll(source[at : at + 8], (2 * k - by) % 8, 0) if (2 * k - by) % 8 else source[at : at + 8]
                for k, source in enumerate(sources)
            ]
            first = jnp.where(sub < 2, moved[0], moved[1])
            last = jnp.where(sub < 6, moved[2], moved[3])
            blocks.append(jnp.where(sub < 4, first, last))
        pairs.append(blocks)
    for field in range(FIELDS):
        low, high = field * 16, field * 16 + 16
        base = base_ref[0, low:high, :].astype(jnp.float32) + bias_ref[low:high, :]
        base = jnp.concatenate([base, base[:, : RING - LON]], axis=1)
        change = jnp.concatenate([blocks[field] for blocks in pairs], axis=0)
        own = (base + change).astype(jnp.bfloat16)
        fields_ref[field // 2, field % 2] = own[:, :LON]
        held_ref[pl.ds(pl.multiple_of(step * 16 * FIELDS + low, 16), 16), :] = own

    @pl.when(step == pl.num_programs(0) - 1)
    def _():
        rows = held_ref.shape[0]
        picked = jnp.dot(held_ref[...], picks_ref[...], preferred_element_type=jnp.float32)
        row = lax.broadcasted_iota(jnp.int32, (rows, SLOTS), 0)
        here = row % 256 // 16 * ROWS + row % ROWS == plane_ref[...]
        found = jnp.where(here, picked, 0.0).astype(jnp.bfloat16)
        count = rows // PLANES
        column = lax.broadcasted_iota(jnp.int32, (count, rows), 1)
        member = column // 256 * STEP + column % 16 // ROWS
        mine = member == lax.broadcasted_iota(jnp.int32, (count, rows), 0)
        seen = jnp.dot(
            mine.astype(jnp.bfloat16), found, preferred_element_type=jnp.float32
        )
        if earlier_ref is not None:
            seen = jnp.concatenate([earlier_ref[...], seen], axis=0)
        observed_ref[...] = seen


def cost(microseconds):
    return pl.CostEstimate(
        flops=int(microseconds * 1e9), transcendentals=0, bytes_accessed=int(microseconds * 1e6)
    )


def forecast(start, own, base, top, bottom, shared, earlier):
    count = top.shape[0]
    steps = count // STEP
    first = start // STEP
    whole = lambda array: pl.BlockSpec(array.shape, lambda m: (0,) * array.ndim)
    kernel = forecast_kernel
    if earlier is None:
        kernel = lambda *refs: forecast_kernel(*refs[:-3], None, *refs[-3:])
        seen = count
    else:
        shared = [*shared, earlier]
        seen = count + earlier.shape[0]
    return pl.pallas_call(
        kernel,
        grid=(steps,),
        in_specs=[
            pl.BlockSpec((STEP, ROWS, FIELDS, LON), lambda m: (first + m, 0, 0, 0)),
            pl.BlockSpec((1, 16 * FIELDS, LON), lambda m: (first + m, 0, 0)),
            pl.BlockSpec((STEP, 2, FIELDS, LON), lambda m: (m, 0, 0, 0)),
            pl.BlockSpec((STEP, 2, FIELDS, LON), lambda m: (m, 0, 0, 0)),
        ]
        + [whole(array) for array in shared],
        out_specs=[
            pl.BlockSpec((N_ENS, 2, 16, LON), lambda m: (0, 0, m, 0)),
            pl.BlockSpec((seen, SLOTS), lambda m: (0, 0)),
        ],
        out_shape=[
            jax.ShapeDtypeStruct((N_ENS, 2, count * ROWS, LON), jnp.bfloat16),
            jax.ShapeDtypeStruct((seen, SLOTS), jnp.float32),
        ],
        scratch_shapes=[pltpu.VMEM((count * PLANES, RING), jnp.bfloat16)],
        cost_estimate=cost(2 * count),
        compiler_params=pltpu.CompilerParams(vmem_limit_bytes=VMEM_LIMIT),
    )(own, base, top, bottom, *shared)


def products_kernel(place_ref, count_ref, value_ref, sigma_ref, *refs):
    pieces, out_ref, held_ref = refs[:N_ENS], refs[N_ENS], refs[N_ENS + 1]
    for step, piece in enumerate(pieces):
        at = pl.multiple_of((place_ref[0] ^ step) * GROUP, GROUP)
        held_ref[pl.ds(at, GROUP), :] = piece[...]
    observed = held_ref[...]
    mean = jnp.sum(observed, axis=0, keepdims=True) / MEMBERS
    slot = lax.broadcasted_iota(jnp.int32, (1, SLOTS), 1)
    live = (slot < count_ref[0]).astype(jnp.float32)
    sigma = sigma_ref[...]
    anomalies = (observed - mean) * (live / (sigma * math.sqrt(MEMBERS - 1)))
    innov = live * (value_ref[...] - mean) / sigma
    left = jnp.concatenate([anomalies, jnp.broadcast_to(innov, (8, SLOTS))], axis=0)
    out_ref[...] = lax.dot_general(
        left,
        anomalies,
        (((1,), (1,)), ((), ())),
        precision=lax.Precision.HIGHEST,
        preferred_element_type=jnp.float32,
    )


def products(pieces, places, count, value, sigma):
    vmem = pl.BlockSpec(memory_space=pltpu.VMEM)
    smem = pl.BlockSpec(memory_space=pltpu.SMEM)
    return pl.pallas_call(
        products_kernel,
        in_specs=[smem, smem] + [vmem] * (2 + N_ENS),
        out_specs=vmem,
        out_shape=jax.ShapeDtypeStruct((MEMBERS + 8, MEMBERS), jnp.float32),
        cost_estimate=cost(1),
        scratch_shapes=[pltpu.VMEM((MEMBERS, SLOTS), jnp.float32)],
    )(places, count, value.reshape(1, SLOTS), sigma.reshape(1, SLOTS), *pieces)


def transform_kernel(a_ref, b_ref, c_ref, d_ref, factor_ref, weights_ref, transform_ref):
    n = MEMBERS
    total = (a_ref[...] + b_ref[...]) + (c_ref[...] + d_ref[...])
    row = lax.broadcasted_iota(jnp.int32, (n, n), 0)
    column = lax.broadcasted_iota(jnp.int32, (n, n), 1)
    eye = (row == column).astype(jnp.float32)
    gram = total[0:n] + eye
    blocks = [[gram[b : b + 8], eye[b : b + 8]] for b in range(0, n, 8)]
    within = lax.broadcasted_iota(jnp.int32, (8, n), 0)
    wide = lambda value: jnp.broadcast_to(value, (8, n))
    for b in range(n // 8):
        upper, inverse = blocks[b]
        columns = [wide(upper[:, 8 * b + k : 8 * b + k + 1]) for k in range(8)]
        scales, steps, rows = [], [], []
        for k in range(8):
            scale = lax.rsqrt(wide(columns[k][k : k + 1]))
            share = columns[k] * scale
            step = {}
            for later in range(k + 1, 8):
                step[later] = wide(share[later : later + 1])
                columns[later] = columns[later] - share * step[later]
            upper_row = wide(upper[k : k + 1]) * scale
            inverse_row = wide(inverse[k : k + 1]) * scale
            share = jnp.where(within > k, share, 0.0)
            upper = jnp.where(within == k, upper_row, upper - share * upper_row)
            inverse = jnp.where(within == k, inverse_row, inverse - share * inverse_row)
            scales.append(scale)
            steps.append(step)
            rows.append((upper_row, inverse_row))
        for t in range(b + 1, n // 8):
            later_upper, later_inverse = blocks[t]
            columns = [wide(later_upper[:, 8 * b + k : 8 * b + k + 1]) for k in range(8)]
            for k in range(8):
                share = columns[k] * scales[k]
                for later in range(k + 1, 8):
                    columns[later] = columns[later] - share * steps[k][later]
                later_upper = later_upper - share * rows[k][0]
                later_inverse = later_inverse - share * rows[k][1]
            blocks[t] = [later_upper, later_inverse]
        blocks[b] = [upper, inverse]
    upper = jnp.concatenate([pair[0] for pair in blocks], axis=0)
    inverse = jnp.concatenate([pair[1] for pair in blocks], axis=0)
    factor_ref[...] = jnp.where(row <= column, upper, 0.0).T
    proj = total[n : n + 1]
    middle = jnp.sum(inverse * proj, axis=1, keepdims=True)
    weights = jnp.sum(inverse * middle, axis=0, keepdims=True) / math.sqrt(n - 1)
    weights_ref[...] = weights
    coeff = inverse + weights
    transform = coeff - jnp.mean(coeff, axis=1, keepdims=True) + 1.0 / n
    transform_ref[...] = transform.astype(jnp.bfloat16)


def transform_of(parts):
    vmem = pl.BlockSpec(memory_space=pltpu.VMEM)
    return pl.pallas_call(
        transform_kernel,
        in_specs=[vmem] * 4,
        out_specs=[vmem, vmem, vmem],
        out_shape=[
            jax.ShapeDtypeStruct((MEMBERS, MEMBERS), jnp.float32),
            jax.ShapeDtypeStruct((1, MEMBERS), jnp.float32),
            jax.ShapeDtypeStruct((MEMBERS, MEMBERS), jnp.bfloat16),
        ],
        cost_estimate=cost(1),
    )(*parts)


def update_kernel(transform_ref, early_ref, late_ref, out_ref, spread_ref):
    rows = MEMBERS * ROWS
    half = rows // 2

    @pl.when((pl.program_id(0) == 0) & (pl.program_id(1) == 0))
    def _():
        shape = (rows, MEMBERS)
        row = lax.broadcasted_iota(jnp.int32, shape, 0)
        column = lax.broadcasted_iota(jnp.int32, shape, 1)
        held = row % half // 32 * GROUP + row // half * 8 + row % 32 // ROWS
        repeat = (row // ROWS == column).astype(jnp.bfloat16)
        placed = (held == column).astype(jnp.bfloat16)
        tall = jnp.dot(repeat, transform_ref[...], preferred_element_type=jnp.float32)
        wide = lax.dot_general(
            tall.astype(jnp.bfloat16),
            placed,
            (((1,), (1,)), ((), ())),
            preferred_element_type=jnp.float32,
        )
        own = lax.broadcasted_iota(jnp.int32, (rows, rows), 0) % ROWS
        same = own == lax.broadcasted_iota(jnp.int32, (rows, rows), 1) % ROWS
        spread_ref[...] = jnp.where(same, wide, 0.0).astype(jnp.bfloat16)

    width = early_ref.shape[-1]
    fields = jnp.concatenate(
        [early_ref[:, 0].reshape(half, width), late_ref[:, 0].reshape(half, width)], axis=0
    )
    mixed = jnp.dot(spread_ref[...], fields, preferred_element_type=jnp.float32)
    out_ref[:, 0] = mixed.astype(jnp.bfloat16).reshape(N_ENS, GROUP * ROWS, width)


def update(transform, early, late):
    rows = MEMBERS * ROWS
    half = pl.BlockSpec((N_ENS, 1, 8 * ROWS, RING // 2), lambda c, x: (0, c, 0, x))
    return pl.pallas_call(
        update_kernel,
        grid=(2, 2),
        in_specs=[pl.BlockSpec((MEMBERS, MEMBERS), lambda c, x: (0, 0)), half, half],
        out_specs=pl.BlockSpec(
            (N_ENS, 1, GROUP * ROWS, RING // 2), lambda c, x: (0, c, 0, x)
        ),
        out_shape=jax.ShapeDtypeStruct((N_ENS, 2, GROUP * ROWS, LON), jnp.bfloat16),
        scratch_shapes=[pltpu.VMEM((rows, rows), jnp.bfloat16)],
        cost_estimate=cost(4),
        compiler_params=pltpu.CompilerParams(vmem_limit_bytes=VMEM_LIMIT),
    )(transform, early, late)


def on_device(
    ensemble_weather,
    conv_in,
    bias_in,
    conv_out,
    bias_out,
    observed_entry_index,
    obs_count,
    obs_value,
    obs_sigma,
):
    tiles = lax.axis_size("map")
    tile = lax.axis_index("map")
    own_place = lax.axis_index("ens")
    down = [(i, i + 1) for i in range(tiles - 1)]
    up = [(i + 1, i) for i in range(tiles - 1)]

    def swap(value, axis, step):
        pairs = [(i, i ^ step) for i in range(lax.axis_size(axis))]
        return lax.ppermute(value, axis, pairs)

    share = GROUP // CHUNKS
    exchange = lambda value: lax.all_to_all(
        value, "ens", split_axis=0, concat_axis=0, tiled=True
    )
    own = jnp.transpose(ensemble_weather, (0, 2, 1, 3))

    def edges(chunk):
        part = own[chunk * share : (chunk + 1) * share]
        return part[:, ROWS - 2 :], part[:, :2]

    def halo(rows):
        return lax.ppermute(rows[0], "map", down), lax.ppermute(rows[1], "map", up)

    halos = [halo(edges(0))]
    shared = prepare(
        tile, tiles, conv_in, bias_in, conv_out, bias_out, observed_entry_index
    )
    next_edges, shared = lax.optimization_barrier((edges(1), shared))
    halos.append(halo(next_edges))
    base = jnp.transpose(
        ensemble_weather.reshape(GROUP // STEP, STEP, FIELDS, ROWS, LON), (0, 2, 1, 3, 4)
    ).reshape(GROUP // STEP, STEP * PLANES, LON)
    fields, observed = [], None
    for chunk, (top, bottom) in enumerate(halos):
        moved, observed = forecast(chunk * share, own, base, top, bottom, shared, observed)
        fields.append(moved)
    early = exchange(fields[0])
    pieces = [observed] + [swap(observed, "ens", step) for step in range(1, N_ENS)]
    places = own_place.astype(jnp.int32).reshape(1)
    pieces, late, early = lax.optimization_barrier((pieces, fields[1], early))
    late = exchange(late)
    part = products(pieces, places, obs_count, obs_value, obs_sigma)
    near = [part] + [swap(part, "map", step) for step in (1, 2, 3)]
    row = (near[0] + near[1]) + (near[2] + near[3])
    factor, mean_weights, transform = transform_of(
        [row] + [swap(row, "map", step) for step in (4, 8, 12)]
    )
    back = exchange(update(transform, early, late))
    back = back.reshape(N_ENS, 2, GROUP, ROWS, LON)
    analysis = jnp.transpose(back, (2, 0, 1, 3, 4)).reshape(GROUP, FIELDS, ROWS, LON)
    return (analysis, factor, mean_weights.reshape(MEMBERS))


def solution(mesh):
    placed = (
        P("ens", None, "map", None),
        P(),
        P(),
        P(),
        P(),
        P("map"),
        P("map"),
        P("map"),
        P("map"),
    )
    return jax.shard_map(
        on_device,
        mesh=mesh,
        in_specs=placed,
        out_specs=(P("ens", None, "map", None), P(), P()),
        check_vma=False,
    )
```

time: 175 us -> 174 us (level)
  starting transfers between devices: 42.2 us -> 46.5 us
  other arithmetic: 4.92 us -> 0.9 us
    ppermute x13, starting transfers between devices: 17.1 us -> 21.5 us  [swap(): return lax.ppermute(value, axis, pairs)]
    transpose x1, local copies, waits for them, and re-layouts: 1.28 us -> 5 us  [on_device(): jnp.transpose(back, (2, 0, 1, 3, 4)).reshape(GROUP, FIELDS, ROWS, LON)]
    slice x3 -> x1, local copies, waits for them, and re-layouts: 5.31 us -> 1.91 us  [edges(): return (part[:, ROWS - 2:], part[:, :2])]
    ppermute x13, waiting for transfers between devices: 13.1 us -> 9.87 us  [swap(): return lax.ppermute(value, axis, pairs)]
    unnamed x49 -> x31, local copies, waits for them, and re-layouts: 3.9 us -> 5.82 us
    reshape x5 -> x3, local copies, waits for them, and re-layouts: 7.25 us -> 8.71 us  [the longest x1 4.05 us: on_device(): ensemble_weather.reshape(GROUP // STEP, STEP, FIELDS, ROWS, LON)]
    pallas_call x3 -> x4, Pallas kernels: 38.4 us -> 38.7 us  [the longest x2 30.7 us: forecast(): pl.pallas_call(kernel, grid=(steps,), in_specs=[pl.BlockSpec((STEP, ROWS,...]
  transfers between devices with their start and end apart: 19 -> 19, of which waited for: 7 -> 8; matrix products, arithmetic and copies ran while one was open for 9% -> 4% of each run, Pallas kernels for 22% -> 23%
where the time goes in v5:
time: 174 us; the launch traced here: 173 us
  starting transfers between devices  46.5 us (27%)
  Pallas kernels  46.2 us (27%)
  blocking collectives  44.9 us (26%)
  local copies, waits for them, and re-layouts  21.4 us (12%)
  waiting for transfers between devices  12 us (7%)
    all_to_all x1, blocking collectives, on_device(): lax.all_to_all(value, 'ens', split_axis=0, concat_axis=0, tiled=True)  44.9 us
    pallas_call x2, Pallas kernels, forecast(): pl.pallas_call(kernel, grid=(steps,), in_specs=[pl.BlockSpec((STEP, ROWS,...  30.7 us
    ppermute x13, starting transfers between devices, swap(): return lax.ppermute(value, axis, pairs)  21.5 us
    all_to_all x2, starting transfers between devices, on_device(): lax.all_to_all(value, 'ens', split_axis=0, concat_axis=0, tiled=True)  13 us
    ppermute x13, waiting for transfers between devices, swap(): return lax.ppermute(value, axis, pairs)  9.87 us
    ppermute x2, starting transfers between devices, halo(): lax.ppermute(rows[0], 'map', down)  9.45 us
    unnamed x31, local copies, waits for them, and re-layouts  5.82 us
    pallas_call x1, Pallas kernels, transform_of(): pl.pallas_call(transform_kernel, in_specs=[vmem] * 4, out_specs=[vmem, vm...  5.67 us
  transfers between devices with their start and end apart: 19, of which 8 were waited for; matrix products, arithmetic and copies ran while one was open for 4% of the time, Pallas kernels for 23%

profile of v5, /device:TPU:1, one launch (start us, length us, event | category | flops | bytes accessed | tf_op | source)
XLA Modules:
  0.0 173.4 jit_solution(4974541681625702573)
XLA Ops:
  0.6 2.7 %copy.21 = bf16[16,16,4,1440]{3,1,2,0:T(8,128)(2,1)S(1)} copy(bf16[16,16,4,1440]{3,2,1,0:T(4,128)(2,1)} %param.9) | data formatting | bytes 5898240 | tf_op args[0]
  3.3 0.0 copy-start.1
  3.3 1.9 %fusion = (bf16[8,2,16,1440]{3,2,1,0:T(8,128)(2,1)}, bf16[8,2,16,1440]{3,2,1,0:T(8,128)(2,1)}, bf16[8,2,16,1440]{3,2,1,0:T(8,128)(2,1)}, bf16[8,2,16,1440]{3,2,1,0:T(8,128)(2,1)}) fusion(bf16[16,4,16,1440]{3,2,1,0:T(8,128)(2,1)S(1)} %bitcast.26), kind=kLoop, calls=%fused_computation.2 | loop fusion | bytes 5898240 | tf_op jit(solution)/shard_map/slice | solution.py:453
  5.2 0.7 copy-done.1
  6.0 1.3 collective-permute-start.3
  7.2 5.9 %collective-permute-start.2 = (bf16[8,2,16,1440]{3,2,1,0:T(8,128)(2,1)}, bf16[8,2,16,1440]{3,2,1,0:T(8,128)(2,1)}, u32[]{:S(2)}, u32[]{:S(2)}) collective-permute-start(bf16[8,2,16,1440]{3,2,1,0:T(8,128)(2,1)} %get-tuple-element.74), channel_id=1, source_target_pairs={{0,1},{1,2},{2,3},{3,4},{4,5},{5,6},{6,7},{7,8},{8,9},{9,10},{10,1... | collective-permute-start | bytes 2211848 | tf_op jit(solution)/shard_map/ppermute | solution.py:456
  13.1 2.4 %shard_map.112 = (bf16[384,256]{1,0:T(8,128)(2,1)}, bf16[384,256]{1,0:T(8,128)(2,1)}, bf16[96,256]{1,0:T(8,128)(2,1)}, bf16[192,256]{1,0:T(8,128)(2,1)}, bf16[96...) custom-call(s32[1]{0:T(128)} %bitcast.7.tile_ref, ...), custom_call_target="tpu_custom_call" | custom-call | flops 3000000000 | bytes 3000000 | tf_op jit(solution)/shard_map/pallas_call | solution.py:107
  15.5 3.6 %collective-permute-start = (bf16[8,2,16,1440]{3,2,1,0:T(8,128)(2,1)}, bf16[8,2,16,1440]{3,2,1,0:T(8,128)(2,1)}, u32[]{:S(2)}, u32[]{:S(2)}) collective-permute-start(bf16[8,2,16,1440]{3,2,1,0:T(8,128)(2,1)} %get-tuple-element.46), channel_id=1, source_target_pairs={{0,1},{1,2},{2,3},{3,4},{4,5},{5,6},{6,7},{7,8},{8,9},{9,10},{10,1... | collective-permute-start | bytes 2211848 | tf_op jit(solution)/shard_map/ppermute | solution.py:456
  19.1 1.3 collective-permute-start.1
  20.4 4.0 %copy.16 = bf16[4,4,16,4,1440]{4,0,3,1,2:T(4,128)(2,1)S(1)} copy(bf16[4,4,16,4,1440]{4,3,2,1,0:T(4,128)(2,1)S(1)} %bitcast.25) | data formatting | bytes 5898240 | tf_op jit(solution)/shard_map/reshape | solution.py:465
  24.5 2.2 %copy.18.refs_1_.base_ref = bf16[4,256,1440]{2,1,0:T(8,128)(2,1)} copy(bf16[4,256,1440]{2,0,1:T(4,128)(2,1)S(1)} %bitcast.30) | data formatting | bytes 5898240 | tf_op jit(solution)/shard_map/reshape | solution.py:466
  26.7 1.2 collective-permute-done.3.refs_3_
  27.9 0.9 collective-permute-done.2.refs_2_
  28.7 15.3 %shard_map.113 = (bf16[8,2,32,1440]{3,2,1,0:T(8,128)(2,1)}, f32[8,256]{1,0:T(8,128)}) custom-call(bf16[16,4,16,1440]{3,2,1,0:T(8,128)(2,1)} %bitcast.27, bf16[4,256,1440]{2,1,0:T(8,128)(2,1)} %copy.18.refs_1_.base_ref, bf16[8,2,16,1440]{3,2,1,0:T(8,128)(2,1)} %collective-permute-done.2.refs_2_, bf16[8,2,16,1440]{3,2,1,0:T(8,128)(2,1)} %collective-permute-done.3.refs_3_, ...), custom_call_target="tpu_custom_call" | custom-call | flops 16000000000 | bytes 16000000 | tf_op jit(solution)/shard_map/pallas_call | solution.py:250
  44.1 7.1 %all-to-all-start = ((bf16[8,2,32,1440]{3,2,1,0:T(8,128)(2,1)}), bf16[8,2,32,1440]{3,2,1,0:T(8,128)(2,1)S(1)}, u32[]{:S(2)}, u32[]{:S(2)}) async-start(bf16[8,2,32,1440]{3,2,1,0:T(8,128)(2,1)} %get-tuple-element.59), calls=%async_computation | async-start | bytes 3145728 | tf_op jit(solution)/shard_map/all_to_all | solution.py:446
  51.2 0.0 collective-permute-done.top_ref
  51.2 0.0 collective-permute-done.1.bottom_ref
  51.2 15.4 %shard_map.114 = (bf16[8,2,32,1440]{3,2,1,0:T(8,128)(2,1)}, f32[16,256]{1,0:T(8,128)}) custom-call(bf16[16,4,16,1440]{3,2,1,0:T(8,128)(2,1)} %bitcast.28, bf16[4,256,1440]{2,1,0:T(8,128)(2,1)} %copy.18.refs_1_.base_ref, bf16[8,2,16,1440]{3,2,1,0:T(8,128)(2,1)} %collective-permute-done.top_ref, bf16[8,2,16,1440]{3,2,1,0:T(8,128)(2,1)} %collective-permute-done.1.bottom_ref, ...), custom_call_target="tpu_custom_call" | custom-call | flops 16000000000 | bytes 16000000 | tf_op jit(solution)/shard_map/pallas_call | solution.py:250
  66.5 2.9 %collective-permute-start.10 = (f32[16,256]{1,0:T(8,128)}, f32[16,256]{1,0:T(8,128)S(1)}, u32[]{:S(2)}, u32[]{:S(2)}) collective-permute-start(f32[16,256]{1,0:T(8,128)} %get-tuple-element.60.refs_0_), channel_id=1, source_target_pairs={{0,112},{16,96},{32,80},{48,64},{64,48},{80,32},{96,16},{112,0},{1... | collective-permute-start | bytes 49160 | tf_op jit(solution)/shard_map/ppermute | solution.py:443
  69.5 2.1 %collective-permute-start.8 = (f32[16,256]{1,0:T(8,128)}, f32[16,256]{1,0:T(8,128)S(1)}, u32[]{:S(2)}, u32[]{:S(2)}) collective-permute-start(f32[16,256]{1,0:T(8,128)} %get-tuple-element.60.refs_0_), channel_id=1, source_target_pairs={{0,80},{16,64},{32,112},{48,96},{64,16},{80,0},{96,48},{112,32},{1... | collective-permute-start | bytes 49160 | tf_op jit(solution)/shard_map/ppermute | solution.py:443
  71.5 1.3 collective-permute-start.7
  72.8 0.5 collective-permute-start.6
  73.3 1.1 collective-permute-start.5
  74.5 0.5 collective-permute-start.4
  75.0 0.9 collective-permute-done.7.refs_4_
  75.8 0.8 collective-permute-done.6.refs_3_
  76.6 0.0 copy-start.14
  76.7 5.9 %all-to-all-start.1 = ((bf16[8,2,32,1440]{3,2,1,0:T(8,128)(2,1)}), bf16[8,2,32,1440]{3,2,1,0:T(8,128)(2,1)S(1)}, u32[]{:S(2)}, u32[]{:S(2)}) async-start(bf16[8,2,32,1440]{3,2,1,0:T(8,128)(2,1)} %get-tuple-element.70), calls=%async_computation.1 | async-start | bytes 3145728 | tf_op jit(solution)/shard_map/all_to_all | solution.py:446
  83.3 1.8 %shard_map.115 = f32[136,128]{1,0:T(8,128)} custom-call(s32[1]{0:T(128)} %bitcast.place_ref, s32[1]{0:T(128)S(6)} %copy.22.count_ref, f32[1,256]{1,0:T(1,128)} %bitcast.35, f32[1,256]{1,0:T(1,128)} %bitcast.36, f32[16,256]{1,0:T(8,128)} %get-tuple-element.60.refs_0_, f32[16,256]{1,0:T(8,128)} %copy-done.14, f32[16,256]{1,0:T(8,128)} %copy-done.13, ...), custom_call_target="tpu_custom_call" | custom-call | flops 1000000000 | bytes 1000000 | tf_op jit(solution)/shard_map/pallas_call | solution.py:299
  85.1 5.9 %collective-permute-start.13 = (f32[136,128]{1,0:T(8,128)}, f32[136,128]{1,0:T(8,128)S(1)}, u32[]{:S(2)}, u32[]{:S(2)}) collective-permute-start(f32[136,128]{1,0:T(8,128)} %shard_map.115), channel_id=1, source_target_pairs={{0,3},{1,2},{2,1},{3,0},{4,7},{5,6},{6,5},{7,4},{8,11},{9,10},{10,... | collective-permute-start | bytes 208904 | tf_op jit(solution)/shard_map/ppermute | solution.py:443
  91.0 0.7 collective-permute-start.11
  91.7 2.6 %collective-permute-done.13 = f32[136,128]{1,0:T(8,128)S(1)} collective-permute-done((f32[136,128]{1,0:T(8,128)}, f32[136,128]{1,0:T(8,128)S(1)}, u32[]{:S(2)}, u32[]{:S(2)}) %collective-permute-start.13) | collective-permute-done | bytes 69664 | tf_op jit(solution)/shard_map/ppermute | solution.py:443
  94.2 1.6 collective-permute-done.12
  95.9 0.9 add_add_fusion.a_ref
  96.8 0.0 copy-start.4
  96.8 5.8 %collective-permute-start.16 = (f32[136,128]{1,0:T(8,128)S(1)}, f32[136,128]{1,0:T(8,128)S(1)}, u32[]{:S(2)}, u32[]{:S(2)}) collective-permute-start(f32[136,128]{1,0:T(8,128)S(1)} %add_add_fusion.a_ref), channel_id=1, source_target_pairs={{0,12},{1,13},{2,14},{3,15},{4,8},{5,9},{6,10},{7,11},{8,4},{9,5},... | collective-permute-start | bytes 208904 | tf_op jit(solution)/shard_map/ppermute | solution.py:443
  102.6 0.1 collective-permute-start.15
  102.7 0.6 collective-permute-start.14
  103.3 1.3 collective-permute-done.16.d_ref
  104.6 2.7 %collective-permute-done.15.c_ref = f32[136,128]{1,0:T(8,128)S(1)} collective-permute-done((f32[136,128]{1,0:T(8,128)S(1)}, f32[136,128]{1,0:T(8,128)S(1)}, u32[]{:S(2)}, u32[]{:S(2)}) %collective-permute-start.15) | collective-permute-done | bytes 69664 | tf_op jit(solution)/shard_map/ppermute | solution.py:443
  107.3 0.6 copy-done.6
  107.9 0.6 copy-done.7
  108.6 5.7 %shard_map.116 = (f32[128,128]{1,0:T(8,128)}, f32[1,128]{1,0:T(1,128)}, bf16[128,128]{1,0:T(8,128)(2,1)}) custom-call(f32[136,128]{1,0:T(8,128)} %copy-done.4, f32[136,128]{1,0:T(8,128)} %copy-done.7, f32[136,128]{1,0:T(8,128)} %copy-done.6, f32[136,128]{1,0:T(8,128)} %copy-done.5), custom_call_target="tpu_custom_call" | custom-call | flops 1000000000 | bytes 1000000 | tf_op jit(solution)/shard_map/pallas_call | solution.py:363
  114.2 1.1 copy-done.3
  115.4 5.7 %shard_map.117 = bf16[8,2,64,1440]{3,2,1,0:T(8,128)(2,1)} custom-call(bf16[128,128]{1,0:T(8,128)(2,1)} %get-tuple-element.68.transform_ref, bf16[8,2,32,1440]{3,2,1,0:T(8,128)(2,1)} %copy-done.2, bf16[8,2,32,1440]{3,2,1,0:T(8,128)(2,1)} %copy-done.3), custom_call_target="tpu_custom_call" | custom-call | flops 4000000000 | bytes 4000000 | tf_op jit(solution)/shard_map/pallas_call | solution.py:410
  121.0 44.9 %all_to_all.15 = bf16[8,2,64,1440]{3,2,1,0:T(8,128)(2,1)S(1)} all-to-all(bf16[8,2,64,1440]{3,2,1,0:T(8,128)(2,1)} %shard_map.117), channel_id=1, replica_groups=mesh['ens'=8,'map'=16] {'ens'}, dimensions={0} | all-to-all | bytes 5898240 | tf_op jit(solution)/shard_map/all_to_all | solution.py:446
  165.9 2.5 %reshape.59 = bf16[8,2,16,4,1440]{4,3,2,1,0:T(4,128)(2,1)} reshape(bf16[8,2,64,1440]{3,2,1,0:T(8,128)(2,1)S(1)} %all_to_all.15) | data formatting | bytes 5898240 | tf_op jit(solution)/shard_map/reshape | solution.py:483
  168.4 5.0 %copy.19 = bf16[16,8,2,4,1440]{4,3,2,1,0:T(4,128)(2,1)} copy(bf16[16,8,2,4,1440]{4,3,0,2,1:T(4,128)(2,1)} %bitcast.29) | data formatting | bytes 5898240 | tf_op jit(solution)/shard_map/transpose | solution.py:484
  (34 shorter events, 0.1 us)
Async XLA Ops:
  3.3 2.7 %copy-start.1 = (bf16[16,16,4,1440]{3,1,2,0:T(8,128)(2,1)}, bf16[16,16,4,1440]{3,1,2,0:T(8,128)(2,1)S(1)}, u32[]{:S(2)}) copy-start(bf16[16,16,4,1440]{3,1,2,0:T(8,128)(2,1)S(1)} %copy.21) | copy-start | bytes 8847364
  6.0 21.9 %collective-permute-start.3 = (bf16[8,2,16,1440]{3,2,1,0:T(8,128)(2,1)}, bf16[8,2,16,1440]{3,2,1,0:T(8,128)(2,1)}, u32[]{:S(2)}, u32[]{:S(2)}) collective-permute-start(bf16[8,2,16,1440]{3,2,1,0:T(8,128)(2,1)} %get-tuple-element.73), channel_id=1, source_target_pairs={{1,0},{2,1},{3,2},{4,3},{5,4},{6,5},{7,6},{8,7},{9,8},{10,9},{11,1... | collective-permute-start | bytes 2211848 | tf_op jit(solution)/shard_map/ppermute | solution.py:456
  7.2 21.5 %collective-permute-start.2 = (bf16[8,2,16,1440]{3,2,1,0:T(8,128)(2,1)}, bf16[8,2,16,1440]{3,2,1,0:T(8,128)(2,1)}, u32[]{:S(2)}, u32[]{:S(2)}) collective-permute-start(bf16[8,2,16,1440]{3,2,1,0:T(8,128)(2,1)} %get-tuple-element.74), channel_id=1, source_target_pairs={{0,1},{1,2},{2,3},{3,4},{4,5},{5,6},{6,7},{7,8},{8,9},{9,10},{10,1... | collective-permute-start | bytes 2211848 | tf_op jit(solution)/shard_map/ppermute | solution.py:456
  13.1 7.3 %copy-start = (bf16[16,16,4,1440]{3,2,1,0:T(4,128)(2,1)S(1)}, bf16[16,16,4,1440]{3,2,1,0:T(4,128)(2,1)}, u32[]{:S(2)}) copy-start(bf16[16,16,4,1440]{3,2,1,0:T(4,128)(2,1)} %param.9) | copy-start | bytes 8847364
  15.5 35.6 %collective-permute-start = (bf16[8,2,16,1440]{3,2,1,0:T(8,128)(2,1)}, bf16[8,2,16,1440]{3,2,1,0:T(8,128)(2,1)}, u32[]{:S(2)}, u32[]{:S(2)}) collective-permute-start(bf16[8,2,16,1440]{3,2,1,0:T(8,128)(2,1)} %get-tuple-element.46), channel_id=1, source_target_pairs={{0,1},{1,2},{2,3},{3,4},{4,5},{5,6},{6,7},{7,8},{8,9},{9,10},{10,1... | collective-permute-start | bytes 2211848 | tf_op jit(solution)/shard_map/ppermute | solution.py:456
  19.1 32.1 %collective-permute-start.1 = (bf16[8,2,16,1440]{3,2,1,0:T(8,128)(2,1)}, bf16[8,2,16,1440]{3,2,1,0:T(8,128)(2,1)}, u32[]{:S(2)}, u32[]{:S(2)}) collective-permute-start(bf16[8,2,16,1440]{3,2,1,0:T(8,128)(2,1)} %get-tuple-element.47), channel_id=1, source_target_pairs={{1,0},{2,1},{3,2},{4,3},{5,4},{6,5},{7,6},{8,7},{9,8},{10,9},{11,1... | collective-permute-start | bytes 2211848 | tf_op jit(solution)/shard_map/ppermute | solution.py:456
  44.1 32.6 %all-to-all-start = ((bf16[8,2,32,1440]{3,2,1,0:T(8,128)(2,1)}), bf16[8,2,32,1440]{3,2,1,0:T(8,128)(2,1)S(1)}, u32[]{:S(2)}, u32[]{:S(2)}) async-start(bf16[8,2,32,1440]{3,2,1,0:T(8,128)(2,1)} %get-tuple-element.59), calls=%async_computation | async-start | bytes 3145728 | tf_op jit(solution)/shard_map/all_to_all | solution.py:446
  66.5 6.8 %collective-permute-start.10 = (f32[16,256]{1,0:T(8,128)}, f32[16,256]{1,0:T(8,128)S(1)}, u32[]{:S(2)}, u32[]{:S(2)}) collective-permute-start(f32[16,256]{1,0:T(8,128)} %get-tuple-element.60.refs_0_), channel_id=1, source_target_pairs={{0,112},{16,96},{32,80},{48,64},{64,48},{80,32},{96,16},{112,0},{1... | collective-permute-start | bytes 49160 | tf_op jit(solution)/shard_map/ppermute | solution.py:443
  69.5 5.0 %collective-permute-start.9 = (f32[16,256]{1,0:T(8,128)}, f32[16,256]{1,0:T(8,128)S(1)}, u32[]{:S(2)}, u32[]{:S(2)}) collective-permute-start(f32[16,256]{1,0:T(8,128)} %get-tuple-element.60.refs_0_), channel_id=1, source_target_pairs={{0,96},{16,112},{32,64},{48,80},{64,32},{80,48},{96,0},{112,16},{1... | collective-permute-start | bytes 49160 | tf_op jit(solution)/shard_map/ppermute | solution.py:443
  69.5 5.5 %collective-permute-start.8 = (f32[16,256]{1,0:T(8,128)}, f32[16,256]{1,0:T(8,128)S(1)}, u32[]{:S(2)}, u32[]{:S(2)}) collective-permute-start(f32[16,256]{1,0:T(8,128)} %get-tuple-element.60.refs_0_), channel_id=1, source_target_pairs={{0,80},{16,64},{32,112},{48,96},{64,16},{80,0},{96,48},{112,32},{1... | collective-permute-start | bytes 49160 | tf_op jit(solution)/shard_map/ppermute | solution.py:443
  71.5 4.3 %collective-permute-start.7 = (f32[16,256]{1,0:T(8,128)}, f32[16,256]{1,0:T(8,128)S(1)}, u32[]{:S(2)}, u32[]{:S(2)}) collective-permute-start(f32[16,256]{1,0:T(8,128)} %get-tuple-element.60.refs_0_), channel_id=1, source_target_pairs={{0,64},{16,80},{32,96},{48,112},{64,0},{80,16},{96,32},{112,48},{1... | collective-permute-start | bytes 49160 | tf_op jit(solution)/shard_map/ppermute | solution.py:443
  72.8 3.8 %collective-permute-start.6 = (f32[16,256]{1,0:T(8,128)}, f32[16,256]{1,0:T(8,128)S(1)}, u32[]{:S(2)}, u32[]{:S(2)}) collective-permute-start(f32[16,256]{1,0:T(8,128)} %get-tuple-element.60.refs_0_), channel_id=1, source_target_pairs={{0,48},{16,32},{32,16},{48,0},{64,112},{80,96},{96,80},{112,64},{1... | collective-permute-start | bytes 49160 | tf_op jit(solution)/shard_map/ppermute | solution.py:443
  73.3 9.9 %copy-start.8 = (f32[16,256]{1,0:T(8,128)}, f32[16,256]{1,0:T(8,128)S(1)}, u32[]{:S(2)}) copy-start(f32[16,256]{1,0:T(8,128)S(1)} %collective-permute-done.10.refs_7_) | copy-start | bytes 49156
  73.3 3.3 %collective-permute-start.5 = (f32[16,256]{1,0:T(8,128)}, f32[16,256]{1,0:T(8,128)S(1)}, u32[]{:S(2)}, u32[]{:S(2)}) collective-permute-start(f32[16,256]{1,0:T(8,128)} %get-tuple-element.60.refs_0_), channel_id=1, source_target_pairs={{0,32},{16,48},{32,0},{48,16},{64,96},{80,112},{96,64},{112,80},{1... | collective-permute-start | bytes 49160 | tf_op jit(solution)/shard_map/ppermute | solution.py:443
  74.5 8.8 %copy-start.9 = (f32[16,256]{1,0:T(8,128)}, f32[16,256]{1,0:T(8,128)S(1)}, u32[]{:S(2)}) copy-start(f32[16,256]{1,0:T(8,128)S(1)} %collective-permute-done.9.refs_6_) | copy-start | bytes 49156
  74.5 2.2 %collective-permute-start.4 = (f32[16,256]{1,0:T(8,128)}, f32[16,256]{1,0:T(8,128)S(1)}, u32[]{:S(2)}, u32[]{:S(2)}) collective-permute-start(f32[16,256]{1,0:T(8,128)} %get-tuple-element.60.refs_0_), channel_id=1, source_target_pairs={{0,16},{16,0},{32,48},{48,32},{64,80},{80,64},{96,112},{112,96},{1... | collective-permute-start | bytes 49160 | tf_op jit(solution)/shard_map/ppermute | solution.py:443
  75.0 8.3 %copy-start.10 = (f32[16,256]{1,0:T(8,128)}, f32[16,256]{1,0:T(8,128)S(1)}, u32[]{:S(2)}) copy-start(f32[16,256]{1,0:T(8,128)S(1)} %collective-permute-done.8.refs_5_) | copy-start | bytes 49156
  75.8 7.4 %copy-start.11 = (f32[16,256]{1,0:T(8,128)}, f32[16,256]{1,0:T(8,128)S(1)}, u32[]{:S(2)}) copy-start(f32[16,256]{1,0:T(8,128)S(1)} %collective-permute-done.7.refs_4_) | copy-start | bytes 49156
  76.6 6.6 %copy-start.12 = (f32[16,256]{1,0:T(8,128)}, f32[16,256]{1,0:T(8,128)S(1)}, u32[]{:S(2)}) copy-start(f32[16,256]{1,0:T(8,128)S(1)} %collective-permute-done.6.refs_3_) | copy-start | bytes 49156
  76.6 6.6 %copy-start.13 = (f32[16,256]{1,0:T(8,128)}, f32[16,256]{1,0:T(8,128)S(1)}, u32[]{:S(2)}) copy-start(f32[16,256]{1,0:T(8,128)S(1)} %collective-permute-done.5.refs_2_) | copy-start | bytes 49156
  76.6 6.6 %copy-start.14 = (f32[16,256]{1,0:T(8,128)}, f32[16,256]{1,0:T(8,128)S(1)}, u32[]{:S(2)}) copy-start(f32[16,256]{1,0:T(8,128)S(1)} %collective-permute-done.4.refs_1_) | copy-start | bytes 49156
  76.7 8.4 %copy-start.2 = (bf16[8,2,32,1440]{3,2,1,0:T(8,128)(2,1)}, bf16[8,2,32,1440]{3,2,1,0:T(8,128)(2,1)S(1)}, u32[]{:S(2)}) copy-start(bf16[8,2,32,1440]{3,2,1,0:T(8,128)(2,1)S(1)} %all-to-all-done.early_ref) | copy-start | bytes 4423684
  76.7 37.6 %all-to-all-start.1 = ((bf16[8,2,32,1440]{3,2,1,0:T(8,128)(2,1)}), bf16[8,2,32,1440]{3,2,1,0:T(8,128)(2,1)S(1)}, u32[]{:S(2)}, u32[]{:S(2)}) async-start(bf16[8,2,32,1440]{3,2,1,0:T(8,128)(2,1)} %get-tuple-element.70), calls=%async_computation.1 | async-start | bytes 3145728 | tf_op jit(solution)/shard_map/all_to_all | solution.py:446
  85.1 9.1 %collective-permute-start.13 = (f32[136,128]{1,0:T(8,128)}, f32[136,128]{1,0:T(8,128)S(1)}, u32[]{:S(2)}, u32[]{:S(2)}) collective-permute-start(f32[136,128]{1,0:T(8,128)} %shard_map.115), channel_id=1, source_target_pairs={{0,3},{1,2},{2,1},{3,0},{4,7},{5,6},{6,5},{7,4},{8,11},{9,10},{10,... | collective-permute-start | bytes 208904 | tf_op jit(solution)/shard_map/ppermute | solution.py:443
  91.0 4.9 %collective-permute-start.12 = (f32[136,128]{1,0:T(8,128)}, f32[136,128]{1,0:T(8,128)S(1)}, u32[]{:S(2)}, u32[]{:S(2)}) collective-permute-start(f32[136,128]{1,0:T(8,128)} %shard_map.115), channel_id=1, source_target_pairs={{0,2},{1,3},{2,0},{3,1},{4,6},{5,7},{6,4},{7,5},{8,10},{9,11},{10,... | collective-permute-start | bytes 208904 | tf_op jit(solution)/shard_map/ppermute | solution.py:443
  91.0 4.9 %collective-permute-start.11 = (f32[136,128]{1,0:T(8,128)}, f32[136,128]{1,0:T(8,128)S(1)}, u32[]{:S(2)}, u32[]{:S(2)}) collective-permute-start(f32[136,128]{1,0:T(8,128)} %shard_map.115), channel_id=1, source_target_pairs={{0,1},{1,0},{2,3},{3,2},{4,5},{5,4},{6,7},{7,6},{8,9},{9,8},{10,11... | collective-permute-start | bytes 208904 | tf_op jit(solution)/shard_map/ppermute | solution.py:443
  96.8 10.5 %copy-start.4 = (f32[136,128]{1,0:T(8,128)}, f32[136,128]{1,0:T(8,128)S(1)}, u32[]{:S(2)}) copy-start(f32[136,128]{1,0:T(8,128)S(1)} %add_add_fusion.a_ref) | copy-start | bytes 208900
  96.8 7.8 %collective-permute-start.16 = (f32[136,128]{1,0:T(8,128)S(1)}, f32[136,128]{1,0:T(8,128)S(1)}, u32[]{:S(2)}, u32[]{:S(2)}) collective-permute-start(f32[136,128]{1,0:T(8,128)S(1)} %add_add_fusion.a_ref), channel_id=1, source_target_pairs={{0,12},{1,13},{2,14},{3,15},{4,8},{5,9},{6,10},{7,11},{8,4},{9,5},... | collective-permute-start | bytes 208904 | tf_op jit(solution)/shard_map/ppermute | solution.py:443
  102.6 4.7 %collective-permute-start.15 = (f32[136,128]{1,0:T(8,128)S(1)}, f32[136,128]{1,0:T(8,128)S(1)}, u32[]{:S(2)}, u32[]{:S(2)}) collective-permute-start(f32[136,128]{1,0:T(8,128)S(1)} %add_add_fusion.a_ref), channel_id=1, source_target_pairs={{0,8},{1,9},{2,10},{3,11},{4,12},{5,13},{6,14},{7,15},{8,0},{9,1},... | collective-permute-start | bytes 208904 | tf_op jit(solution)/shard_map/ppermute | solution.py:443
  102.7 4.6 %collective-permute-start.14 = (f32[136,128]{1,0:T(8,128)S(1)}, f32[136,128]{1,0:T(8,128)S(1)}, u32[]{:S(2)}, u32[]{:S(2)}) collective-permute-start(f32[136,128]{1,0:T(8,128)S(1)} %add_add_fusion.a_ref), channel_id=1, source_target_pairs={{0,4},{1,5},{2,6},{3,7},{4,0},{5,1},{6,2},{7,3},{8,12},{9,13},{10,... | collective-permute-start | bytes 208904 | tf_op jit(solution)/shard_map/ppermute | solution.py:443
  104.6 2.7 %copy-start.5 = (f32[136,128]{1,0:T(8,128)}, f32[136,128]{1,0:T(8,128)S(1)}, u32[]{:S(2)}) copy-start(f32[136,128]{1,0:T(8,128)S(1)} %collective-permute-done.16.d_ref) | copy-start | bytes 208900
  107.3 0.6 copy-start.6
  107.9 0.6 copy-start.7
  114.2 1.1 copy-start.3

commit v6 on v5

--- a/solution.py
+++ b/solution.py
@@ -383,7 +383,8 @@
         row = lax.broadcasted_iota(jnp.int32, shape, 0)
         column = lax.broadcasted_iota(jnp.int32, shape, 1)
         held = row % half // 32 * GROUP + row // half * 8 + row % 32 // ROWS
-        repeat = (row // ROWS == column).astype(jnp.bfloat16)
+        wanted = row // 64 * GROUP + row % GROUP
+        repeat = (wanted == column).astype(jnp.bfloat16)
         placed = (held == column).astype(jnp.bfloat16)
         tall = jnp.dot(repeat, transform_ref[...], preferred_element_type=jnp.float32)
         wide = lax.dot_general(
@@ -392,7 +393,7 @@
             (((1,), (1,)), ((), ())),
             preferred_element_type=jnp.float32,
         )
-        own = lax.broadcasted_iota(jnp.int32, (rows, rows), 0) % ROWS
+        own = lax.broadcasted_iota(jnp.int32, (rows, rows), 0) // GROUP % ROWS
         same = own == lax.broadcasted_iota(jnp.int32, (rows, rows), 1) % ROWS
         spread_ref[...] = jnp.where(same, wide, 0.0).astype(jnp.bfloat16)
 
@@ -459,11 +460,11 @@
     shared = prepare(
         tile, tiles, conv_in, bias_in, conv_out, bias_out, observed_entry_index
     )
-    next_edges, shared = lax.optimization_barrier((edges(1), shared))
-    halos.append(halo(next_edges))
     base = jnp.transpose(
         ensemble_weather.reshape(GROUP // STEP, STEP, FIELDS, ROWS, LON), (0, 2, 1, 3, 4)
     ).reshape(GROUP // STEP, STEP * PLANES, LON)
+    next_edges, shared, base = lax.optimization_barrier((edges(1), shared, base))
+    halos.append(halo(next_edges))
     fields, observed = [], None
     for chunk, (top, bottom) in enumerate(halos):
         moved, observed = forecast(chunk * share, own, base, top, bottom, shared, observed)
@@ -480,8 +481,8 @@
         [row] + [swap(row, "map", step) for step in (4, 8, 12)]
     )
     back = exchange(update(transform, early, late))
-    back = back.reshape(N_ENS, 2, GROUP, ROWS, LON)
-    analysis = jnp.transpose(back, (2, 0, 1, 3, 4)).reshape(GROUP, FIELDS, ROWS, LON)
+    back = back.reshape(FIELDS, ROWS, GROUP, LON)
+    analysis = jnp.transpose(back, (2, 0, 1, 3))
     return (analysis, factor, mean_weights.reshape(MEMBERS))
 
 

time: 174 us -> 171 us (0.983)
  starting transfers between devices: 46.5 us -> 42.6 us
  waiting for transfers between devices: 12 us -> 15.2 us
  local copies, waits for them, and re-layouts: 21.4 us -> 19.6 us
    transpose x1 -> x0, local copies, waits for them, and re-layouts: 5 us -> none  [on_device(): jnp.transpose(back, (2, 0, 1, 3, 4)).reshape(GROUP, FIELDS, ROWS, LON)]
    ppermute x13, starting transfers between devices: 21.5 us -> 17 us  [swap(): return lax.ppermute(value, axis, pairs)]
    ppermute x13, waiting for transfers between devices: 9.87 us -> 12.9 us  [swap(): return lax.ppermute(value, axis, pairs)]
    optimization_barrier x0 -> x1, local copies, waits for them, and re-layouts: none -> 2.2 us  [on_device(): lax.optimization_barrier((edges(1), shared, base))]
    reshape x2 -> x1, local copies, waits for them, and re-layouts: 4.66 us -> 4.09 us  [on_device(): back = back.reshape(FIELDS, ROWS, GROUP, LON)]
    unnamed x31 -> x33, local copies, waits for them, and re-layouts: 5.82 us -> 5.93 us
  transfers between devices with their start and end apart: 19 -> 19, of which waited for: 8 -> 9; matrix products, arithmetic and copies ran while one was open for 4% -> 5% of each run, Pallas kernels for 23% -> 24%
where the time goes in v6:
time: 171 us; the launch traced here: 170 us
  Pallas kernels  46.2 us (27%)
  blocking collectives  44.3 us (26%)
  starting transfers between devices  42.6 us (25%)
  local copies, waits for them, and re-layouts  19.6 us (11%)
  waiting for transfers between devices  15.2 us (9%)
    all_to_all x1, blocking collectives, on_device(): lax.all_to_all(value, 'ens', split_axis=0, concat_axis=0, tiled=True)  44.3 us
    pallas_call x2, Pallas kernels, forecast(): pl.pallas_call(kernel, grid=(steps,), in_specs=[pl.BlockSpec((STEP, ROWS,...  30.7 us
    ppermute x13, starting transfers between devices, swap(): return lax.ppermute(value, axis, pairs)  17 us
    ppermute x13, waiting for transfers between devices, swap(): return lax.ppermute(value, axis, pairs)  12.9 us
    all_to_all x2, starting transfers between devices, on_device(): lax.all_to_all(value, 'ens', split_axis=0, concat_axis=0, tiled=True)  12.6 us
    ppermute x2, starting transfers between devices, halo(): lax.ppermute(rows[0], 'map', down)  10.2 us
    unnamed x33, local copies, waits for them, and re-layouts  5.93 us
    pallas_call x1, Pallas kernels, update(): pl.pallas_call(update_kernel, grid=(2, 2), in_specs=[pl.BlockSpec((MEMBER...  5.68 us
  transfers between devices with their start and end apart: 19, of which 9 were waited for; matrix products, arithmetic and copies ran while one was open for 5% of the time, Pallas kernels for 24%

profile of v6, /device:TPU:1, one launch (start us, length us, event | category | flops | bytes accessed | tf_op | source)
XLA Modules:
  0.0 170.3 jit_solution(7694742943962632740)
XLA Ops:
  0.6 2.7 %copy.23 = bf16[16,16,4,1440]{3,1,2,0:T(8,128)(2,1)S(1)} copy(bf16[16,16,4,1440]{3,2,1,0:T(4,128)(2,1)} %param.9) | data formatting | bytes 5898240 | tf_op args[0]
  3.3 0.0 copy-start.1
  3.3 0.0 copy-start
  3.3 1.7 fusion
  5.0 1.4 copy-done.1
  6.4 5.4 %collective-permute-start.2 = (bf16[8,2,16,1440]{3,2,1,0:T(8,128)(2,1)}, bf16[8,2,16,1440]{3,2,1,0:T(8,128)(2,1)}, u32[]{:S(2)}, u32[]{:S(2)}) collective-permute-start(bf16[8,2,16,1440]{3,2,1,0:T(8,128)(2,1)} %get-tuple-element.76), channel_id=1, source_target_pairs={{0,1},{1,2},{2,3},{3,4},{4,5},{5,6},{6,7},{7,8},{8,9},{9,10},{10,1... | collective-permute-start | bytes 2211848 | tf_op jit(solution)/shard_map/ppermute | solution.py:457
  11.8 1.3 collective-permute-start.3
  13.1 5.7 %copy.16 = bf16[4,4,16,4,1440]{4,0,3,1,2:T(4,128)(2,1)} copy(bf16[4,4,16,4,1440]{4,3,2,1,0:T(4,128)(2,1)S(1)} %bitcast.25) | data formatting | bytes 5898240 | tf_op jit(solution)/shard_map/reshape | solution.py:464
  18.8 2.4 %shard_map.112 = (bf16[384,256]{1,0:T(8,128)(2,1)}, bf16[384,256]{1,0:T(8,128)(2,1)}, bf16[96,256]{1,0:T(8,128)(2,1)}, bf16[192,256]{1,0:T(8,128)(2,1)}, bf16[96...) custom-call(s32[1]{0:T(128)} %bitcast.4.tile_ref, ...), custom_call_target="tpu_custom_call" | custom-call | flops 3000000000 | bytes 3000000 | tf_op jit(solution)/shard_map/pallas_call | solution.py:107
  21.2 4.9 %collective-permute-start = (bf16[8,2,16,1440]{3,2,1,0:T(8,128)(2,1)}, bf16[8,2,16,1440]{3,2,1,0:T(8,128)(2,1)}, u32[]{:S(2)}, u32[]{:S(2)}) collective-permute-start(bf16[8,2,16,1440]{3,2,1,0:T(8,128)(2,1)} %get-tuple-element.48), channel_id=1, source_target_pairs={{0,1},{1,2},{2,3},{3,4},{4,5},{5,6},{6,7},{7,8},{8,9},{9,10},{10,1... | collective-permute-start | bytes 2211848 | tf_op jit(solution)/shard_map/ppermute | solution.py:457
  26.1 1.5 collective-permute-start.1
  27.6 2.2 %copy.18.refs_1_.base_ref = bf16[4,256,1440]{2,1,0:T(8,128)(2,1)} copy(bf16[4,256,1440]{2,0,1:T(4,128)(2,1)S(1)} %bitcast.29) | data formatting | bytes 5898240 | tf_op jit(solution)/shard_map/optimization_barrier | solution.py:466
  29.8 0.0 collective-permute-done.2.refs_2_
  29.8 2.3 %collective-permute-done.3.refs_3_ = bf16[8,2,16,1440]{3,2,1,0:T(8,128)(2,1)} collective-permute-done((bf16[8,2,16,1440]{3,2,1,0:T(8,128)(2,1)}, bf16[8,2,16,1440]{3,2,1,0:T(8,128)(2,1)}, u32[]{:S(2)}, u32[]{:S(2)}) %collective-permute-start.3) | collective-permute-done | bytes 737312 | tf_op jit(solution)/shard_map/ppermute | solution.py:457
  32.1 15.3 %shard_map.113 = (bf16[8,2,32,1440]{3,2,1,0:T(8,128)(2,1)}, f32[8,256]{1,0:T(8,128)}) custom-call(bf16[16,4,16,1440]{3,2,1,0:T(8,128)(2,1)} %bitcast.27, bf16[4,256,1440]{2,1,0:T(8,128)(2,1)} %copy.18.refs_1_.base_ref, bf16[8,2,16,1440]{3,2,1,0:T(8,128)(2,1)} %collective-permute-done.2.refs_2_, bf16[8,2,16,1440]{3,2,1,0:T(8,128)(2,1)} %collective-permute-done.3.refs_3_, ...), custom_call_target="tpu_custom_call" | custom-call | flops 16000000000 | bytes 16000000 | tf_op jit(solution)/shard_map/pallas_call | solution.py:250
  47.4 7.6 %all-to-all-start = ((bf16[8,2,32,1440]{3,2,1,0:T(8,128)(2,1)}), bf16[8,2,32,1440]{3,2,1,0:T(8,128)(2,1)S(1)}, u32[]{:S(2)}, u32[]{:S(2)}) async-start(bf16[8,2,32,1440]{3,2,1,0:T(8,128)(2,1)} %get-tuple-element.61), calls=%async_computation | async-start | bytes 3145728 | tf_op jit(solution)/shard_map/all_to_all | solution.py:447
  55.1 0.0 collective-permute-done.top_ref
  55.1 0.0 collective-permute-done.1.bottom_ref
  55.1 15.4 %shard_map.114 = (bf16[8,2,32,1440]{3,2,1,0:T(8,128)(2,1)}, f32[16,256]{1,0:T(8,128)}) custom-call(bf16[16,4,16,1440]{3,2,1,0:T(8,128)(2,1)} %bitcast.28, bf16[4,256,1440]{2,1,0:T(8,128)(2,1)} %copy.18.refs_1_.base_ref, bf16[8,2,16,1440]{3,2,1,0:T(8,128)(2,1)} %collective-permute-done.top_ref, bf16[8,2,16,1440]{3,2,1,0:T(8,128)(2,1)} %collective-permute-done.1.bottom_ref, ...), custom_call_target="tpu_custom_call" | custom-call | flops 16000000000 | bytes 16000000 | tf_op jit(solution)/shard_map/pallas_call | solution.py:250
  70.4 2.9 %collective-permute-start.10 = (f32[16,256]{1,0:T(8,128)}, f32[16,256]{1,0:T(8,128)S(1)}, u32[]{:S(2)}, u32[]{:S(2)}) collective-permute-start(f32[16,256]{1,0:T(8,128)} %get-tuple-element.62.refs_0_), channel_id=1, source_target_pairs={{0,112},{16,96},{32,80},{48,64},{64,48},{80,32},{96,16},{112,0},{1... | collective-permute-start | bytes 49160 | tf_op jit(solution)/shard_map/ppermute | solution.py:444
  73.3 0.2 collective-permute-start.4
  73.5 2.0 %collective-permute-start.6 = (f32[16,256]{1,0:T(8,128)}, f32[16,256]{1,0:T(8,128)S(1)}, u32[]{:S(2)}, u32[]{:S(2)}) collective-permute-start(f32[16,256]{1,0:T(8,128)} %get-tuple-element.62.refs_0_), channel_id=1, source_target_pairs={{0,48},{16,32},{32,16},{48,0},{64,112},{80,96},{96,80},{112,64},{1... | collective-permute-start | bytes 49160 | tf_op jit(solution)/shard_map/ppermute | solution.py:444
  75.5 0.6 collective-permute-start.7
  76.1 0.5 collective-permute-done.10.refs_7_
  76.5 1.9 %collective-permute-start.8 = (f32[16,256]{1,0:T(8,128)}, f32[16,256]{1,0:T(8,128)S(1)}, u32[]{:S(2)}, u32[]{:S(2)}) collective-permute-start(f32[16,256]{1,0:T(8,128)} %get-tuple-element.62.refs_0_), channel_id=1, source_target_pairs={{0,80},{16,64},{32,112},{48,96},{64,16},{80,0},{96,48},{112,32},{1... | collective-permute-start | bytes 49160 | tf_op jit(solution)/shard_map/ppermute | solution.py:444
  78.5 1.1 collective-permute-start.9
  79.6 0.2 collective-permute-done.7.refs_4_
  79.8 1.6 collective-permute-done.8.refs_5_
  81.4 1.1 collective-permute-done.9.refs_6_
  82.5 5.0 %all-to-all-start.1 = ((bf16[8,2,32,1440]{3,2,1,0:T(8,128)(2,1)}), bf16[8,2,32,1440]{3,2,1,0:T(8,128)(2,1)S(1)}, u32[]{:S(2)}, u32[]{:S(2)}) async-start(bf16[8,2,32,1440]{3,2,1,0:T(8,128)(2,1)} %get-tuple-element.72), calls=%async_computation.1 | async-start | bytes 3145728 | tf_op jit(solution)/shard_map/all_to_all | solution.py:447
  88.2 1.8 %shard_map.115 = f32[136,128]{1,0:T(8,128)} custom-call(s32[1]{0:T(128)} %bitcast.place_ref, s32[1]{0:T(128)S(6)} %copy.24.count_ref, f32[1,256]{1,0:T(1,128)} %bitcast.35, f32[1,256]{1,0:T(1,128)} %bitcast.36, f32[16,256]{1,0:T(8,128)} %get-tuple-element.62.refs_0_, f32[16,256]{1,0:T(8,128)} %copy-done.10, f32[16,256]{1,0:T(8,128)} %copy-done.11, ...), custom_call_target="tpu_custom_call" | custom-call | flops 1000000000 | bytes 1000000 | tf_op jit(solution)/shard_map/pallas_call | solution.py:299
  90.1 0.8 collective-permute-start.11
  90.9 3.6 %collective-permute-start.12 = (f32[136,128]{1,0:T(8,128)}, f32[136,128]{1,0:T(8,128)S(1)}, u32[]{:S(2)}, u32[]{:S(2)}) collective-permute-start(f32[136,128]{1,0:T(8,128)} %shard_map.115), channel_id=1, source_target_pairs={{0,2},{1,3},{2,0},{3,1},{4,6},{5,7},{6,4},{7,5},{8,10},{9,11},{10,... | collective-permute-start | bytes 208904 | tf_op jit(solution)/shard_map/ppermute | solution.py:444
  94.4 4.0 %collective-permute-done.12 = f32[136,128]{1,0:T(8,128)S(1)} collective-permute-done((f32[136,128]{1,0:T(8,128)}, f32[136,128]{1,0:T(8,128)S(1)}, u32[]{:S(2)}, u32[]{:S(2)}) %collective-permute-start.12) | collective-permute-done | bytes 69664 | tf_op jit(solution)/shard_map/ppermute | solution.py:444
  98.4 1.2 collective-permute-done.13
  99.6 0.9 add_add_fusion.a_ref
  100.5 0.0 copy-start.5
  100.5 1.4 collective-permute-start.14
  101.9 1.6 collective-permute-start.15
  103.5 1.0 collective-permute-start.16
  104.5 3.0 %collective-permute-done.15.c_ref = f32[136,128]{1,0:T(8,128)S(1)} collective-permute-done((f32[136,128]{1,0:T(8,128)S(1)}, f32[136,128]{1,0:T(8,128)S(1)}, u32[]{:S(2)}, u32[]{:S(2)}) %collective-permute-start.15) | collective-permute-done | bytes 69664 | tf_op jit(solution)/shard_map/ppermute | solution.py:444
  107.5 1.3 collective-permute-done.16.d_ref
  108.8 0.6 copy-done.8
  109.4 5.7 %shard_map.116 = (f32[128,128]{1,0:T(8,128)}, f32[1,128]{1,0:T(1,128)}, bf16[128,128]{1,0:T(8,128)(2,1)}) custom-call(f32[136,128]{1,0:T(8,128)} %copy-done.5, f32[136,128]{1,0:T(8,128)} %copy-done.6, f32[136,128]{1,0:T(8,128)} %copy-done.7, f32[136,128]{1,0:T(8,128)} %copy-done.8), custom_call_target="tpu_custom_call" | custom-call | flops 1000000000 | bytes 1000000 | tf_op jit(solution)/shard_map/pallas_call | solution.py:363
  115.1 1.2 copy-done.4
  116.3 5.7 %shard_map.117 = bf16[8,2,64,1440]{3,2,1,0:T(8,128)(2,1)} custom-call(bf16[128,128]{1,0:T(8,128)(2,1)} %get-tuple-element.70.transform_ref, bf16[8,2,32,1440]{3,2,1,0:T(8,128)(2,1)} %copy-done.3, bf16[8,2,32,1440]{3,2,1,0:T(8,128)(2,1)} %copy-done.4), custom_call_target="tpu_custom_call" | custom-call | flops 4000000000 | bytes 4000000 | tf_op jit(solution)/shard_map/pallas_call | solution.py:411
  121.9 44.3 %all_to_all.15 = bf16[8,2,64,1440]{3,2,1,0:T(8,128)(2,1)S(1)} all-to-all(bf16[8,2,64,1440]{3,2,1,0:T(8,128)(2,1)} %shard_map.117), channel_id=1, replica_groups=mesh['ens'=8,'map'=16] {'ens'}, dimensions={0} | all-to-all | bytes 5898240 | tf_op jit(solution)/shard_map/all_to_all | solution.py:447
  166.2 4.1 %copy.22 = bf16[16,4,16,1440]{3,1,0,2:T(4,128)(2,1)} copy(bf16[16,4,16,1440]{3,2,1,0:T(8,128)(2,1)S(1)} %bitcast.30) | data formatting | bytes 5898240 | tf_op jit(solution)/shard_map/reshape | solution.py:484
  (35 shorter events, 0.1 us)
Async XLA Ops:
  3.3 3.2 %copy-start.1 = (bf16[16,16,4,1440]{3,1,2,0:T(8,128)(2,1)}, bf16[16,16,4,1440]{3,1,2,0:T(8,128)(2,1)S(1)}, u32[]{:S(2)}) copy-start(bf16[16,16,4,1440]{3,1,2,0:T(8,128)(2,1)S(1)} %copy.23) | copy-start | bytes 8847364
  3.3 9.8 %copy-start = (bf16[16,16,4,1440]{3,2,1,0:T(4,128)(2,1)S(1)}, bf16[16,16,4,1440]{3,2,1,0:T(4,128)(2,1)}, u32[]{:S(2)}) copy-start(bf16[16,16,4,1440]{3,2,1,0:T(4,128)(2,1)} %param.9) | copy-start | bytes 8847364
  6.4 23.3 %collective-permute-start.2 = (bf16[8,2,16,1440]{3,2,1,0:T(8,128)(2,1)}, bf16[8,2,16,1440]{3,2,1,0:T(8,128)(2,1)}, u32[]{:S(2)}, u32[]{:S(2)}) collective-permute-start(bf16[8,2,16,1440]{3,2,1,0:T(8,128)(2,1)} %get-tuple-element.76), channel_id=1, source_target_pairs={{0,1},{1,2},{2,3},{3,4},{4,5},{5,6},{6,7},{7,8},{8,9},{9,10},{10,1... | collective-permute-start | bytes 2211848 | tf_op jit(solution)/shard_map/ppermute | solution.py:457
  11.8 20.3 %collective-permute-start.3 = (bf16[8,2,16,1440]{3,2,1,0:T(8,128)(2,1)}, bf16[8,2,16,1440]{3,2,1,0:T(8,128)(2,1)}, u32[]{:S(2)}, u32[]{:S(2)}) collective-permute-start(bf16[8,2,16,1440]{3,2,1,0:T(8,128)(2,1)} %get-tuple-element.75), channel_id=1, source_target_pairs={{1,0},{2,1},{3,2},{4,3},{5,4},{6,5},{7,6},{8,7},{9,8},{10,9},{11,1... | collective-permute-start | bytes 2211848 | tf_op jit(solution)/shard_map/ppermute | solution.py:457
  18.8 8.7 %copy-start.2 = (bf16[4,4,16,4,1440]{4,0,3,1,2:T(4,128)(2,1)S(1)}, bf16[4,4,16,4,1440]{4,0,3,1,2:T(4,128)(2,1)}, u32[]{:S(2)}) copy-start(bf16[4,4,16,4,1440]{4,0,3,1,2:T(4,128)(2,1)} %copy.16) | copy-start | bytes 8847364
  21.2 33.8 %collective-permute-start = (bf16[8,2,16,1440]{3,2,1,0:T(8,128)(2,1)}, bf16[8,2,16,1440]{3,2,1,0:T(8,128)(2,1)}, u32[]{:S(2)}, u32[]{:S(2)}) collective-permute-start(bf16[8,2,16,1440]{3,2,1,0:T(8,128)(2,1)} %get-tuple-element.48), channel_id=1, source_target_pairs={{0,1},{1,2},{2,3},{3,4},{4,5},{5,6},{6,7},{7,8},{8,9},{9,10},{10,1... | collective-permute-start | bytes 2211848 | tf_op jit(solution)/shard_map/ppermute | solution.py:457
  26.1 29.0 %collective-permute-start.1 = (bf16[8,2,16,1440]{3,2,1,0:T(8,128)(2,1)}, bf16[8,2,16,1440]{3,2,1,0:T(8,128)(2,1)}, u32[]{:S(2)}, u32[]{:S(2)}) collective-permute-start(bf16[8,2,16,1440]{3,2,1,0:T(8,128)(2,1)} %get-tuple-element.49), channel_id=1, source_target_pairs={{1,0},{2,1},{3,2},{4,3},{5,4},{6,5},{7,6},{8,7},{9,8},{10,9},{11,1... | collective-permute-start | bytes 2211848 | tf_op jit(solution)/shard_map/ppermute | solution.py:457
  47.4 35.1 %all-to-all-start = ((bf16[8,2,32,1440]{3,2,1,0:T(8,128)(2,1)}), bf16[8,2,32,1440]{3,2,1,0:T(8,128)(2,1)S(1)}, u32[]{:S(2)}, u32[]{:S(2)}) async-start(bf16[8,2,32,1440]{3,2,1,0:T(8,128)(2,1)} %get-tuple-element.61), calls=%async_computation | async-start | bytes 3145728 | tf_op jit(solution)/shard_map/all_to_all | solution.py:447
  70.4 6.1 %collective-permute-start.10 = (f32[16,256]{1,0:T(8,128)}, f32[16,256]{1,0:T(8,128)S(1)}, u32[]{:S(2)}, u32[]{:S(2)}) collective-permute-start(f32[16,256]{1,0:T(8,128)} %get-tuple-element.62.refs_0_), channel_id=1, source_target_pairs={{0,112},{16,96},{32,80},{48,64},{64,48},{80,32},{96,16},{112,0},{1... | collective-permute-start | bytes 49160 | tf_op jit(solution)/shard_map/ppermute | solution.py:444
  73.3 5.2 %collective-permute-start.4 = (f32[16,256]{1,0:T(8,128)}, f32[16,256]{1,0:T(8,128)S(1)}, u32[]{:S(2)}, u32[]{:S(2)}) collective-permute-start(f32[16,256]{1,0:T(8,128)} %get-tuple-element.62.refs_0_), channel_id=1, source_target_pairs={{0,16},{16,0},{32,48},{48,32},{64,80},{80,64},{96,112},{112,96},{1... | collective-permute-start | bytes 49160 | tf_op jit(solution)/shard_map/ppermute | solution.py:444
  73.5 6.1 %collective-permute-start.5 = (f32[16,256]{1,0:T(8,128)}, f32[16,256]{1,0:T(8,128)S(1)}, u32[]{:S(2)}, u32[]{:S(2)}) collective-permute-start(f32[16,256]{1,0:T(8,128)} %get-tuple-element.62.refs_0_), channel_id=1, source_target_pairs={{0,32},{16,48},{32,0},{48,16},{64,96},{80,112},{96,64},{112,80},{1... | collective-permute-start | bytes 49160 | tf_op jit(solution)/shard_map/ppermute | solution.py:444
  73.5 6.1 %collective-permute-start.6 = (f32[16,256]{1,0:T(8,128)}, f32[16,256]{1,0:T(8,128)S(1)}, u32[]{:S(2)}, u32[]{:S(2)}) collective-permute-start(f32[16,256]{1,0:T(8,128)} %get-tuple-element.62.refs_0_), channel_id=1, source_target_pairs={{0,48},{16,32},{32,16},{48,0},{64,112},{80,96},{96,80},{112,64},{1... | collective-permute-start | bytes 49160 | tf_op jit(solution)/shard_map/ppermute | solution.py:444
  75.5 4.3 %collective-permute-start.7 = (f32[16,256]{1,0:T(8,128)}, f32[16,256]{1,0:T(8,128)S(1)}, u32[]{:S(2)}, u32[]{:S(2)}) collective-permute-start(f32[16,256]{1,0:T(8,128)} %get-tuple-element.62.refs_0_), channel_id=1, source_target_pairs={{0,64},{16,80},{32,96},{48,112},{64,0},{80,16},{96,32},{112,48},{1... | collective-permute-start | bytes 49160 | tf_op jit(solution)/shard_map/ppermute | solution.py:444
  76.5 11.6 %copy-start.9 = (f32[16,256]{1,0:T(8,128)}, f32[16,256]{1,0:T(8,128)S(1)}, u32[]{:S(2)}) copy-start(f32[16,256]{1,0:T(8,128)S(1)} %collective-permute-done.10.refs_7_) | copy-start | bytes 49156
  76.5 4.9 %collective-permute-start.8 = (f32[16,256]{1,0:T(8,128)}, f32[16,256]{1,0:T(8,128)S(1)}, u32[]{:S(2)}, u32[]{:S(2)}) collective-permute-start(f32[16,256]{1,0:T(8,128)} %get-tuple-element.62.refs_0_), channel_id=1, source_target_pairs={{0,80},{16,64},{32,112},{48,96},{64,16},{80,0},{96,48},{112,32},{1... | collective-permute-start | bytes 49160 | tf_op jit(solution)/shard_map/ppermute | solution.py:444
  78.5 9.7 %copy-start.10 = (f32[16,256]{1,0:T(8,128)}, f32[16,256]{1,0:T(8,128)S(1)}, u32[]{:S(2)}) copy-start(f32[16,256]{1,0:T(8,128)S(1)} %collective-permute-done.4.refs_1_) | copy-start | bytes 49156
  78.5 4.0 %collective-permute-start.9 = (f32[16,256]{1,0:T(8,128)}, f32[16,256]{1,0:T(8,128)S(1)}, u32[]{:S(2)}, u32[]{:S(2)}) collective-permute-start(f32[16,256]{1,0:T(8,128)} %get-tuple-element.62.refs_0_), channel_id=1, source_target_pairs={{0,96},{16,112},{32,64},{48,80},{64,32},{80,48},{96,0},{112,16},{1... | collective-permute-start | bytes 49160 | tf_op jit(solution)/shard_map/ppermute | solution.py:444
  79.6 8.6 %copy-start.11 = (f32[16,256]{1,0:T(8,128)}, f32[16,256]{1,0:T(8,128)S(1)}, u32[]{:S(2)}) copy-start(f32[16,256]{1,0:T(8,128)S(1)} %collective-permute-done.5.refs_2_) | copy-start | bytes 49156
  79.6 8.6 %copy-start.12 = (f32[16,256]{1,0:T(8,128)}, f32[16,256]{1,0:T(8,128)S(1)}, u32[]{:S(2)}) copy-start(f32[16,256]{1,0:T(8,128)S(1)} %collective-permute-done.6.refs_3_) | copy-start | bytes 49156
  79.8 8.4 %copy-start.13 = (f32[16,256]{1,0:T(8,128)}, f32[16,256]{1,0:T(8,128)S(1)}, u32[]{:S(2)}) copy-start(f32[16,256]{1,0:T(8,128)S(1)} %collective-permute-done.7.refs_4_) | copy-start | bytes 49156
  81.4 6.8 %copy-start.14 = (f32[16,256]{1,0:T(8,128)}, f32[16,256]{1,0:T(8,128)S(1)}, u32[]{:S(2)}) copy-start(f32[16,256]{1,0:T(8,128)S(1)} %collective-permute-done.8.refs_5_) | copy-start | bytes 49156
  82.5 5.7 %copy-start.15 = (f32[16,256]{1,0:T(8,128)}, f32[16,256]{1,0:T(8,128)S(1)}, u32[]{:S(2)}) copy-start(f32[16,256]{1,0:T(8,128)S(1)} %collective-permute-done.9.refs_6_) | copy-start | bytes 49156
  82.5 7.5 %copy-start.3 = (bf16[8,2,32,1440]{3,2,1,0:T(8,128)(2,1)}, bf16[8,2,32,1440]{3,2,1,0:T(8,128)(2,1)S(1)}, u32[]{:S(2)}) copy-start(bf16[8,2,32,1440]{3,2,1,0:T(8,128)(2,1)S(1)} %all-to-all-done.early_ref) | copy-start | bytes 4423684
  82.5 32.6 %all-to-all-start.1 = ((bf16[8,2,32,1440]{3,2,1,0:T(8,128)(2,1)}), bf16[8,2,32,1440]{3,2,1,0:T(8,128)(2,1)S(1)}, u32[]{:S(2)}, u32[]{:S(2)}) async-start(bf16[8,2,32,1440]{3,2,1,0:T(8,128)(2,1)} %get-tuple-element.72), calls=%async_computation.1 | async-start | bytes 3145728 | tf_op jit(solution)/shard_map/all_to_all | solution.py:447
  90.1 4.4 %collective-permute-start.11 = (f32[136,128]{1,0:T(8,128)}, f32[136,128]{1,0:T(8,128)S(1)}, u32[]{:S(2)}, u32[]{:S(2)}) collective-permute-start(f32[136,128]{1,0:T(8,128)} %shard_map.115), channel_id=1, source_target_pairs={{0,1},{1,0},{2,3},{3,2},{4,5},{5,4},{6,7},{7,6},{8,9},{9,8},{10,11... | collective-permute-start | bytes 208904 | tf_op jit(solution)/shard_map/ppermute | solution.py:444
  90.9 7.5 %collective-permute-start.12 = (f32[136,128]{1,0:T(8,128)}, f32[136,128]{1,0:T(8,128)S(1)}, u32[]{:S(2)}, u32[]{:S(2)}) collective-permute-start(f32[136,128]{1,0:T(8,128)} %shard_map.115), channel_id=1, source_target_pairs={{0,2},{1,3},{2,0},{3,1},{4,6},{5,7},{6,4},{7,5},{8,10},{9,11},{10,... | collective-permute-start | bytes 208904 | tf_op jit(solution)/shard_map/ppermute | solution.py:444
  94.4 5.2 %collective-permute-start.13 = (f32[136,128]{1,0:T(8,128)}, f32[136,128]{1,0:T(8,128)S(1)}, u32[]{:S(2)}, u32[]{:S(2)}) collective-permute-start(f32[136,128]{1,0:T(8,128)} %shard_map.115), channel_id=1, source_target_pairs={{0,3},{1,2},{2,1},{3,0},{4,7},{5,6},{6,5},{7,4},{8,11},{9,10},{10,... | collective-permute-start | bytes 208904 | tf_op jit(solution)/shard_map/ppermute | solution.py:444
  100.5 8.3 %copy-start.5 = (f32[136,128]{1,0:T(8,128)}, f32[136,128]{1,0:T(8,128)S(1)}, u32[]{:S(2)}) copy-start(f32[136,128]{1,0:T(8,128)S(1)} %add_add_fusion.a_ref) | copy-start | bytes 208900
  100.5 3.9 %collective-permute-start.14 = (f32[136,128]{1,0:T(8,128)S(1)}, f32[136,128]{1,0:T(8,128)S(1)}, u32[]{:S(2)}, u32[]{:S(2)}) collective-permute-start(f32[136,128]{1,0:T(8,128)S(1)} %add_add_fusion.a_ref), channel_id=1, source_target_pairs={{0,4},{1,5},{2,6},{3,7},{4,0},{5,1},{6,2},{7,3},{8,12},{9,13},{10,... | collective-permute-start | bytes 208904 | tf_op jit(solution)/shard_map/ppermute | solution.py:444
  101.9 5.6 %collective-permute-start.15 = (f32[136,128]{1,0:T(8,128)S(1)}, f32[136,128]{1,0:T(8,128)S(1)}, u32[]{:S(2)}, u32[]{:S(2)}) collective-permute-start(f32[136,128]{1,0:T(8,128)S(1)} %add_add_fusion.a_ref), channel_id=1, source_target_pairs={{0,8},{1,9},{2,10},{3,11},{4,12},{5,13},{6,14},{7,15},{8,0},{9,1},... | collective-permute-start | bytes 208904 | tf_op jit(solution)/shard_map/ppermute | solution.py:444
  103.5 5.3 %collective-permute-start.16 = (f32[136,128]{1,0:T(8,128)S(1)}, f32[136,128]{1,0:T(8,128)S(1)}, u32[]{:S(2)}, u32[]{:S(2)}) collective-permute-start(f32[136,128]{1,0:T(8,128)S(1)} %add_add_fusion.a_ref), channel_id=1, source_target_pairs={{0,12},{1,13},{2,14},{3,15},{4,8},{5,9},{6,10},{7,11},{8,4},{9,5},... | collective-permute-start | bytes 208904 | tf_op jit(solution)/shard_map/ppermute | solution.py:444
  104.5 4.3 %copy-start.6 = (f32[136,128]{1,0:T(8,128)}, f32[136,128]{1,0:T(8,128)S(1)}, u32[]{:S(2)}) copy-start(f32[136,128]{1,0:T(8,128)S(1)} %collective-permute-done.14.b_ref) | copy-start | bytes 208900
  107.5 1.3 copy-start.7
  108.8 0.6 copy-start.8
  115.1 1.2 copy-start.4

commit v7 on v6

--- a/solution.py
+++ b/solution.py
@@ -272,10 +272,11 @@
 
 
 def products_kernel(place_ref, count_ref, value_ref, sigma_ref, *refs):
-    pieces, out_ref, held_ref = refs[:N_ENS], refs[N_ENS], refs[N_ENS + 1]
-    for step, piece in enumerate(pieces):
+    pieces, out_ref, held_ref = refs[: N_ENS // 2], refs[N_ENS // 2], refs[N_ENS // 2 + 1]
+    for step in range(N_ENS):
         at = pl.multiple_of((place_ref[0] ^ step) * GROUP, GROUP)
-        held_ref[pl.ds(at, GROUP), :] = piece[...]
+        low = step % 2 * GROUP
+        held_ref[pl.ds(at, GROUP), :] = pieces[step // 2][low : low + GROUP, :]
     observed = held_ref[...]
     mean = jnp.sum(observed, axis=0, keepdims=True) / MEMBERS
     slot = lax.broadcasted_iota(jnp.int32, (1, SLOTS), 1)
@@ -298,7 +299,7 @@
     smem = pl.BlockSpec(memory_space=pltpu.SMEM)
     return pl.pallas_call(
         products_kernel,
-        in_specs=[smem, smem] + [vmem] * (2 + N_ENS),
+        in_specs=[smem, smem] + [vmem] * (2 + N_ENS // 2),
         out_specs=vmem,
         out_shape=jax.ShapeDtypeStruct((MEMBERS + 8, MEMBERS), jnp.float32),
         cost_estimate=cost(1),
@@ -370,6 +371,7 @@
             jax.ShapeDtypeStruct((MEMBERS, MEMBERS), jnp.bfloat16),
         ],
         cost_estimate=cost(1),
+        compiler_params=pltpu.CompilerParams(vmem_limit_bytes=60 * 1024 * 1024),
     )(*parts)
 
 
@@ -470,7 +472,8 @@
         moved, observed = forecast(chunk * share, own, base, top, bottom, shared, observed)
         fields.append(moved)
     early = exchange(fields[0])
-    pieces = [observed] + [swap(observed, "ens", step) for step in range(1, N_ENS)]
+    observed = jnp.concatenate([observed, swap(observed, "ens", 1)], axis=0)
+    pieces = [observed] + [swap(observed, "ens", step) for step in range(2, N_ENS, 2)]
     places = own_place.astype(jnp.int32).reshape(1)
     pieces, late, early = lax.optimization_barrier((pieces, fields[1], early))
     late = exchange(late)

time: 171 us -> 168 us (0.982)
  starting transfers between devices: 42.6 us -> 38.5 us
    ppermute x13 -> x10, starting transfers between devices: 17 us -> 12.4 us  [swap(): return lax.ppermute(value, axis, pairs)]
    ppermute x13 -> x10, waiting for transfers between devices: 12.9 us -> 11.8 us  [swap(): return lax.ppermute(value, axis, pairs)]
    unnamed x33 -> x28, local copies, waits for them, and re-layouts: 5.93 us -> 6.62 us
  transfers between devices with their start and end apart: 19 -> 16, of which waited for: 9 -> 9; matrix products, arithmetic and copies ran while one was open for 5% -> 6% of each run, Pallas kernels for 24% -> 24%
where the time goes in v7:
time: 168 us; the launch traced here: 167 us
  Pallas kernels  46.2 us (28%)
  blocking collectives  45.8 us (27%)
  starting transfers between devices  38.5 us (23%)
  local copies, waits for them, and re-layouts  20.3 us (12%)
  waiting for transfers between devices  14.2 us (8%)
    all_to_all x1, blocking collectives, on_device(): lax.all_to_all(value, 'ens', split_axis=0, concat_axis=0, tiled=True)  45.8 us
    pallas_call x2, Pallas kernels, forecast(): pl.pallas_call(kernel, grid=(steps,), in_specs=[pl.BlockSpec((STEP, ROWS,...  30.7 us
    all_to_all x2, starting transfers between devices, on_device(): lax.all_to_all(value, 'ens', split_axis=0, concat_axis=0, tiled=True)  13.2 us
    ppermute x10, starting transfers between devices, swap(): return lax.ppermute(value, axis, pairs)  12.4 us
    ppermute x10, waiting for transfers between devices, swap(): return lax.ppermute(value, axis, pairs)  11.8 us
    ppermute x2, starting transfers between devices, halo(): lax.ppermute(rows[0], 'map', down)  10.2 us
    unnamed x28, local copies, waits for them, and re-layouts  6.62 us
    pallas_call x1, Pallas kernels, update(): pl.pallas_call(update_kernel, grid=(2, 2), in_specs=[pl.BlockSpec((MEMBER...  5.68 us
  transfers between devices with their start and end apart: 16, of which 9 were waited for; matrix products, arithmetic and copies ran while one was open for 6% of the time, Pallas kernels for 24%

profile of v7, /device:TPU:1, one launch (start us, length us, event | category | flops | bytes accessed | tf_op | source)
XLA Modules:
  0.0 167.3 jit_solution(1096640625632111580)
XLA Ops:
  0.6 2.7 %copy.23 = bf16[16,16,4,1440]{3,1,2,0:T(8,128)(2,1)S(1)} copy(bf16[16,16,4,1440]{3,2,1,0:T(4,128)(2,1)} %param.9) | data formatting | bytes 5898240 | tf_op args[0]
  3.3 0.0 copy-start.1
  3.3 0.0 copy-start
  3.3 1.7 %fusion = (bf16[8,2,16,1440]{3,2,1,0:T(8,128)(2,1)}, bf16[8,2,16,1440]{3,2,1,0:T(8,128)(2,1)}, bf16[8,2,16,1440]{3,2,1,0:T(8,128)(2,1)}, bf16[8,2,16,1440]{3,2,1,0:T(8,128)(2,1)}) fusion(bf16[16,4,16,1440]{3,2,1,0:T(8,128)(2,1)S(1)} %bitcast.26), kind=kLoop, calls=%fused_computation.5 | loop fusion | bytes 5898240 | tf_op jit(solution)/shard_map/slice | solution.py:456
  5.0 1.4 copy-done.1
  6.4 5.4 %collective-permute-start.2 = (bf16[8,2,16,1440]{3,2,1,0:T(8,128)(2,1)}, bf16[8,2,16,1440]{3,2,1,0:T(8,128)(2,1)}, u32[]{:S(2)}, u32[]{:S(2)}) collective-permute-start(bf16[8,2,16,1440]{3,2,1,0:T(8,128)(2,1)} %get-tuple-element.68), channel_id=1, source_target_pairs={{0,1},{1,2},{2,3},{3,4},{4,5},{5,6},{6,7},{7,8},{8,9},{9,10},{10,1... | collective-permute-start | bytes 2211848 | tf_op jit(solution)/shard_map/ppermute | solution.py:459
  11.8 1.3 collective-permute-start.3
  13.1 5.7 %copy.16 = bf16[4,4,16,4,1440]{4,0,3,1,2:T(4,128)(2,1)} copy(bf16[4,4,16,4,1440]{4,3,2,1,0:T(4,128)(2,1)S(1)} %bitcast.25) | data formatting | bytes 5898240 | tf_op jit(solution)/shard_map/reshape | solution.py:466
  18.8 2.4 %shard_map.112 = (bf16[384,256]{1,0:T(8,128)(2,1)}, bf16[384,256]{1,0:T(8,128)(2,1)}, bf16[96,256]{1,0:T(8,128)(2,1)}, bf16[192,256]{1,0:T(8,128)(2,1)}, bf16[96...) custom-call(s32[1]{0:T(128)} %bitcast.4.tile_ref, ...), custom_call_target="tpu_custom_call" | custom-call | flops 3000000000 | bytes 3000000 | tf_op jit(solution)/shard_map/pallas_call | solution.py:107
  21.2 4.9 %collective-permute-start = (bf16[8,2,16,1440]{3,2,1,0:T(8,128)(2,1)}, bf16[8,2,16,1440]{3,2,1,0:T(8,128)(2,1)}, u32[]{:S(2)}, u32[]{:S(2)}) collective-permute-start(bf16[8,2,16,1440]{3,2,1,0:T(8,128)(2,1)} %get-tuple-element.44), channel_id=1, source_target_pairs={{0,1},{1,2},{2,3},{3,4},{4,5},{5,6},{6,7},{7,8},{8,9},{9,10},{10,1... | collective-permute-start | bytes 2211848 | tf_op jit(solution)/shard_map/ppermute | solution.py:459
  26.1 1.5 collective-permute-start.1
  27.5 2.2 %copy.18.refs_1_.base_ref = bf16[4,256,1440]{2,1,0:T(8,128)(2,1)} copy(bf16[4,256,1440]{2,0,1:T(4,128)(2,1)S(1)} %bitcast.29) | data formatting | bytes 5898240 | tf_op jit(solution)/shard_map/optimization_barrier | solution.py:468
  29.7 0.0 collective-permute-done.2.refs_2_
  29.7 2.4 %collective-permute-done.3.refs_3_ = bf16[8,2,16,1440]{3,2,1,0:T(8,128)(2,1)} collective-permute-done((bf16[8,2,16,1440]{3,2,1,0:T(8,128)(2,1)}, bf16[8,2,16,1440]{3,2,1,0:T(8,128)(2,1)}, u32[]{:S(2)}, u32[]{:S(2)}) %collective-permute-start.3) | collective-permute-done | bytes 737312 | tf_op jit(solution)/shard_map/ppermute | solution.py:459
  32.1 15.3 %shard_map.113 = (bf16[8,2,32,1440]{3,2,1,0:T(8,128)(2,1)}, f32[8,256]{1,0:T(8,128)}) custom-call(bf16[16,4,16,1440]{3,2,1,0:T(8,128)(2,1)} %bitcast.27, bf16[4,256,1440]{2,1,0:T(8,128)(2,1)} %copy.18.refs_1_.base_ref, bf16[8,2,16,1440]{3,2,1,0:T(8,128)(2,1)} %collective-permute-done.2.refs_2_, bf16[8,2,16,1440]{3,2,1,0:T(8,128)(2,1)} %collective-permute-done.3.refs_3_, ...), custom_call_target="tpu_custom_call" | custom-call | flops 16000000000 | bytes 16000000 | tf_op jit(solution)/shard_map/pallas_call | solution.py:250
  47.5 7.6 %all-to-all-start = ((bf16[8,2,32,1440]{3,2,1,0:T(8,128)(2,1)}), bf16[8,2,32,1440]{3,2,1,0:T(8,128)(2,1)S(1)}, u32[]{:S(2)}, u32[]{:S(2)}) async-start(bf16[8,2,32,1440]{3,2,1,0:T(8,128)(2,1)} %get-tuple-element.57), calls=%async_computation | async-start | bytes 3145728 | tf_op jit(solution)/shard_map/all_to_all | solution.py:449
  55.1 0.0 collective-permute-done.top_ref
  55.1 0.0 collective-permute-done.1.bottom_ref
  55.1 15.3 %shard_map.114 = (bf16[8,2,32,1440]{3,2,1,0:T(8,128)(2,1)}, f32[16,256]{1,0:T(8,128)}) custom-call(bf16[16,4,16,1440]{3,2,1,0:T(8,128)(2,1)} %bitcast.28, bf16[4,256,1440]{2,1,0:T(8,128)(2,1)} %copy.18.refs_1_.base_ref, bf16[8,2,16,1440]{3,2,1,0:T(8,128)(2,1)} %collective-permute-done.top_ref, bf16[8,2,16,1440]{3,2,1,0:T(8,128)(2,1)} %collective-permute-done.1.bottom_ref, ...), custom_call_target="tpu_custom_call" | custom-call | flops 16000000000 | bytes 16000000 | tf_op jit(solution)/shard_map/pallas_call | solution.py:250
  70.4 0.1 collective-permute-start.4
  70.5 0.7 constant_dynamic-update-slice_fusion.1
  71.2 0.7 collective-permute-done.4
  71.9 1.4 collective-permute-start.5
  73.3 2.4 %collective-permute-start.6 = (f32[32,256]{1,0:T(8,128)S(1)}, f32[32,256]{1,0:T(8,128)S(1)}, u32[]{:S(2)}, u32[]{:S(2)}) collective-permute-start(f32[32,256]{1,0:T(8,128)S(1)} %constant_dynamic-update-slice_fusion.refs_0_), channel_id=1, source_target_pairs={{0,64},{16,80},{32,96},{48,112},{64,0},{80,16},{96,32},{112,48},{1... | collective-permute-start | bytes 98312 | tf_op jit(solution)/shard_map/ppermute | solution.py:446
  75.7 0.1 collective-permute-start.7
  75.7 0.0 collective-permute-done.5.refs_1_
  75.7 1.9 %collective-permute-done.6.refs_2_ = f32[32,256]{1,0:T(8,128)S(1)} collective-permute-done((f32[32,256]{1,0:T(8,128)S(1)}, f32[32,256]{1,0:T(8,128)S(1)}, u32[]{:S(2)}, u32[]{:S(2)}) %collective-permute-start.6) | collective-permute-done | bytes 32800 | tf_op jit(solution)/shard_map/ppermute | solution.py:446
  77.7 1.9 %collective-permute-done.7.refs_3_ = f32[32,256]{1,0:T(8,128)S(1)} collective-permute-done((f32[32,256]{1,0:T(8,128)S(1)}, f32[32,256]{1,0:T(8,128)S(1)}, u32[]{:S(2)}, u32[]{:S(2)}) %collective-permute-start.7) | collective-permute-done | bytes 32800 | tf_op jit(solution)/shard_map/ppermute | solution.py:446
  79.6 5.5 %all-to-all-start.1 = ((bf16[8,2,32,1440]{3,2,1,0:T(8,128)(2,1)}), bf16[8,2,32,1440]{3,2,1,0:T(8,128)(2,1)S(1)}, u32[]{:S(2)}, u32[]{:S(2)}) async-start(bf16[8,2,32,1440]{3,2,1,0:T(8,128)(2,1)} %get-tuple-element.64), calls=%async_computation.1 | async-start | bytes 3145728 | tf_op jit(solution)/shard_map/all_to_all | solution.py:449
  85.9 1.8 %shard_map.115 = f32[136,128]{1,0:T(8,128)} custom-call(s32[1]{0:T(128)} %bitcast.place_ref, s32[1]{0:T(128)S(6)} %copy.25.count_ref, f32[1,256]{1,0:T(1,128)} %bitcast.35, f32[1,256]{1,0:T(1,128)} %bitcast.36, f32[32,256]{1,0:T(8,128)} %copy-done.6, f32[32,256]{1,0:T(8,128)} %copy-done.10, f32[32,256]{1,0:T(8,128)} %copy-done.11, f32[32,256]{1,0:T(8,128)} %copy-done.12), custom_call_target="tpu_custom_call" | custom-call | flops 1000000000 | bytes 1000000 | tf_op jit(solution)/shard_map/pallas_call | solution.py:300
  87.7 3.2 %collective-permute-start.10 = (f32[136,128]{1,0:T(8,128)}, f32[136,128]{1,0:T(8,128)S(1)}, u32[]{:S(2)}, u32[]{:S(2)}) collective-permute-start(f32[136,128]{1,0:T(8,128)} %shard_map.115), channel_id=1, source_target_pairs={{0,3},{1,2},{2,1},{3,0},{4,7},{5,6},{6,5},{7,4},{8,11},{9,10},{10,... | collective-permute-start | bytes 208904 | tf_op jit(solution)/shard_map/ppermute | solution.py:446
  90.9 1.3 collective-permute-start.9
  92.2 1.4 collective-permute-done.10
  93.5 1.0 collective-permute-done.8
  94.6 1.2 collective-permute-done.9
  95.8 0.9 add_add_fusion.a_ref
  96.7 0.0 copy-start.5
  96.7 1.4 collective-permute-start.11
  98.1 1.6 collective-permute-start.12
  99.6 1.0 collective-permute-start.13
  100.6 2.4 %collective-permute-done.12.c_ref = f32[136,128]{1,0:T(8,128)S(1)} collective-permute-done((f32[136,128]{1,0:T(8,128)S(1)}, f32[136,128]{1,0:T(8,128)S(1)}, u32[]{:S(2)}, u32[]{:S(2)}) %collective-permute-start.12) | collective-permute-done | bytes 69664 | tf_op jit(solution)/shard_map/ppermute | solution.py:446
  103.0 1.3 collective-permute-done.13.d_ref
  104.3 0.6 copy-done.9
  104.9 5.7 %shard_map.116 = (f32[128,128]{1,0:T(8,128)}, f32[1,128]{1,0:T(1,128)}, bf16[128,128]{1,0:T(8,128)(2,1)}) custom-call(f32[136,128]{1,0:T(8,128)} %copy-done.5, f32[136,128]{1,0:T(8,128)} %copy-done.7, f32[136,128]{1,0:T(8,128)} %copy-done.8, f32[136,128]{1,0:T(8,128)} %copy-done.9), custom_call_target="tpu_custom_call" | custom-call | flops 1000000000 | bytes 1000000 | tf_op jit(solution)/shard_map/pallas_call | solution.py:364
  110.6 1.1 copy-done.4
  111.7 5.7 %shard_map.117 = bf16[8,2,64,1440]{3,2,1,0:T(8,128)(2,1)} custom-call(bf16[128,128]{1,0:T(8,128)(2,1)} %get-tuple-element.62.transform_ref, bf16[8,2,32,1440]{3,2,1,0:T(8,128)(2,1)} %copy-done.3, bf16[8,2,32,1440]{3,2,1,0:T(8,128)(2,1)} %copy-done.4), custom_call_target="tpu_custom_call" | custom-call | flops 4000000000 | bytes 4000000 | tf_op jit(solution)/shard_map/pallas_call | solution.py:413
  117.4 45.8 %all_to_all.15 = bf16[8,2,64,1440]{3,2,1,0:T(8,128)(2,1)S(1)} all-to-all(bf16[8,2,64,1440]{3,2,1,0:T(8,128)(2,1)} %shard_map.117), channel_id=1, replica_groups=mesh['ens'=8,'map'=16] {'ens'}, dimensions={0} | all-to-all | bytes 5898240 | tf_op jit(solution)/shard_map/all_to_all | solution.py:449
  163.2 4.1 %copy.22 = bf16[16,4,16,1440]{3,1,0,2:T(4,128)(2,1)} copy(bf16[16,4,16,1440]{3,2,1,0:T(8,128)(2,1)S(1)} %bitcast.30) | data formatting | bytes 5898240 | tf_op jit(solution)/shard_map/reshape | solution.py:487
  (25 shorter events, 0.1 us)
Async XLA Ops:
  3.3 3.2 %copy-start.1 = (bf16[16,16,4,1440]{3,1,2,0:T(8,128)(2,1)}, bf16[16,16,4,1440]{3,1,2,0:T(8,128)(2,1)S(1)}, u32[]{:S(2)}) copy-start(bf16[16,16,4,1440]{3,1,2,0:T(8,128)(2,1)S(1)} %copy.23) | copy-start | bytes 8847364
  3.3 9.8 %copy-start = (bf16[16,16,4,1440]{3,2,1,0:T(4,128)(2,1)S(1)}, bf16[16,16,4,1440]{3,2,1,0:T(4,128)(2,1)}, u32[]{:S(2)}) copy-start(bf16[16,16,4,1440]{3,2,1,0:T(4,128)(2,1)} %param.9) | copy-start | bytes 8847364
  6.4 23.3 %collective-permute-start.2 = (bf16[8,2,16,1440]{3,2,1,0:T(8,128)(2,1)}, bf16[8,2,16,1440]{3,2,1,0:T(8,128)(2,1)}, u32[]{:S(2)}, u32[]{:S(2)}) collective-permute-start(bf16[8,2,16,1440]{3,2,1,0:T(8,128)(2,1)} %get-tuple-element.68), channel_id=1, source_target_pairs={{0,1},{1,2},{2,3},{3,4},{4,5},{5,6},{6,7},{7,8},{8,9},{9,10},{10,1... | collective-permute-start | bytes 2211848 | tf_op jit(solution)/shard_map/ppermute | solution.py:459
  11.8 20.3 %collective-permute-start.3 = (bf16[8,2,16,1440]{3,2,1,0:T(8,128)(2,1)}, bf16[8,2,16,1440]{3,2,1,0:T(8,128)(2,1)}, u32[]{:S(2)}, u32[]{:S(2)}) collective-permute-start(bf16[8,2,16,1440]{3,2,1,0:T(8,128)(2,1)} %get-tuple-element.67), channel_id=1, source_target_pairs={{1,0},{2,1},{3,2},{4,3},{5,4},{6,5},{7,6},{8,7},{9,8},{10,9},{11,1... | collective-permute-start | bytes 2211848 | tf_op jit(solution)/shard_map/ppermute | solution.py:459
  18.8 8.7 %copy-start.2 = (bf16[4,4,16,4,1440]{4,0,3,1,2:T(4,128)(2,1)S(1)}, bf16[4,4,16,4,1440]{4,0,3,1,2:T(4,128)(2,1)}, u32[]{:S(2)}) copy-start(bf16[4,4,16,4,1440]{4,0,3,1,2:T(4,128)(2,1)} %copy.16) | copy-start | bytes 8847364
  21.2 33.9 %collective-permute-start = (bf16[8,2,16,1440]{3,2,1,0:T(8,128)(2,1)}, bf16[8,2,16,1440]{3,2,1,0:T(8,128)(2,1)}, u32[]{:S(2)}, u32[]{:S(2)}) collective-permute-start(bf16[8,2,16,1440]{3,2,1,0:T(8,128)(2,1)} %get-tuple-element.44), channel_id=1, source_target_pairs={{0,1},{1,2},{2,3},{3,4},{4,5},{5,6},{6,7},{7,8},{8,9},{9,10},{10,1... | collective-permute-start | bytes 2211848 | tf_op jit(solution)/shard_map/ppermute | solution.py:459
  26.1 29.0 %collective-permute-start.1 = (bf16[8,2,16,1440]{3,2,1,0:T(8,128)(2,1)}, bf16[8,2,16,1440]{3,2,1,0:T(8,128)(2,1)}, u32[]{:S(2)}, u32[]{:S(2)}) collective-permute-start(bf16[8,2,16,1440]{3,2,1,0:T(8,128)(2,1)} %get-tuple-element.45), channel_id=1, source_target_pairs={{1,0},{2,1},{3,2},{4,3},{5,4},{6,5},{7,6},{8,7},{9,8},{10,9},{11,1... | collective-permute-start | bytes 2211848 | tf_op jit(solution)/shard_map/ppermute | solution.py:459
  47.5 32.2 %all-to-all-start = ((bf16[8,2,32,1440]{3,2,1,0:T(8,128)(2,1)}), bf16[8,2,32,1440]{3,2,1,0:T(8,128)(2,1)S(1)}, u32[]{:S(2)}, u32[]{:S(2)}) async-start(bf16[8,2,32,1440]{3,2,1,0:T(8,128)(2,1)} %get-tuple-element.57), calls=%async_computation | async-start | bytes 3145728 | tf_op jit(solution)/shard_map/all_to_all | solution.py:449
  70.4 1.5 collective-permute-start.4
  71.9 14.0 %copy-start.6 = (f32[32,256]{1,0:T(8,128)}, f32[32,256]{1,0:T(8,128)S(1)}, u32[]{:S(2)}) copy-start(f32[32,256]{1,0:T(8,128)S(1)} %constant_dynamic-update-slice_fusion.refs_0_) | copy-start | bytes 98308
  71.9 3.9 %collective-permute-start.5 = (f32[32,256]{1,0:T(8,128)S(1)}, f32[32,256]{1,0:T(8,128)S(1)}, u32[]{:S(2)}, u32[]{:S(2)}) collective-permute-start(f32[32,256]{1,0:T(8,128)S(1)} %constant_dynamic-update-slice_fusion.refs_0_), channel_id=1, source_target_pairs={{0,32},{16,48},{32,0},{48,16},{64,96},{80,112},{96,64},{112,80},{1... | collective-permute-start | bytes 98312 | tf_op jit(solution)/shard_map/ppermute | solution.py:446
  73.3 4.4 %collective-permute-start.6 = (f32[32,256]{1,0:T(8,128)S(1)}, f32[32,256]{1,0:T(8,128)S(1)}, u32[]{:S(2)}, u32[]{:S(2)}) collective-permute-start(f32[32,256]{1,0:T(8,128)S(1)} %constant_dynamic-update-slice_fusion.refs_0_), channel_id=1, source_target_pairs={{0,64},{16,80},{32,96},{48,112},{64,0},{80,16},{96,32},{112,48},{1... | collective-permute-start | bytes 98312 | tf_op jit(solution)/shard_map/ppermute | solution.py:446
  75.7 4.0 %collective-permute-start.7 = (f32[32,256]{1,0:T(8,128)S(1)}, f32[32,256]{1,0:T(8,128)S(1)}, u32[]{:S(2)}, u32[]{:S(2)}) collective-permute-start(f32[32,256]{1,0:T(8,128)S(1)} %constant_dynamic-update-slice_fusion.refs_0_), channel_id=1, source_target_pairs={{0,96},{16,112},{32,64},{48,80},{64,32},{80,48},{96,0},{112,16},{1... | collective-permute-start | bytes 98312 | tf_op jit(solution)/shard_map/ppermute | solution.py:446
  75.7 10.1 %copy-start.10 = (f32[32,256]{1,0:T(8,128)}, f32[32,256]{1,0:T(8,128)S(1)}, u32[]{:S(2)}) copy-start(f32[32,256]{1,0:T(8,128)S(1)} %collective-permute-done.5.refs_1_) | copy-start | bytes 98308
  77.7 8.2 %copy-start.11 = (f32[32,256]{1,0:T(8,128)}, f32[32,256]{1,0:T(8,128)S(1)}, u32[]{:S(2)}) copy-start(f32[32,256]{1,0:T(8,128)S(1)} %collective-permute-done.6.refs_2_) | copy-start | bytes 98308
  79.6 6.2 %copy-start.12 = (f32[32,256]{1,0:T(8,128)}, f32[32,256]{1,0:T(8,128)S(1)}, u32[]{:S(2)}) copy-start(f32[32,256]{1,0:T(8,128)S(1)} %collective-permute-done.7.refs_3_) | copy-start | bytes 98308
  79.6 8.0 %copy-start.3 = (bf16[8,2,32,1440]{3,2,1,0:T(8,128)(2,1)}, bf16[8,2,32,1440]{3,2,1,0:T(8,128)(2,1)S(1)}, u32[]{:S(2)}) copy-start(bf16[8,2,32,1440]{3,2,1,0:T(8,128)(2,1)S(1)} %all-to-all-done.early_ref) | copy-start | bytes 4423684
  79.6 31.0 %all-to-all-start.1 = ((bf16[8,2,32,1440]{3,2,1,0:T(8,128)(2,1)}), bf16[8,2,32,1440]{3,2,1,0:T(8,128)(2,1)S(1)}, u32[]{:S(2)}, u32[]{:S(2)}) async-start(bf16[8,2,32,1440]{3,2,1,0:T(8,128)(2,1)} %get-tuple-element.64), calls=%async_computation.1 | async-start | bytes 3145728 | tf_op jit(solution)/shard_map/all_to_all | solution.py:449
  87.7 5.9 %collective-permute-start.10 = (f32[136,128]{1,0:T(8,128)}, f32[136,128]{1,0:T(8,128)S(1)}, u32[]{:S(2)}, u32[]{:S(2)}) collective-permute-start(f32[136,128]{1,0:T(8,128)} %shard_map.115), channel_id=1, source_target_pairs={{0,3},{1,2},{2,1},{3,0},{4,7},{5,6},{6,5},{7,4},{8,11},{9,10},{10,... | collective-permute-start | bytes 208904 | tf_op jit(solution)/shard_map/ppermute | solution.py:446
  90.9 3.7 %collective-permute-start.8 = (f32[136,128]{1,0:T(8,128)}, f32[136,128]{1,0:T(8,128)S(1)}, u32[]{:S(2)}, u32[]{:S(2)}) collective-permute-start(f32[136,128]{1,0:T(8,128)} %shard_map.115), channel_id=1, source_target_pairs={{0,1},{1,0},{2,3},{3,2},{4,5},{5,4},{6,7},{7,6},{8,9},{9,8},{10,11... | collective-permute-start | bytes 208904 | tf_op jit(solution)/shard_map/ppermute | solution.py:446
  90.9 4.9 %collective-permute-start.9 = (f32[136,128]{1,0:T(8,128)}, f32[136,128]{1,0:T(8,128)S(1)}, u32[]{:S(2)}, u32[]{:S(2)}) collective-permute-start(f32[136,128]{1,0:T(8,128)} %shard_map.115), channel_id=1, source_target_pairs={{0,2},{1,3},{2,0},{3,1},{4,6},{5,7},{6,4},{7,5},{8,10},{9,11},{10,... | collective-permute-start | bytes 208904 | tf_op jit(solution)/shard_map/ppermute | solution.py:446
  96.7 7.6 %copy-start.5 = (f32[136,128]{1,0:T(8,128)}, f32[136,128]{1,0:T(8,128)S(1)}, u32[]{:S(2)}) copy-start(f32[136,128]{1,0:T(8,128)S(1)} %add_add_fusion.a_ref) | copy-start | bytes 208900
  96.7 3.9 %collective-permute-start.11 = (f32[136,128]{1,0:T(8,128)S(1)}, f32[136,128]{1,0:T(8,128)S(1)}, u32[]{:S(2)}, u32[]{:S(2)}) collective-permute-start(f32[136,128]{1,0:T(8,128)S(1)} %add_add_fusion.a_ref), channel_id=1, source_target_pairs={{0,4},{1,5},{2,6},{3,7},{4,0},{5,1},{6,2},{7,3},{8,12},{9,13},{10,... | collective-permute-start | bytes 208904 | tf_op jit(solution)/shard_map/ppermute | solution.py:446
  98.1 5.0 %collective-permute-start.12 = (f32[136,128]{1,0:T(8,128)S(1)}, f32[136,128]{1,0:T(8,128)S(1)}, u32[]{:S(2)}, u32[]{:S(2)}) collective-permute-start(f32[136,128]{1,0:T(8,128)S(1)} %add_add_fusion.a_ref), channel_id=1, source_target_pairs={{0,8},{1,9},{2,10},{3,11},{4,12},{5,13},{6,14},{7,15},{8,0},{9,1},... | collective-permute-start | bytes 208904 | tf_op jit(solution)/shard_map/ppermute | solution.py:446
  99.6 4.7 %collective-permute-start.13 = (f32[136,128]{1,0:T(8,128)S(1)}, f32[136,128]{1,0:T(8,128)S(1)}, u32[]{:S(2)}, u32[]{:S(2)}) collective-permute-start(f32[136,128]{1,0:T(8,128)S(1)} %add_add_fusion.a_ref), channel_id=1, source_target_pairs={{0,12},{1,13},{2,14},{3,15},{4,8},{5,9},{6,10},{7,11},{8,4},{9,5},... | collective-permute-start | bytes 208904 | tf_op jit(solution)/shard_map/ppermute | solution.py:446
  100.6 3.7 %copy-start.7 = (f32[136,128]{1,0:T(8,128)}, f32[136,128]{1,0:T(8,128)S(1)}, u32[]{:S(2)}) copy-start(f32[136,128]{1,0:T(8,128)S(1)} %collective-permute-done.11.b_ref) | copy-start | bytes 208900
  103.0 1.3 copy-start.8
  104.3 0.6 copy-start.9
  110.6 1.1 copy-start.4

commit v8 on v7

--- a/solution.py
+++ b/solution.py
@@ -187,27 +187,33 @@
             )
 
     sub = lax.broadcasted_iota(jnp.int32, (8, RING), 0)
-    pairs = []
-    for pair in range(STEP // 2):
-        sources = [*changes(2 * pair), *changes(2 * pair + 1)]
-        blocks = []
-        for field in range(FIELDS):
-            at, by = field // 4 * 8, field % 4 * 2
-            moved = [
-                pltpu.roll(source[at : at + 8], (2 * k - by) % 8, 0) if (2 * k - by) % 8 else source[at : at + 8]
-                for k, source in enumerate(sources)
-            ]
+    members = [list(changes(member)) for member in range(STEP)]
+    for field in range(FIELDS):
+        at, by = field // 4 * 8, field % 4 * 2
+        halves = []
+        for pair in range(2):
+            moved = []
+            for k, parts in enumerate(members):
+                rows = parts[pair][at : at + 8]
+                turn = (2 * k - by) % 8
+                moved.append(pltpu.roll(rows, turn, 0) if turn else rows)
             first = jnp.where(sub < 2, moved[0], moved[1])
             last = jnp.where(sub < 6, moved[2], moved[3])
-            blocks.append(jnp.where(sub < 4, first, last))
-        pairs.append(blocks)
-    for field in range(FIELDS):
+            halves.append(jnp.where(sub < 4, first, last))
         low, high = field * 16, field * 16 + 16
         base = base_ref[0, low:high, :].astype(jnp.float32) + bias_ref[low:high, :]
         base = jnp.concatenate([base, base[:, : RING - LON]], axis=1)
-        change = jnp.concatenate([blocks[field] for blocks in pairs], axis=0)
-        own = (base + change).astype(jnp.bfloat16)
-        fields_ref[field // 2, field % 2] = own[:, :LON]
+        a, b = base[:8], base[8:]
+        a4, a6 = pltpu.roll(a, 4, 0), pltpu.roll(a, 6, 0)
+        b2, b4 = pltpu.roll(b, 2, 0), pltpu.roll(b, 4, 0)
+        choose = lambda *four: jnp.where(
+            sub < 4, jnp.where(sub < 2, *four[:2]), jnp.where(sub < 6, *four[2:])
+        )
+        base = jnp.concatenate([choose(a, a6, b4, b2), choose(a6, a4, b2, b)], axis=0)
+        own = (base + jnp.concatenate(halves, axis=0)).astype(jnp.bfloat16)
+        for pair in range(2):
+            block = own[8 * pair : 8 * pair + 8, :LON]
+            fields_ref[field // 2, field % 2 * 2 + pair, 0] = block
         held_ref[pl.ds(pl.multiple_of(step * 16 * FIELDS + low, 16), 16), :] = own
 
     @pl.when(step == pl.num_programs(0) - 1)
@@ -215,11 +221,11 @@
         rows = held_ref.shape[0]
         picked = jnp.dot(held_ref[...], picks_ref[...], preferred_element_type=jnp.float32)
         row = lax.broadcasted_iota(jnp.int32, (rows, SLOTS), 0)
-        here = row % 256 // 16 * ROWS + row % ROWS == plane_ref[...]
+        here = row % 256 // 8 * 2 + row % 2 == plane_ref[...]
         found = jnp.where(here, picked, 0.0).astype(jnp.bfloat16)
         count = rows // PLANES
         column = lax.broadcasted_iota(jnp.int32, (count, rows), 1)
-        member = column // 256 * STEP + column % 16 // ROWS
+        member = column // 256 * STEP + column % 8 // 2
         mine = member == lax.broadcasted_iota(jnp.int32, (count, rows), 0)
         seen = jnp.dot(
             mine.astype(jnp.bfloat16), found, preferred_element_type=jnp.float32
@@ -258,11 +264,11 @@
         ]
         + [whole(array) for array in shared],
         out_specs=[
-            pl.BlockSpec((N_ENS, 2, 16, LON), lambda m: (0, 0, m, 0)),
+            pl.BlockSpec((N_ENS, 4, 1, 8, LON), lambda m: (0, 0, m, 0, 0)),
             pl.BlockSpec((seen, SLOTS), lambda m: (0, 0)),
         ],
         out_shape=[
-            jax.ShapeDtypeStruct((N_ENS, 2, count * ROWS, LON), jnp.bfloat16),
+            jax.ShapeDtypeStruct((N_ENS, 4, steps, 8, LON), jnp.bfloat16),
             jax.ShapeDtypeStruct((seen, SLOTS), jnp.float32),
         ],
         scratch_shapes=[pltpu.VMEM((count * PLANES, RING), jnp.bfloat16)],
@@ -376,16 +382,16 @@
 
 
 def update_kernel(transform_ref, early_ref, late_ref, out_ref, spread_ref):
-    rows = MEMBERS * ROWS
+    rows = MEMBERS * 2
     half = rows // 2
 
-    @pl.when((pl.program_id(0) == 0) & (pl.program_id(1) == 0))
+    @pl.when(pl.program_id(0) == 0)
     def _():
         shape = (rows, MEMBERS)
         row = lax.broadcasted_iota(jnp.int32, shape, 0)
         column = lax.broadcasted_iota(jnp.int32, shape, 1)
-        held = row % half // 32 * GROUP + row // half * 8 + row % 32 // ROWS
-        wanted = row // 64 * GROUP + row % GROUP
+        held = row % half // 16 * GROUP + row // half * 8 + row % 16 // 2
+        wanted = row // 32 * GROUP + row % GROUP
         repeat = (wanted == column).astype(jnp.bfloat16)
         placed = (held == column).astype(jnp.bfloat16)
         tall = jnp.dot(repeat, transform_ref[...], preferred_element_type=jnp.float32)
@@ -395,33 +401,31 @@
             (((1,), (1,)), ((), ())),
             preferred_element_type=jnp.float32,
         )
-        own = lax.broadcasted_iota(jnp.int32, (rows, rows), 0) // GROUP % ROWS
-        same = own == lax.broadcasted_iota(jnp.int32, (rows, rows), 1) % ROWS
+        own = lax.broadcasted_iota(jnp.int32, (rows, rows), 0) // GROUP % 2
+        same = own == lax.broadcasted_iota(jnp.int32, (rows, rows), 1) % 2
         spread_ref[...] = jnp.where(same, wide, 0.0).astype(jnp.bfloat16)
 
-    width = early_ref.shape[-1]
     fields = jnp.concatenate(
-        [early_ref[:, 0].reshape(half, width), late_ref[:, 0].reshape(half, width)], axis=0
+        [early_ref[:, 0].reshape(half, LON), late_ref[:, 0].reshape(half, LON)], axis=0
     )
     mixed = jnp.dot(spread_ref[...], fields, preferred_element_type=jnp.float32)
-    out_ref[:, 0] = mixed.astype(jnp.bfloat16).reshape(N_ENS, GROUP * ROWS, width)
+    out_ref[:, 0] = mixed.astype(jnp.bfloat16).reshape(N_ENS, GROUP * 2, LON)
 
 
 def update(transform, early, late):
-    rows = MEMBERS * ROWS
-    half = pl.BlockSpec((N_ENS, 1, 8 * ROWS, RING // 2), lambda c, x: (0, c, 0, x))
+    rows = MEMBERS * 2
+    half = pl.BlockSpec((N_ENS, 1, 16, LON), lambda q: (0, q, 0, 0))
+    joined = (N_ENS, 4, 16, LON)
     return pl.pallas_call(
         update_kernel,
-        grid=(2, 2),
-        in_specs=[pl.BlockSpec((MEMBERS, MEMBERS), lambda c, x: (0, 0)), half, half],
-        out_specs=pl.BlockSpec(
-            (N_ENS, 1, GROUP * ROWS, RING // 2), lambda c, x: (0, c, 0, x)
-        ),
-        out_shape=jax.ShapeDtypeStruct((N_ENS, 2, GROUP * ROWS, LON), jnp.bfloat16),
+        grid=(4,),
+        in_specs=[pl.BlockSpec((MEMBERS, MEMBERS), lambda q: (0, 0)), half, half],
+        out_specs=pl.BlockSpec((N_ENS, 1, GROUP * 2, LON), lambda q: (0, q, 0, 0)),
+        out_shape=jax.ShapeDtypeStruct((N_ENS, 4, GROUP * 2, LON), jnp.bfloat16),
         scratch_shapes=[pltpu.VMEM((rows, rows), jnp.bfloat16)],
-        cost_estimate=cost(4),
+        cost_estimate=cost(3),
         compiler_params=pltpu.CompilerParams(vmem_limit_bytes=VMEM_LIMIT),
-    )(transform, early, late)
+    )(transform, early.reshape(joined), late.reshape(joined))
 
 
 def on_device(

time: 168 us -> 168 us (level)
  transfers between devices with their start and end apart: 16 -> 16, of which waited for: 9 -> 9; matrix products, arithmetic and copies ran while one was open for 6% -> 6% of each run, Pallas kernels for 24% -> 25%
where the time goes in v8:
time: 168 us
  Pallas kernels  46.5 us (28%)
  blocking collectives  45.8 us (27%)
  starting transfers between devices  38.5 us (23%)
  local copies, waits for them, and re-layouts  20.3 us (12%)
  waiting for transfers between devices  14.2 us (8%)
    all_to_all x1, blocking collectives, on_device(): lax.all_to_all(value, 'ens', split_axis=0, concat_axis=0, tiled=True)  45.8 us
    pallas_call x2, Pallas kernels, forecast(): pl.pallas_call(kernel, grid=(steps,), in_specs=[pl.BlockSpec((STEP, ROWS,...  31.5 us
    all_to_all x2, starting transfers between devices, on_device(): lax.all_to_all(value, 'ens', split_axis=0, concat_axis=0, tiled=True)  13.2 us
    ppermute x10, starting transfers between devices, swap(): return lax.ppermute(value, axis, pairs)  12.4 us
    ppermute x10, waiting for transfers between devices, swap(): return lax.ppermute(value, axis, pairs)  11.8 us
    ppermute x2, starting transfers between devices, halo(): lax.ppermute(rows[0], 'map', down)  10.2 us
    unnamed x28, local copies, waits for them, and re-layouts  6.62 us
    reshape x1, local copies, waits for them, and re-layouts, on_device(): ensemble_weather.reshape(GROUP // STEP, STEP, FIELDS, ROWS, LON)  5.67 us
  transfers between devices with their start and end apart: 16, of which 9 were waited for; matrix products, arithmetic and copies ran while one was open for 6% of the time, Pallas kernels for 25%

profile of v8, /device:TPU:1, one launch (start us, length us, event | category | flops | bytes accessed | tf_op | source)
XLA Modules:
  0.0 167.7 jit_solution(18398554043161052077)
XLA Ops:
  0.6 2.7 %copy.23 = bf16[16,16,4,1440]{3,1,2,0:T(8,128)(2,1)S(1)} copy(bf16[16,16,4,1440]{3,2,1,0:T(4,128)(2,1)} %param.9) | data formatting | bytes 5898240 | tf_op args[0]
  3.3 0.0 copy-start.1
  3.3 0.0 copy-start
  3.3 1.7 %fusion = (bf16[8,2,16,1440]{3,2,1,0:T(8,128)(2,1)}, bf16[8,2,16,1440]{3,2,1,0:T(8,128)(2,1)}, bf16[8,2,16,1440]{3,2,1,0:T(8,128)(2,1)}, bf16[8,2,16,1440]{3,2,1,0:T(8,128)(2,1)}) fusion(bf16[16,4,16,1440]{3,2,1,0:T(8,128)(2,1)S(1)} %bitcast.28), kind=kLoop, calls=%fused_computation.5 | loop fusion | bytes 5898240 | tf_op jit(solution)/shard_map/slice | solution.py:460
  5.0 1.4 copy-done.1
  6.4 5.4 %collective-permute-start.2 = (bf16[8,2,16,1440]{3,2,1,0:T(8,128)(2,1)}, bf16[8,2,16,1440]{3,2,1,0:T(8,128)(2,1)}, u32[]{:S(2)}, u32[]{:S(2)}) collective-permute-start(bf16[8,2,16,1440]{3,2,1,0:T(8,128)(2,1)} %get-tuple-element.68), channel_id=1, source_target_pairs={{0,1},{1,2},{2,3},{3,4},{4,5},{5,6},{6,7},{7,8},{8,9},{9,10},{10,1... | collective-permute-start | bytes 2211848 | tf_op jit(solution)/shard_map/ppermute | solution.py:463
  11.8 1.3 collective-permute-start.3
  13.1 5.7 %copy.16 = bf16[4,4,16,4,1440]{4,0,3,1,2:T(4,128)(2,1)} copy(bf16[4,4,16,4,1440]{4,3,2,1,0:T(4,128)(2,1)S(1)} %bitcast.27) | data formatting | bytes 5898240 | tf_op jit(solution)/shard_map/reshape | solution.py:470
  18.8 2.4 %shard_map.112 = (bf16[384,256]{1,0:T(8,128)(2,1)}, bf16[384,256]{1,0:T(8,128)(2,1)}, bf16[96,256]{1,0:T(8,128)(2,1)}, bf16[192,256]{1,0:T(8,128)(2,1)}, bf16[96...) custom-call(s32[1]{0:T(128)} %bitcast.4.tile_ref, ...), custom_call_target="tpu_custom_call" | custom-call | flops 3000000000 | bytes 3000000 | tf_op jit(solution)/shard_map/pallas_call | solution.py:107
  21.2 4.9 %collective-permute-start = (bf16[8,2,16,1440]{3,2,1,0:T(8,128)(2,1)}, bf16[8,2,16,1440]{3,2,1,0:T(8,128)(2,1)}, u32[]{:S(2)}, u32[]{:S(2)}) collective-permute-start(bf16[8,2,16,1440]{3,2,1,0:T(8,128)(2,1)} %get-tuple-element.44), channel_id=1, source_target_pairs={{0,1},{1,2},{2,3},{3,4},{4,5},{5,6},{6,7},{7,8},{8,9},{9,10},{10,1... | collective-permute-start | bytes 2211848 | tf_op jit(solution)/shard_map/ppermute | solution.py:463
  26.1 1.5 collective-permute-start.1
  27.5 2.2 %copy.18.refs_1_.base_ref = bf16[4,256,1440]{2,1,0:T(8,128)(2,1)} copy(bf16[4,256,1440]{2,0,1:T(4,128)(2,1)S(1)} %bitcast.31) | data formatting | bytes 5898240 | tf_op jit(solution)/shard_map/optimization_barrier | solution.py:472
  29.7 0.0 collective-permute-done.2.refs_2_
  29.7 2.4 %collective-permute-done.3.refs_3_ = bf16[8,2,16,1440]{3,2,1,0:T(8,128)(2,1)} collective-permute-done((bf16[8,2,16,1440]{3,2,1,0:T(8,128)(2,1)}, bf16[8,2,16,1440]{3,2,1,0:T(8,128)(2,1)}, u32[]{:S(2)}, u32[]{:S(2)}) %collective-permute-start.3) | collective-permute-done | bytes 737312 | tf_op jit(solution)/shard_map/ppermute | solution.py:463
  32.1 15.8 %shard_map.113 = (bf16[8,4,2,8,1440]{4,3,2,1,0:T(8,128)(2,1)}, f32[8,256]{1,0:T(8,128)}) custom-call(bf16[16,4,16,1440]{3,2,1,0:T(8,128)(2,1)} %bitcast.29, bf16[4,256,1440]{2,1,0:T(8,128)(2,1)} %copy.18.refs_1_.base_ref, bf16[8,2,16,1440]{3,2,1,0:T(8,128)(2,1)} %collective-permute-done.2.refs_2_, bf16[8,2,16,1440]{3,2,1,0:T(8,128)(2,1)} %collective-permute-done.3.refs_3_, ...), custom_call_target="tpu_custom_call" | custom-call | flops 16000000000 | bytes 16000000 | tf_op jit(solution)/shard_map/pallas_call | solution.py:256
  47.9 7.6 %all-to-all-start = ((bf16[8,4,2,8,1440]{4,3,2,1,0:T(8,128)(2,1)}), bf16[8,4,2,8,1440]{4,3,2,1,0:T(8,128)(2,1)S(1)}, u32[]{:S(2)}, u32[]{:S(2)}) async-start(bf16[8,4,2,8,1440]{4,3,2,1,0:T(8,128)(2,1)} %get-tuple-element.57), calls=%async_computation | async-start | bytes 3145728 | tf_op jit(solution)/shard_map/all_to_all | solution.py:453
  55.5 15.8 %shard_map.114 = (bf16[8,4,2,8,1440]{4,3,2,1,0:T(8,128)(2,1)}, f32[16,256]{1,0:T(8,128)}) custom-call(bf16[16,4,16,1440]{3,2,1,0:T(8,128)(2,1)} %bitcast.30, bf16[4,256,1440]{2,1,0:T(8,128)(2,1)} %copy.18.refs_1_.base_ref, bf16[8,2,16,1440]{3,2,1,0:T(8,128)(2,1)} %collective-permute-done.top_ref, bf16[8,2,16,1440]{3,2,1,0:T(8,128)(2,1)} %collective-permute-done.1.bottom_ref, ...), custom_call_target="tpu_custom_call" | custom-call | flops 16000000000 | bytes 16000000 | tf_op jit(solution)/shard_map/pallas_call | solution.py:256
  71.3 0.1 collective-permute-start.4
  71.4 0.7 constant_dynamic-update-slice_fusion.1
  72.1 0.7 collective-permute-done.4
  72.8 1.4 collective-permute-start.5
  74.2 2.4 %collective-permute-start.6 = (f32[32,256]{1,0:T(8,128)S(1)}, f32[32,256]{1,0:T(8,128)S(1)}, u32[]{:S(2)}, u32[]{:S(2)}) collective-permute-start(f32[32,256]{1,0:T(8,128)S(1)} %constant_dynamic-update-slice_fusion.refs_0_), channel_id=1, source_target_pairs={{0,64},{16,80},{32,96},{48,112},{64,0},{80,16},{96,32},{112,48},{1... | collective-permute-start | bytes 98312 | tf_op jit(solution)/shard_map/ppermute | solution.py:450
  76.6 0.1 collective-permute-start.7
  76.7 0.0 collective-permute-done.5.refs_1_
  76.7 1.9 %collective-permute-done.6.refs_2_ = f32[32,256]{1,0:T(8,128)S(1)} collective-permute-done((f32[32,256]{1,0:T(8,128)S(1)}, f32[32,256]{1,0:T(8,128)S(1)}, u32[]{:S(2)}, u32[]{:S(2)}) %collective-permute-start.6) | collective-permute-done | bytes 32800 | tf_op jit(solution)/shard_map/ppermute | solution.py:450
  78.6 2.0 %collective-permute-done.7.refs_3_ = f32[32,256]{1,0:T(8,128)S(1)} collective-permute-done((f32[32,256]{1,0:T(8,128)S(1)}, f32[32,256]{1,0:T(8,128)S(1)}, u32[]{:S(2)}, u32[]{:S(2)}) %collective-permute-start.7) | collective-permute-done | bytes 32800 | tf_op jit(solution)/shard_map/ppermute | solution.py:450
  80.6 0.0 all-to-all-done
  80.6 5.5 %all-to-all-start.1 = ((bf16[8,4,2,8,1440]{4,3,2,1,0:T(8,128)(2,1)}), bf16[8,4,2,8,1440]{4,3,2,1,0:T(8,128)(2,1)S(1)}, u32[]{:S(2)}, u32[]{:S(2)}) async-start(bf16[8,4,2,8,1440]{4,3,2,1,0:T(8,128)(2,1)} %get-tuple-element.64), calls=%async_computation.1 | async-start | bytes 3145728 | tf_op jit(solution)/shard_map/all_to_all | solution.py:453
  86.8 1.8 %shard_map.115 = f32[136,128]{1,0:T(8,128)} custom-call(s32[1]{0:T(128)} %bitcast.place_ref, s32[1]{0:T(128)S(6)} %copy.25.count_ref, f32[1,256]{1,0:T(1,128)} %bitcast.39, f32[1,256]{1,0:T(1,128)} %bitcast.40, f32[32,256]{1,0:T(8,128)} %copy-done.6, f32[32,256]{1,0:T(8,128)} %copy-done.10, f32[32,256]{1,0:T(8,128)} %copy-done.11, f32[32,256]{1,0:T(8,128)} %copy-done.12), custom_call_target="tpu_custom_call" | custom-call | flops 1000000000 | bytes 1000000 | tf_op jit(solution)/shard_map/pallas_call | solution.py:306
  88.6 3.2 %collective-permute-start.10 = (f32[136,128]{1,0:T(8,128)}, f32[136,128]{1,0:T(8,128)S(1)}, u32[]{:S(2)}, u32[]{:S(2)}) collective-permute-start(f32[136,128]{1,0:T(8,128)} %shard_map.115), channel_id=1, source_target_pairs={{0,3},{1,2},{2,1},{3,0},{4,7},{5,6},{6,5},{7,4},{8,11},{9,10},{10,... | collective-permute-start | bytes 208904 | tf_op jit(solution)/shard_map/ppermute | solution.py:450
  91.8 0.0 collective-permute-start.8
  91.8 1.3 collective-permute-start.9
  93.1 1.4 collective-permute-done.10
  94.5 1.0 collective-permute-done.8
  95.5 1.2 collective-permute-done.9
  96.7 0.9 add_add_fusion.a_ref
  97.6 0.0 copy-start.5
  97.6 1.4 collective-permute-start.11
  99.0 1.6 collective-permute-start.12
  100.6 1.0 collective-permute-start.13
  101.6 2.4 %collective-permute-done.12.c_ref = f32[136,128]{1,0:T(8,128)S(1)} collective-permute-done((f32[136,128]{1,0:T(8,128)S(1)}, f32[136,128]{1,0:T(8,128)S(1)}, u32[]{:S(2)}, u32[]{:S(2)}) %collective-permute-start.12) | collective-permute-done | bytes 69664 | tf_op jit(solution)/shard_map/ppermute | solution.py:450
  104.0 1.3 collective-permute-done.13.d_ref
  105.2 0.6 copy-done.9
  105.9 5.7 %shard_map.116 = (f32[128,128]{1,0:T(8,128)}, f32[1,128]{1,0:T(1,128)}, bf16[128,128]{1,0:T(8,128)(2,1)}) custom-call(f32[136,128]{1,0:T(8,128)} %copy-done.5, f32[136,128]{1,0:T(8,128)} %copy-done.7, f32[136,128]{1,0:T(8,128)} %copy-done.8, f32[136,128]{1,0:T(8,128)} %copy-done.9), custom_call_target="tpu_custom_call" | custom-call | flops 1000000000 | bytes 1000000 | tf_op jit(solution)/shard_map/pallas_call | solution.py:370
  111.5 1.1 copy-done.4
  112.7 5.2 %shard_map.117 = bf16[8,4,32,1440]{3,2,1,0:T(8,128)(2,1)} custom-call(bf16[128,128]{1,0:T(8,128)(2,1)} %get-tuple-element.62.transform_ref, bf16[8,4,16,1440]{3,2,1,0:T(8,128)(2,1)} %bitcast.34, bf16[8,4,16,1440]{3,2,1,0:T(8,128)(2,1)} %bitcast.35), custom_call_target="tpu_custom_call" | custom-call | flops 3000000000 | bytes 3000000 | tf_op jit(solution)/shard_map/pallas_call | solution.py:419
  117.8 45.8 %all_to_all.15 = bf16[8,4,32,1440]{3,2,1,0:T(8,128)(2,1)S(1)} all-to-all(bf16[8,4,32,1440]{3,2,1,0:T(8,128)(2,1)} %shard_map.117), channel_id=1, replica_groups=mesh['ens'=8,'map'=16] {'ens'}, dimensions={0} | all-to-all | bytes 5898240 | tf_op jit(solution)/shard_map/all_to_all | solution.py:453
  163.6 4.1 %copy.22 = bf16[16,4,16,1440]{3,1,0,2:T(4,128)(2,1)} copy(bf16[16,4,16,1440]{3,2,1,0:T(8,128)(2,1)S(1)} %bitcast.32) | data formatting | bytes 5898240 | tf_op jit(solution)/shard_map/reshape | solution.py:491
  (25 shorter events, 0.1 us)
Async XLA Ops:
  3.3 3.2 %copy-start.1 = (bf16[16,16,4,1440]{3,1,2,0:T(8,128)(2,1)}, bf16[16,16,4,1440]{3,1,2,0:T(8,128)(2,1)S(1)}, u32[]{:S(2)}) copy-start(bf16[16,16,4,1440]{3,1,2,0:T(8,128)(2,1)S(1)} %copy.23) | copy-start | bytes 8847364
  3.3 9.8 %copy-start = (bf16[16,16,4,1440]{3,2,1,0:T(4,128)(2,1)S(1)}, bf16[16,16,4,1440]{3,2,1,0:T(4,128)(2,1)}, u32[]{:S(2)}) copy-start(bf16[16,16,4,1440]{3,2,1,0:T(4,128)(2,1)} %param.9) | copy-start | bytes 8847364
  6.4 23.3 %collective-permute-start.2 = (bf16[8,2,16,1440]{3,2,1,0:T(8,128)(2,1)}, bf16[8,2,16,1440]{3,2,1,0:T(8,128)(2,1)}, u32[]{:S(2)}, u32[]{:S(2)}) collective-permute-start(bf16[8,2,16,1440]{3,2,1,0:T(8,128)(2,1)} %get-tuple-element.68), channel_id=1, source_target_pairs={{0,1},{1,2},{2,3},{3,4},{4,5},{5,6},{6,7},{7,8},{8,9},{9,10},{10,1... | collective-permute-start | bytes 2211848 | tf_op jit(solution)/shard_map/ppermute | solution.py:463
  11.8 20.3 %collective-permute-start.3 = (bf16[8,2,16,1440]{3,2,1,0:T(8,128)(2,1)}, bf16[8,2,16,1440]{3,2,1,0:T(8,128)(2,1)}, u32[]{:S(2)}, u32[]{:S(2)}) collective-permute-start(bf16[8,2,16,1440]{3,2,1,0:T(8,128)(2,1)} %get-tuple-element.67), channel_id=1, source_target_pairs={{1,0},{2,1},{3,2},{4,3},{5,4},{6,5},{7,6},{8,7},{9,8},{10,9},{11,1... | collective-permute-start | bytes 2211848 | tf_op jit(solution)/shard_map/ppermute | solution.py:463
  18.8 8.7 %copy-start.2 = (bf16[4,4,16,4,1440]{4,0,3,1,2:T(4,128)(2,1)S(1)}, bf16[4,4,16,4,1440]{4,0,3,1,2:T(4,128)(2,1)}, u32[]{:S(2)}) copy-start(bf16[4,4,16,4,1440]{4,0,3,1,2:T(4,128)(2,1)} %copy.16) | copy-start | bytes 8847364
  21.2 34.3 %collective-permute-start = (bf16[8,2,16,1440]{3,2,1,0:T(8,128)(2,1)}, bf16[8,2,16,1440]{3,2,1,0:T(8,128)(2,1)}, u32[]{:S(2)}, u32[]{:S(2)}) collective-permute-start(bf16[8,2,16,1440]{3,2,1,0:T(8,128)(2,1)} %get-tuple-element.44), channel_id=1, source_target_pairs={{0,1},{1,2},{2,3},{3,4},{4,5},{5,6},{6,7},{7,8},{8,9},{9,10},{10,1... | collective-permute-start | bytes 2211848 | tf_op jit(solution)/shard_map/ppermute | solution.py:463
  26.1 29.5 %collective-permute-start.1 = (bf16[8,2,16,1440]{3,2,1,0:T(8,128)(2,1)}, bf16[8,2,16,1440]{3,2,1,0:T(8,128)(2,1)}, u32[]{:S(2)}, u32[]{:S(2)}) collective-permute-start(bf16[8,2,16,1440]{3,2,1,0:T(8,128)(2,1)} %get-tuple-element.45), channel_id=1, source_target_pairs={{1,0},{2,1},{3,2},{4,3},{5,4},{6,5},{7,6},{8,7},{9,8},{10,9},{11,1... | collective-permute-start | bytes 2211848 | tf_op jit(solution)/shard_map/ppermute | solution.py:463
  47.9 32.7 %all-to-all-start = ((bf16[8,4,2,8,1440]{4,3,2,1,0:T(8,128)(2,1)}), bf16[8,4,2,8,1440]{4,3,2,1,0:T(8,128)(2,1)S(1)}, u32[]{:S(2)}, u32[]{:S(2)}) async-start(bf16[8,4,2,8,1440]{4,3,2,1,0:T(8,128)(2,1)} %get-tuple-element.57), calls=%async_computation | async-start | bytes 3145728 | tf_op jit(solution)/shard_map/all_to_all | solution.py:453
  71.3 1.5 collective-permute-start.4
  72.8 14.0 %copy-start.6 = (f32[32,256]{1,0:T(8,128)}, f32[32,256]{1,0:T(8,128)S(1)}, u32[]{:S(2)}) copy-start(f32[32,256]{1,0:T(8,128)S(1)} %constant_dynamic-update-slice_fusion.refs_0_) | copy-start | bytes 98308
  72.8 3.9 %collective-permute-start.5 = (f32[32,256]{1,0:T(8,128)S(1)}, f32[32,256]{1,0:T(8,128)S(1)}, u32[]{:S(2)}, u32[]{:S(2)}) collective-permute-start(f32[32,256]{1,0:T(8,128)S(1)} %constant_dynamic-update-slice_fusion.refs_0_), channel_id=1, source_target_pairs={{0,32},{16,48},{32,0},{48,16},{64,96},{80,112},{96,64},{112,80},{1... | collective-permute-start | bytes 98312 | tf_op jit(solution)/shard_map/ppermute | solution.py:450
  74.2 4.4 %collective-permute-start.6 = (f32[32,256]{1,0:T(8,128)S(1)}, f32[32,256]{1,0:T(8,128)S(1)}, u32[]{:S(2)}, u32[]{:S(2)}) collective-permute-start(f32[32,256]{1,0:T(8,128)S(1)} %constant_dynamic-update-slice_fusion.refs_0_), channel_id=1, source_target_pairs={{0,64},{16,80},{32,96},{48,112},{64,0},{80,16},{96,32},{112,48},{1... | collective-permute-start | bytes 98312 | tf_op jit(solution)/shard_map/ppermute | solution.py:450
  76.6 4.0 %collective-permute-start.7 = (f32[32,256]{1,0:T(8,128)S(1)}, f32[32,256]{1,0:T(8,128)S(1)}, u32[]{:S(2)}, u32[]{:S(2)}) collective-permute-start(f32[32,256]{1,0:T(8,128)S(1)} %constant_dynamic-update-slice_fusion.refs_0_), channel_id=1, source_target_pairs={{0,96},{16,112},{32,64},{48,80},{64,32},{80,48},{96,0},{112,16},{1... | collective-permute-start | bytes 98312 | tf_op jit(solution)/shard_map/ppermute | solution.py:450
  76.7 10.1 %copy-start.10 = (f32[32,256]{1,0:T(8,128)}, f32[32,256]{1,0:T(8,128)S(1)}, u32[]{:S(2)}) copy-start(f32[32,256]{1,0:T(8,128)S(1)} %collective-permute-done.5.refs_1_) | copy-start | bytes 98308
  78.6 8.2 %copy-start.11 = (f32[32,256]{1,0:T(8,128)}, f32[32,256]{1,0:T(8,128)S(1)}, u32[]{:S(2)}) copy-start(f32[32,256]{1,0:T(8,128)S(1)} %collective-permute-done.6.refs_2_) | copy-start | bytes 98308
  80.6 6.2 %copy-start.12 = (f32[32,256]{1,0:T(8,128)}, f32[32,256]{1,0:T(8,128)S(1)}, u32[]{:S(2)}) copy-start(f32[32,256]{1,0:T(8,128)S(1)} %collective-permute-done.7.refs_3_) | copy-start | bytes 98308
  80.6 8.0 %copy-start.3 = (bf16[8,4,2,8,1440]{4,3,2,1,0:T(8,128)(2,1)}, bf16[8,4,2,8,1440]{4,3,2,1,0:T(8,128)(2,1)S(1)}, u32[]{:S(2)}) copy-start(bf16[8,4,2,8,1440]{4,3,2,1,0:T(8,128)(2,1)S(1)} %all-to-all-done) | copy-start | bytes 4423684
  80.6 31.0 %all-to-all-start.1 = ((bf16[8,4,2,8,1440]{4,3,2,1,0:T(8,128)(2,1)}), bf16[8,4,2,8,1440]{4,3,2,1,0:T(8,128)(2,1)S(1)}, u32[]{:S(2)}, u32[]{:S(2)}) async-start(bf16[8,4,2,8,1440]{4,3,2,1,0:T(8,128)(2,1)} %get-tuple-element.64), calls=%async_computation.1 | async-start | bytes 3145728 | tf_op jit(solution)/shard_map/all_to_all | solution.py:453
  88.6 5.9 %collective-permute-start.10 = (f32[136,128]{1,0:T(8,128)}, f32[136,128]{1,0:T(8,128)S(1)}, u32[]{:S(2)}, u32[]{:S(2)}) collective-permute-start(f32[136,128]{1,0:T(8,128)} %shard_map.115), channel_id=1, source_target_pairs={{0,3},{1,2},{2,1},{3,0},{4,7},{5,6},{6,5},{7,4},{8,11},{9,10},{10,... | collective-permute-start | bytes 208904 | tf_op jit(solution)/shard_map/ppermute | solution.py:450
  91.8 3.7 %collective-permute-start.8 = (f32[136,128]{1,0:T(8,128)}, f32[136,128]{1,0:T(8,128)S(1)}, u32[]{:S(2)}, u32[]{:S(2)}) collective-permute-start(f32[136,128]{1,0:T(8,128)} %shard_map.115), channel_id=1, source_target_pairs={{0,1},{1,0},{2,3},{3,2},{4,5},{5,4},{6,7},{7,6},{8,9},{9,8},{10,11... | collective-permute-start | bytes 208904 | tf_op jit(solution)/shard_map/ppermute | solution.py:450
  91.8 4.9 %collective-permute-start.9 = (f32[136,128]{1,0:T(8,128)}, f32[136,128]{1,0:T(8,128)S(1)}, u32[]{:S(2)}, u32[]{:S(2)}) collective-permute-start(f32[136,128]{1,0:T(8,128)} %shard_map.115), channel_id=1, source_target_pairs={{0,2},{1,3},{2,0},{3,1},{4,6},{5,7},{6,4},{7,5},{8,10},{9,11},{10,... | collective-permute-start | bytes 208904 | tf_op jit(solution)/shard_map/ppermute | solution.py:450
  97.6 7.6 %copy-start.5 = (f32[136,128]{1,0:T(8,128)}, f32[136,128]{1,0:T(8,128)S(1)}, u32[]{:S(2)}) copy-start(f32[136,128]{1,0:T(8,128)S(1)} %add_add_fusion.a_ref) | copy-start | bytes 208900
  97.6 3.9 %collective-permute-start.11 = (f32[136,128]{1,0:T(8,128)S(1)}, f32[136,128]{1,0:T(8,128)S(1)}, u32[]{:S(2)}, u32[]{:S(2)}) collective-permute-start(f32[136,128]{1,0:T(8,128)S(1)} %add_add_fusion.a_ref), channel_id=1, source_target_pairs={{0,4},{1,5},{2,6},{3,7},{4,0},{5,1},{6,2},{7,3},{8,12},{9,13},{10,... | collective-permute-start | bytes 208904 | tf_op jit(solution)/shard_map/ppermute | solution.py:450
  99.0 5.0 %collective-permute-start.12 = (f32[136,128]{1,0:T(8,128)S(1)}, f32[136,128]{1,0:T(8,128)S(1)}, u32[]{:S(2)}, u32[]{:S(2)}) collective-permute-start(f32[136,128]{1,0:T(8,128)S(1)} %add_add_fusion.a_ref), channel_id=1, source_target_pairs={{0,8},{1,9},{2,10},{3,11},{4,12},{5,13},{6,14},{7,15},{8,0},{9,1},... | collective-permute-start | bytes 208904 | tf_op jit(solution)/shard_map/ppermute | solution.py:450
  100.6 4.7 %collective-permute-start.13 = (f32[136,128]{1,0:T(8,128)S(1)}, f32[136,128]{1,0:T(8,128)S(1)}, u32[]{:S(2)}, u32[]{:S(2)}) collective-permute-start(f32[136,128]{1,0:T(8,128)S(1)} %add_add_fusion.a_ref), channel_id=1, source_target_pairs={{0,12},{1,13},{2,14},{3,15},{4,8},{5,9},{6,10},{7,11},{8,4},{9,5},... | collective-permute-start | bytes 208904 | tf_op jit(solution)/shard_map/ppermute | solution.py:450
  101.6 3.7 %copy-start.7 = (f32[136,128]{1,0:T(8,128)}, f32[136,128]{1,0:T(8,128)S(1)}, u32[]{:S(2)}) copy-start(f32[136,128]{1,0:T(8,128)S(1)} %collective-permute-done.11.b_ref) | copy-start | bytes 208900
  104.0 1.3 copy-start.8
  105.2 0.6 copy-start.9
  111.5 1.1 copy-start.4

commit v9 on v7

--- a/solution.py
+++ b/solution.py
@@ -302,7 +302,7 @@
         in_specs=[smem, smem] + [vmem] * (2 + N_ENS // 2),
         out_specs=vmem,
         out_shape=jax.ShapeDtypeStruct((MEMBERS + 8, MEMBERS), jnp.float32),
-        cost_estimate=cost(1),
+        cost_estimate=cost(10),
         scratch_shapes=[pltpu.VMEM((MEMBERS, SLOTS), jnp.float32)],
     )(places, count, value.reshape(1, SLOTS), sigma.reshape(1, SLOTS), *pieces)
 
@@ -370,7 +370,7 @@
             jax.ShapeDtypeStruct((1, MEMBERS), jnp.float32),
             jax.ShapeDtypeStruct((MEMBERS, MEMBERS), jnp.bfloat16),
         ],
-        cost_estimate=cost(1),
+        cost_estimate=cost(10),
         compiler_params=pltpu.CompilerParams(vmem_limit_bytes=60 * 1024 * 1024),
     )(*parts)
 

time: 168 us -> 167 us (level)
  blocking collectives: 45.8 us -> 42.3 us
  waiting for transfers between devices: 14.2 us -> 16.7 us
    all_to_all x2, waiting for transfers between devices: 0.01 us -> 6.32 us  [on_device(): lax.all_to_all(value, 'ens', split_axis=0, concat_axis=0, tiled=True)]
    ppermute x10, waiting for transfers between devices: 11.8 us -> 7.97 us  [swap(): return lax.ppermute(value, axis, pairs)]
    all_to_all x1, blocking collectives: 45.8 us -> 42.3 us  [on_device(): lax.all_to_all(value, 'ens', split_axis=0, concat_axis=0, tiled=True)]
    unnamed x28 -> x30, local copies, waits for them, and re-layouts: 6.62 us -> 7.2 us
  transfers between devices with their start and end apart: 16 -> 16, of which waited for: 9 -> 7; matrix products, arithmetic and copies ran while one was open for 6% -> 5% of each run, Pallas kernels for 24% -> 23%
where the time goes in v9:
time: 167 us
  Pallas kernels  46.2 us (28%)
  blocking collectives  42.3 us (25%)
  starting transfers between devices  39.1 us (23%)
  local copies, waits for them, and re-layouts  20.9 us (13%)
  waiting for transfers between devices  16.7 us (10%)
    all_to_all x1, blocking collectives, on_device(): lax.all_to_all(value, 'ens', split_axis=0, concat_axis=0, tiled=True)  42.3 us
    pallas_call x2, Pallas kernels, forecast(): pl.pallas_call(kernel, grid=(steps,), in_specs=[pl.BlockSpec((STEP, ROWS,...  30.7 us
    all_to_all x2, starting transfers between devices, on_device(): lax.all_to_all(value, 'ens', split_axis=0, concat_axis=0, tiled=True)  13.7 us
    ppermute x10, starting transfers between devices, swap(): return lax.ppermute(value, axis, pairs)  12.4 us
    ppermute x2, starting transfers between devices, halo(): lax.ppermute(rows[0], 'map', down)  10.2 us
    ppermute x10, waiting for transfers between devices, swap(): return lax.ppermute(value, axis, pairs)  7.97 us
    unnamed x30, local copies, waits for them, and re-layouts  7.2 us
    all_to_all x2, waiting for transfers between devices, on_device(): lax.all_to_all(value, 'ens', split_axis=0, concat_axis=0, tiled=True)  6.32 us
  transfers between devices with their start and end apart: 16, of which 7 were waited for; matrix products, arithmetic and copies ran while one was open for 5% of the time, Pallas kernels for 23%

profile of v9, /device:TPU:1, one launch (start us, length us, event | category | flops | bytes accessed | tf_op | source)
XLA Modules:
  0.0 166.6 jit_solution(2054041376564678522)
XLA Ops:
  0.6 2.7 %copy.23 = bf16[16,16,4,1440]{3,1,2,0:T(8,128)(2,1)S(1)} copy(bf16[16,16,4,1440]{3,2,1,0:T(4,128)(2,1)} %param.9) | data formatting | bytes 5898240 | tf_op args[0]
  3.3 0.0 copy-start.1
  3.3 0.0 copy-start
  3.3 1.7 %fusion = (bf16[8,2,16,1440]{3,2,1,0:T(8,128)(2,1)}, bf16[8,2,16,1440]{3,2,1,0:T(8,128)(2,1)}, bf16[8,2,16,1440]{3,2,1,0:T(8,128)(2,1)}, bf16[8,2,16,1440]{3,2,1,0:T(8,128)(2,1)}) fusion(bf16[16,4,16,1440]{3,2,1,0:T(8,128)(2,1)S(1)} %bitcast.26), kind=kLoop, calls=%fused_computation.5 | loop fusion | bytes 5898240 | tf_op jit(solution)/shard_map/slice | solution.py:456
  5.0 1.4 copy-done.1
  6.4 5.4 %collective-permute-start.2 = (bf16[8,2,16,1440]{3,2,1,0:T(8,128)(2,1)}, bf16[8,2,16,1440]{3,2,1,0:T(8,128)(2,1)}, u32[]{:S(2)}, u32[]{:S(2)}) collective-permute-start(bf16[8,2,16,1440]{3,2,1,0:T(8,128)(2,1)} %get-tuple-element.68), channel_id=1, source_target_pairs={{0,1},{1,2},{2,3},{3,4},{4,5},{5,6},{6,7},{7,8},{8,9},{9,10},{10,1... | collective-permute-start | bytes 2211848 | tf_op jit(solution)/shard_map/ppermute | solution.py:459
  11.8 1.3 collective-permute-start.3
  13.1 5.7 %copy.16 = bf16[4,4,16,4,1440]{4,0,3,1,2:T(4,128)(2,1)} copy(bf16[4,4,16,4,1440]{4,3,2,1,0:T(4,128)(2,1)S(1)} %bitcast.25) | data formatting | bytes 5898240 | tf_op jit(solution)/shard_map/reshape | solution.py:466
  18.8 2.4 %shard_map.112 = (bf16[384,256]{1,0:T(8,128)(2,1)}, bf16[384,256]{1,0:T(8,128)(2,1)}, bf16[96,256]{1,0:T(8,128)(2,1)}, bf16[192,256]{1,0:T(8,128)(2,1)}, bf16[96...) custom-call(s32[1]{0:T(128)} %bitcast.4.tile_ref, ...), custom_call_target="tpu_custom_call" | custom-call | flops 3000000000 | bytes 3000000 | tf_op jit(solution)/shard_map/pallas_call | solution.py:107
  21.2 4.9 %collective-permute-start = (bf16[8,2,16,1440]{3,2,1,0:T(8,128)(2,1)}, bf16[8,2,16,1440]{3,2,1,0:T(8,128)(2,1)}, u32[]{:S(2)}, u32[]{:S(2)}) collective-permute-start(bf16[8,2,16,1440]{3,2,1,0:T(8,128)(2,1)} %get-tuple-element.44), channel_id=1, source_target_pairs={{0,1},{1,2},{2,3},{3,4},{4,5},{5,6},{6,7},{7,8},{8,9},{9,10},{10,1... | collective-permute-start | bytes 2211848 | tf_op jit(solution)/shard_map/ppermute | solution.py:459
  26.1 1.5 collective-permute-start.1
  27.5 2.2 %copy.18.refs_1_.base_ref = bf16[4,256,1440]{2,1,0:T(8,128)(2,1)} copy(bf16[4,256,1440]{2,0,1:T(4,128)(2,1)S(1)} %bitcast.29) | data formatting | bytes 5898240 | tf_op jit(solution)/shard_map/optimization_barrier | solution.py:468
  29.8 0.0 collective-permute-done.2.refs_2_
  29.8 2.4 %collective-permute-done.3.refs_3_ = bf16[8,2,16,1440]{3,2,1,0:T(8,128)(2,1)} collective-permute-done((bf16[8,2,16,1440]{3,2,1,0:T(8,128)(2,1)}, bf16[8,2,16,1440]{3,2,1,0:T(8,128)(2,1)}, u32[]{:S(2)}, u32[]{:S(2)}) %collective-permute-start.3) | collective-permute-done | bytes 737312 | tf_op jit(solution)/shard_map/ppermute | solution.py:459
  32.1 15.3 %shard_map.113 = (bf16[8,2,32,1440]{3,2,1,0:T(8,128)(2,1)}, f32[8,256]{1,0:T(8,128)}) custom-call(bf16[16,4,16,1440]{3,2,1,0:T(8,128)(2,1)} %bitcast.27, bf16[4,256,1440]{2,1,0:T(8,128)(2,1)} %copy.18.refs_1_.base_ref, bf16[8,2,16,1440]{3,2,1,0:T(8,128)(2,1)} %collective-permute-done.2.refs_2_, bf16[8,2,16,1440]{3,2,1,0:T(8,128)(2,1)} %collective-permute-done.3.refs_3_, ...), custom_call_target="tpu_custom_call" | custom-call | flops 16000000000 | bytes 16000000 | tf_op jit(solution)/shard_map/pallas_call | solution.py:250
  47.5 7.6 %all-to-all-start = ((bf16[8,2,32,1440]{3,2,1,0:T(8,128)(2,1)}), bf16[8,2,32,1440]{3,2,1,0:T(8,128)(2,1)S(1)}, u32[]{:S(2)}, u32[]{:S(2)}) async-start(bf16[8,2,32,1440]{3,2,1,0:T(8,128)(2,1)} %get-tuple-element.57), calls=%async_computation | async-start | bytes 3145728 | tf_op jit(solution)/shard_map/all_to_all | solution.py:449
  55.1 0.0 collective-permute-done.1.bottom_ref
  55.1 15.3 %shard_map.114 = (bf16[8,2,32,1440]{3,2,1,0:T(8,128)(2,1)}, f32[16,256]{1,0:T(8,128)}) custom-call(bf16[16,4,16,1440]{3,2,1,0:T(8,128)(2,1)} %bitcast.28, bf16[4,256,1440]{2,1,0:T(8,128)(2,1)} %copy.18.refs_1_.base_ref, bf16[8,2,16,1440]{3,2,1,0:T(8,128)(2,1)} %collective-permute-done.top_ref, bf16[8,2,16,1440]{3,2,1,0:T(8,128)(2,1)} %collective-permute-done.1.bottom_ref, ...), custom_call_target="tpu_custom_call" | custom-call | flops 16000000000 | bytes 16000000 | tf_op jit(solution)/shard_map/pallas_call | solution.py:250
  70.4 0.1 collective-permute-start.4
  70.5 0.7 constant_dynamic-update-slice_fusion.1
  71.2 0.7 collective-permute-done.4
  71.9 1.4 collective-permute-start.5
  73.3 2.4 %collective-permute-start.6 = (f32[32,256]{1,0:T(8,128)S(1)}, f32[32,256]{1,0:T(8,128)S(1)}, u32[]{:S(2)}, u32[]{:S(2)}) collective-permute-start(f32[32,256]{1,0:T(8,128)S(1)} %constant_dynamic-update-slice_fusion.refs_0_), channel_id=1, source_target_pairs={{0,64},{16,80},{32,96},{48,112},{64,0},{80,16},{96,32},{112,48},{1... | collective-permute-start | bytes 98312 | tf_op jit(solution)/shard_map/ppermute | solution.py:446
  75.7 0.1 collective-permute-start.7
  76.5 1.3 collective-permute-done.6.refs_2_
  77.8 1.9 %collective-permute-done.7.refs_3_ = f32[32,256]{1,0:T(8,128)S(1)} collective-permute-done((f32[32,256]{1,0:T(8,128)S(1)}, f32[32,256]{1,0:T(8,128)S(1)}, u32[]{:S(2)}, u32[]{:S(2)}) %collective-permute-start.7) | collective-permute-done | bytes 32800 | tf_op jit(solution)/shard_map/ppermute | solution.py:446
  79.7 0.6 copy-done.13
  80.3 1.8 %shard_map.115 = f32[136,128]{1,0:T(8,128)} custom-call(s32[1]{0:T(128)} %bitcast.place_ref, s32[1]{0:T(128)S(6)} %copy.25.count_ref, f32[1,256]{1,0:T(1,128)} %bitcast.35, f32[1,256]{1,0:T(1,128)} %bitcast.36, f32[32,256]{1,0:T(8,128)} %copy-done.7, f32[32,256]{1,0:T(8,128)} %copy-done.11, f32[32,256]{1,0:T(8,128)} %copy-done.12, f32[32,256]{1,0:T(8,128)} %copy-done.13), custom_call_target="tpu_custom_call" | custom-call | flops 10000000000 | bytes 10000000 | tf_op jit(solution)/shard_map/pallas_call | solution.py:300
  82.1 3.2 %collective-permute-start.10 = (f32[136,128]{1,0:T(8,128)}, f32[136,128]{1,0:T(8,128)S(1)}, u32[]{:S(2)}, u32[]{:S(2)}) collective-permute-start(f32[136,128]{1,0:T(8,128)} %shard_map.115), channel_id=1, source_target_pairs={{0,3},{1,2},{2,1},{3,0},{4,7},{5,6},{6,5},{7,4},{8,11},{9,10},{10,... | collective-permute-start | bytes 208904 | tf_op jit(solution)/shard_map/ppermute | solution.py:446
  85.3 0.0 collective-permute-start.8
  85.3 1.3 collective-permute-start.9
  86.6 6.1 %all-to-all-start.1 = ((bf16[8,2,32,1440]{3,2,1,0:T(8,128)(2,1)}), bf16[8,2,32,1440]{3,2,1,0:T(8,128)(2,1)S(1)}, u32[]{:S(2)}, u32[]{:S(2)}) async-start(bf16[8,2,32,1440]{3,2,1,0:T(8,128)(2,1)} %get-tuple-element.64), calls=%async_computation.1 | async-start | bytes 3145728 | tf_op jit(solution)/shard_map/all_to_all | solution.py:449
  92.7 0.0 collective-permute-done.10
  92.7 0.0 collective-permute-done.8
  92.7 0.0 collective-permute-done.9
  92.7 0.0 copy-start.6
  92.7 1.4 collective-permute-start.11
  94.1 1.6 collective-permute-start.12
  95.7 1.0 collective-permute-start.13
  96.7 2.9 %collective-permute-done.12.c_ref = f32[136,128]{1,0:T(8,128)S(1)} collective-permute-done((f32[136,128]{1,0:T(8,128)S(1)}, f32[136,128]{1,0:T(8,128)S(1)}, u32[]{:S(2)}, u32[]{:S(2)}) %collective-permute-start.12) | collective-permute-done | bytes 69664 | tf_op jit(solution)/shard_map/ppermute | solution.py:446
  99.6 1.2 collective-permute-done.13.d_ref
  100.8 0.6 copy-done.10
  101.4 5.7 %shard_map.116 = (f32[128,128]{1,0:T(8,128)}, f32[1,128]{1,0:T(1,128)}, bf16[128,128]{1,0:T(8,128)(2,1)}) custom-call(f32[136,128]{1,0:T(8,128)} %copy-done.6, f32[136,128]{1,0:T(8,128)} %copy-done.8, f32[136,128]{1,0:T(8,128)} %copy-done.9, f32[136,128]{1,0:T(8,128)} %copy-done.10), custom_call_target="tpu_custom_call" | custom-call | flops 10000000000 | bytes 10000000 | tf_op jit(solution)/shard_map/pallas_call | solution.py:364
  107.1 6.3 %all-to-all-done.1.late_ref = bf16[8,2,32,1440]{3,2,1,0:T(8,128)(2,1)S(1)} async-done(((bf16[8,2,32,1440]{3,2,1,0:T(8,128)(2,1)}), bf16[8,2,32,1440]{3,2,1,0:T(8,128)(2,1)S(1)}, u32[]{:S(2)}, u32[]{:S(2)}) %all-to-all-start.1) | async-done | bytes 1474592 | tf_op jit(solution)/shard_map/all_to_all | solution.py:449
  113.4 1.1 copy-done.4
  114.6 5.7 %shard_map.117 = bf16[8,2,64,1440]{3,2,1,0:T(8,128)(2,1)} custom-call(bf16[128,128]{1,0:T(8,128)(2,1)} %get-tuple-element.62.transform_ref, bf16[8,2,32,1440]{3,2,1,0:T(8,128)(2,1)} %copy-done.3, bf16[8,2,32,1440]{3,2,1,0:T(8,128)(2,1)} %copy-done.4), custom_call_target="tpu_custom_call" | custom-call | flops 4000000000 | bytes 4000000 | tf_op jit(solution)/shard_map/pallas_call | solution.py:413
  120.2 42.3 %all_to_all.15 = bf16[8,2,64,1440]{3,2,1,0:T(8,128)(2,1)S(1)} all-to-all(bf16[8,2,64,1440]{3,2,1,0:T(8,128)(2,1)} %shard_map.117), channel_id=1, replica_groups=mesh['ens'=8,'map'=16] {'ens'}, dimensions={0} | all-to-all | bytes 5898240 | tf_op jit(solution)/shard_map/all_to_all | solution.py:449
  162.5 4.1 %copy.22 = bf16[16,4,16,1440]{3,1,0,2:T(4,128)(2,1)} copy(bf16[16,4,16,1440]{3,2,1,0:T(8,128)(2,1)S(1)} %bitcast.30) | data formatting | bytes 5898240 | tf_op jit(solution)/shard_map/reshape | solution.py:487
  (27 shorter events, 0.1 us)
Async XLA Ops:
  3.3 3.2 %copy-start.1 = (bf16[16,16,4,1440]{3,1,2,0:T(8,128)(2,1)}, bf16[16,16,4,1440]{3,1,2,0:T(8,128)(2,1)S(1)}, u32[]{:S(2)}) copy-start(bf16[16,16,4,1440]{3,1,2,0:T(8,128)(2,1)S(1)} %copy.23) | copy-start | bytes 8847364
  3.3 9.8 %copy-start = (bf16[16,16,4,1440]{3,2,1,0:T(4,128)(2,1)S(1)}, bf16[16,16,4,1440]{3,2,1,0:T(4,128)(2,1)}, u32[]{:S(2)}) copy-start(bf16[16,16,4,1440]{3,2,1,0:T(4,128)(2,1)} %param.9) | copy-start | bytes 8847364
  6.4 23.3 %collective-permute-start.2 = (bf16[8,2,16,1440]{3,2,1,0:T(8,128)(2,1)}, bf16[8,2,16,1440]{3,2,1,0:T(8,128)(2,1)}, u32[]{:S(2)}, u32[]{:S(2)}) collective-permute-start(bf16[8,2,16,1440]{3,2,1,0:T(8,128)(2,1)} %get-tuple-element.68), channel_id=1, source_target_pairs={{0,1},{1,2},{2,3},{3,4},{4,5},{5,6},{6,7},{7,8},{8,9},{9,10},{10,1... | collective-permute-start | bytes 2211848 | tf_op jit(solution)/shard_map/ppermute | solution.py:459
  11.8 20.3 %collective-permute-start.3 = (bf16[8,2,16,1440]{3,2,1,0:T(8,128)(2,1)}, bf16[8,2,16,1440]{3,2,1,0:T(8,128)(2,1)}, u32[]{:S(2)}, u32[]{:S(2)}) collective-permute-start(bf16[8,2,16,1440]{3,2,1,0:T(8,128)(2,1)} %get-tuple-element.67), channel_id=1, source_target_pairs={{1,0},{2,1},{3,2},{4,3},{5,4},{6,5},{7,6},{8,7},{9,8},{10,9},{11,1... | collective-permute-start | bytes 2211848 | tf_op jit(solution)/shard_map/ppermute | solution.py:459
  18.8 8.7 %copy-start.2 = (bf16[4,4,16,4,1440]{4,0,3,1,2:T(4,128)(2,1)S(1)}, bf16[4,4,16,4,1440]{4,0,3,1,2:T(4,128)(2,1)}, u32[]{:S(2)}) copy-start(bf16[4,4,16,4,1440]{4,0,3,1,2:T(4,128)(2,1)} %copy.16) | copy-start | bytes 8847364
  21.2 33.9 %collective-permute-start = (bf16[8,2,16,1440]{3,2,1,0:T(8,128)(2,1)}, bf16[8,2,16,1440]{3,2,1,0:T(8,128)(2,1)}, u32[]{:S(2)}, u32[]{:S(2)}) collective-permute-start(bf16[8,2,16,1440]{3,2,1,0:T(8,128)(2,1)} %get-tuple-element.44), channel_id=1, source_target_pairs={{0,1},{1,2},{2,3},{3,4},{4,5},{5,6},{6,7},{7,8},{8,9},{9,10},{10,1... | collective-permute-start | bytes 2211848 | tf_op jit(solution)/shard_map/ppermute | solution.py:459
  26.1 29.0 %collective-permute-start.1 = (bf16[8,2,16,1440]{3,2,1,0:T(8,128)(2,1)}, bf16[8,2,16,1440]{3,2,1,0:T(8,128)(2,1)}, u32[]{:S(2)}, u32[]{:S(2)}) collective-permute-start(bf16[8,2,16,1440]{3,2,1,0:T(8,128)(2,1)} %get-tuple-element.45), channel_id=1, source_target_pairs={{1,0},{2,1},{3,2},{4,3},{5,4},{6,5},{7,6},{8,7},{9,8},{10,9},{11,1... | collective-permute-start | bytes 2211848 | tf_op jit(solution)/shard_map/ppermute | solution.py:459
  47.5 32.2 %all-to-all-start = ((bf16[8,2,32,1440]{3,2,1,0:T(8,128)(2,1)}), bf16[8,2,32,1440]{3,2,1,0:T(8,128)(2,1)S(1)}, u32[]{:S(2)}, u32[]{:S(2)}) async-start(bf16[8,2,32,1440]{3,2,1,0:T(8,128)(2,1)} %get-tuple-element.57), calls=%async_computation | async-start | bytes 3145728 | tf_op jit(solution)/shard_map/all_to_all | solution.py:449
  70.4 1.5 collective-permute-start.4
  71.9 7.8 %copy-start.7 = (f32[32,256]{1,0:T(8,128)}, f32[32,256]{1,0:T(8,128)S(1)}, u32[]{:S(2)}) copy-start(f32[32,256]{1,0:T(8,128)S(1)} %constant_dynamic-update-slice_fusion.refs_0_) | copy-start | bytes 98308
  71.9 4.6 %collective-permute-start.5 = (f32[32,256]{1,0:T(8,128)S(1)}, f32[32,256]{1,0:T(8,128)S(1)}, u32[]{:S(2)}, u32[]{:S(2)}) collective-permute-start(f32[32,256]{1,0:T(8,128)S(1)} %constant_dynamic-update-slice_fusion.refs_0_), channel_id=1, source_target_pairs={{0,32},{16,48},{32,0},{48,16},{64,96},{80,112},{96,64},{112,80},{1... | collective-permute-start | bytes 98312 | tf_op jit(solution)/shard_map/ppermute | solution.py:446
  73.3 4.4 %collective-permute-start.6 = (f32[32,256]{1,0:T(8,128)S(1)}, f32[32,256]{1,0:T(8,128)S(1)}, u32[]{:S(2)}, u32[]{:S(2)}) collective-permute-start(f32[32,256]{1,0:T(8,128)S(1)} %constant_dynamic-update-slice_fusion.refs_0_), channel_id=1, source_target_pairs={{0,64},{16,80},{32,96},{48,112},{64,0},{80,16},{96,32},{112,48},{1... | collective-permute-start | bytes 98312 | tf_op jit(solution)/shard_map/ppermute | solution.py:446
  75.7 4.0 %collective-permute-start.7 = (f32[32,256]{1,0:T(8,128)S(1)}, f32[32,256]{1,0:T(8,128)S(1)}, u32[]{:S(2)}, u32[]{:S(2)}) collective-permute-start(f32[32,256]{1,0:T(8,128)S(1)} %constant_dynamic-update-slice_fusion.refs_0_), channel_id=1, source_target_pairs={{0,96},{16,112},{32,64},{48,80},{64,32},{80,48},{96,0},{112,16},{1... | collective-permute-start | bytes 98312 | tf_op jit(solution)/shard_map/ppermute | solution.py:446
  76.5 3.2 %copy-start.11 = (f32[32,256]{1,0:T(8,128)}, f32[32,256]{1,0:T(8,128)S(1)}, u32[]{:S(2)}) copy-start(f32[32,256]{1,0:T(8,128)S(1)} %collective-permute-done.5.refs_1_) | copy-start | bytes 98308
  77.8 2.0 %copy-start.12 = (f32[32,256]{1,0:T(8,128)}, f32[32,256]{1,0:T(8,128)S(1)}, u32[]{:S(2)}) copy-start(f32[32,256]{1,0:T(8,128)S(1)} %collective-permute-done.6.refs_2_) | copy-start | bytes 98308
  79.7 0.6 copy-start.13
  79.7 2.4 %copy-start.3 = (bf16[8,2,32,1440]{3,2,1,0:T(8,128)(2,1)}, bf16[8,2,32,1440]{3,2,1,0:T(8,128)(2,1)S(1)}, u32[]{:S(2)}) copy-start(bf16[8,2,32,1440]{3,2,1,0:T(8,128)(2,1)S(1)} %all-to-all-done.early_ref) | copy-start | bytes 4423684
  82.1 10.6 %copy-start.5 = (f32[136,128]{1,0:T(8,128)S(1)}, f32[136,128]{1,0:T(8,128)}, u32[]{:S(2)}) copy-start(f32[136,128]{1,0:T(8,128)} %shard_map.115) | copy-start | bytes 208900
  82.1 10.6 %collective-permute-start.10 = (f32[136,128]{1,0:T(8,128)}, f32[136,128]{1,0:T(8,128)S(1)}, u32[]{:S(2)}, u32[]{:S(2)}) collective-permute-start(f32[136,128]{1,0:T(8,128)} %shard_map.115), channel_id=1, source_target_pairs={{0,3},{1,2},{2,1},{3,0},{4,7},{5,6},{6,5},{7,4},{8,11},{9,10},{10,... | collective-permute-start | bytes 208904 | tf_op jit(solution)/shard_map/ppermute | solution.py:446
  85.3 7.4 %collective-permute-start.8 = (f32[136,128]{1,0:T(8,128)}, f32[136,128]{1,0:T(8,128)S(1)}, u32[]{:S(2)}, u32[]{:S(2)}) collective-permute-start(f32[136,128]{1,0:T(8,128)} %shard_map.115), channel_id=1, source_target_pairs={{0,1},{1,0},{2,3},{3,2},{4,5},{5,4},{6,7},{7,6},{8,9},{9,8},{10,11... | collective-permute-start | bytes 208904 | tf_op jit(solution)/shard_map/ppermute | solution.py:446
  85.3 7.4 %collective-permute-start.9 = (f32[136,128]{1,0:T(8,128)}, f32[136,128]{1,0:T(8,128)S(1)}, u32[]{:S(2)}, u32[]{:S(2)}) collective-permute-start(f32[136,128]{1,0:T(8,128)} %shard_map.115), channel_id=1, source_target_pairs={{0,2},{1,3},{2,0},{3,1},{4,6},{5,7},{6,4},{7,5},{8,10},{9,11},{10,... | collective-permute-start | bytes 208904 | tf_op jit(solution)/shard_map/ppermute | solution.py:446
  86.6 26.8 %all-to-all-start.1 = ((bf16[8,2,32,1440]{3,2,1,0:T(8,128)(2,1)}), bf16[8,2,32,1440]{3,2,1,0:T(8,128)(2,1)S(1)}, u32[]{:S(2)}, u32[]{:S(2)}) async-start(bf16[8,2,32,1440]{3,2,1,0:T(8,128)(2,1)} %get-tuple-element.64), calls=%async_computation.1 | async-start | bytes 3145728 | tf_op jit(solution)/shard_map/all_to_all | solution.py:449
  92.7 8.1 %copy-start.6 = (f32[136,128]{1,0:T(8,128)}, f32[136,128]{1,0:T(8,128)S(1)}, u32[]{:S(2)}) copy-start(f32[136,128]{1,0:T(8,128)S(1)} %add_add_fusion.a_ref) | copy-start | bytes 208900
  92.7 3.9 %collective-permute-start.11 = (f32[136,128]{1,0:T(8,128)S(1)}, f32[136,128]{1,0:T(8,128)S(1)}, u32[]{:S(2)}, u32[]{:S(2)}) collective-permute-start(f32[136,128]{1,0:T(8,128)S(1)} %add_add_fusion.a_ref), channel_id=1, source_target_pairs={{0,4},{1,5},{2,6},{3,7},{4,0},{5,1},{6,2},{7,3},{8,12},{9,13},{10,... | collective-permute-start | bytes 208904 | tf_op jit(solution)/shard_map/ppermute | solution.py:446
  94.1 5.5 %collective-permute-start.12 = (f32[136,128]{1,0:T(8,128)S(1)}, f32[136,128]{1,0:T(8,128)S(1)}, u32[]{:S(2)}, u32[]{:S(2)}) collective-permute-start(f32[136,128]{1,0:T(8,128)S(1)} %add_add_fusion.a_ref), channel_id=1, source_target_pairs={{0,8},{1,9},{2,10},{3,11},{4,12},{5,13},{6,14},{7,15},{8,0},{9,1},... | collective-permute-start | bytes 208904 | tf_op jit(solution)/shard_map/ppermute | solution.py:446
  95.7 5.1 %collective-permute-start.13 = (f32[136,128]{1,0:T(8,128)S(1)}, f32[136,128]{1,0:T(8,128)S(1)}, u32[]{:S(2)}, u32[]{:S(2)}) collective-permute-start(f32[136,128]{1,0:T(8,128)S(1)} %add_add_fusion.a_ref), channel_id=1, source_target_pairs={{0,12},{1,13},{2,14},{3,15},{4,8},{5,9},{6,10},{7,11},{8,4},{9,5},... | collective-permute-start | bytes 208904 | tf_op jit(solution)/shard_map/ppermute | solution.py:446
  96.7 4.1 %copy-start.8 = (f32[136,128]{1,0:T(8,128)}, f32[136,128]{1,0:T(8,128)S(1)}, u32[]{:S(2)}) copy-start(f32[136,128]{1,0:T(8,128)S(1)} %collective-permute-done.11.b_ref) | copy-start | bytes 208900
  99.6 1.2 copy-start.9
  100.8 0.6 copy-start.10
  113.4 1.1 copy-start.4
